TPU v7x, 32 devices: a whole 2x2x4 slice. The times are simulated.
32 devices in a mesh: ctx: 8 (over z, y), head: 4 (over x, core).
Axes of the slice: x: 2, y: 2, z: 4, core: 2. Of those that a mesh axis runs over, the one named last changes fastest.
Arguments:
- query: bfloat16 [8, 2, 512, 4096], P('ctx', None, None, 'head'), may hold values from -48 to 48
- key: bfloat16 [8, 2, 512, 512], P('ctx', None, 'head'), may hold values from -18 to 18
- value: bfloat16 [8, 2, 512, 512], P('ctx', None, 'head'), may hold values from -6 to 6
- d_out: bfloat16 [8, 2, 512, 4096], P('ctx', None, None, 'head'), may hold values from -6 to 6
- doc_start: int32 [64], replicated, may hold values from 0 to 1, as said below
Outputs:
- d_query: bfloat16 [8, 2, 512, 4096], P('ctx', None, None, 'head')
- d_key: bfloat16 [8, 2, 512, 512], P('ctx', None, 'head')
- d_value: bfloat16 [8, 2, 512, 512], P('ctx', None, 'head')
Inputs may be any that keep to these rules, and one draw needn't show every extreme that they name: `doc_start`: 1 where a document begins at that block of 128 tokens (blocks in sequence order); block 0 begins one; from every beginning the next beginning, or the end of the sequence, is 1 to 3 blocks away; the first block of every span after the first lies inside a document of exactly 3 blocks that began in the span before.
All inputs are finite; a program needn't handle non-finite values.
Results may differ from a plain program's by a relative error of at most 0.039.
Values may be sent and summed in bfloat16 or wider, within the bound.
No kernel may reach another device: no remote copies, remote signals or barrier semaphores. Data moves between devices by JAX's collectives and lax.ppermute only.
A program may use at most 64 MiB of HBM per device.

v0:
```python
import functools

import jax
import jax.numpy as jnp
from jax import lax
from jax.experimental import pallas as pl
from jax.experimental.pallas import tpu as pltpu
from jax.sharding import PartitionSpec as P

HD = 128
BLK = 128
REACH = 2
SCALE = HD**-0.5
SCALE_LOG2E = SCALE * 1.4426950408889634
LATE = ((1, 1), (1, 2), (2, 1), (3, 1))
EARLY = ((2, 3), (3, 1))
BF16 = jnp.bfloat16
F32 = jnp.float32
VMEM = pl.BlockSpec(memory_space=pltpu.VMEM)
HBM = pl.BlockSpec(memory_space=pltpu.HBM)
ANY = pl.BlockSpec(memory_space=pl.ANY)


def shape(dims, dtype=BF16):
    return jax.ShapeDtypeStruct(dims, dtype)


def call(body, inputs, outs, scratch=(), flops=0, moved=0, limit=12, far=(), after=(), out_spec=VMEM, aliases=None):
    in_specs = [ANY] * len(after) + [
        HBM if i in far else VMEM for i in range(len(inputs))
    ]
    skip = len(after)
    name = body.func.__name__
    return pl.pallas_call(
        lambda *refs: body(*refs[skip:]),
        out_shape=outs,
        in_specs=in_specs,
        out_specs=[out_spec] * len(outs),
        scratch_shapes=list(scratch),
        input_output_aliases=aliases or {},
        compiler_params=pltpu.CompilerParams(vmem_limit_bytes=limit << 20),
        cost_estimate=pl.CostEstimate(flops=flops, bytes_accessed=moved, transcendentals=0),
        name=name,
    )(*after, *inputs)


def carry(pairs, sems):
    copies = [pltpu.make_async_copy(a, b, sems.at[i]) for i, (a, b) in enumerate(pairs)]
    for copy in copies:
        copy.start()
    for copy in copies:
        copy.wait()


def lanes(index):
    return pl.ds(pl.multiple_of(index * HD, HD), HD)


def rows(index, blocks=1):
    return pl.ds(pl.multiple_of(index * BLK, BLK), blocks * BLK)


def slot_of(half):
    odd = lax.rem(lax.axis_index("ctx"), 2)
    return 1 - odd if half == 0 else odd


def is_last():
    return lax.axis_index("ctx") == lax.axis_size("ctx") - 1


def span_of(half):
    ctx = lax.axis_index("ctx")
    return jnp.where(slot_of(half) == 0, ctx, 2 * lax.axis_size("ctx") - 1 - ctx)


def pack_keys(heads, key, value, *refs):
    own, near, sends, sems = refs[0], refs[1], refs[2:-1], refs[-1]
    me = lax.axis_index("head")
    pairs = []
    for half in range(2):
        for t in range(heads):
            there = own.at[half] if t == 0 else near.at[half] if t == 1 else sends[half * (heads - 2) + t - 2]
            for i, array in enumerate((key, value)):
                pairs.append((array.at[0, slot_of(half), :, lanes(me ^ t)], there.at[i]))
    carry(pairs, sems)


def load_queries(doc_start, query, d_out, starts_near, query_near, d_out_near, sems):
    carry([(doc_start, starts_near), (query, query_near), (d_out, d_out_near)], sems)


def join_keys(heads, half, own, near, *refs):
    parts, (span, rim) = refs[: heads - 2], refs[heads - 2 :]
    me = lax.axis_index("head")
    for t in range(heads):
        part = own.at[half] if t == 0 else near.at[half] if t == 1 else parts[t - 2]
        span[0, rows(me ^ t), :] = part[0]
        span[1, rows(me ^ t), :] = part[1]
    rim[...] = span[:, (heads - REACH) * BLK :, :]


def dot(a, b, ca, cb):
    return lax.dot_general(a, b, (((ca,), (cb,)), ((), ())), preferred_element_type=F32)


def products(task):
    n, first, queries, grads, keys, d_queries = task
    count = queries.shape[1] // HD
    window = pl.ds(first * BLK, n * BLK)
    k, v = keys[0, window, :], keys[1, window, :]
    q = jnp.concatenate([queries[:, j * HD : (j + 1) * HD] for j in range(count)], axis=0)
    do = jnp.concatenate([grads[:, j * HD : (j + 1) * HD] for j in range(count)], axis=0)
    return k, q, do, dot(k, q, 1, 1), dot(v, do, 1, 1)


def weigh(task, k, q, do, s, dp):
    n = task[0]
    seen = lax.broadcasted_iota(jnp.int32, (BLK, BLK), 0) <= lax.broadcasted_iota(jnp.int32, (BLK, BLK), 1)
    hide = jnp.where(seen, 0.0, -jnp.inf)
    ps, dss = [], []
    for j in range(s.shape[1] // BLK):
        p_, ds_ = weigh_head(n, hide, s[:, j * BLK : (j + 1) * BLK], dp[:, j * BLK : (j + 1) * BLK])
        ps.append(p_)
        dss.append(ds_)
    return k, q, do, jnp.concatenate(ps, axis=1), jnp.concatenate(dss, axis=1)


def weigh_head(n, hide, s, dp):
    last = s[(n - 1) * BLK :] + hide
    return weigh_all(jnp.concatenate([s[: (n - 1) * BLK], last], axis=0) if n > 1 else last, dp)


def weigh_all(s, dp):
    peak = jnp.max(s, axis=0, keepdims=True)
    w = jnp.exp2((s - peak) * SCALE_LOG2E)
    inverse = 1.0 / jnp.sum(w, axis=0, keepdims=True)
    delta = jnp.sum(w * dp, axis=0, keepdims=True) * inverse
    p = w * inverse
    return p.astype(BF16), (p * (dp - delta)).astype(BF16)


def gather(task, d_keys, k, q, do, p, ds):
    n, first, queries, grads, keys, d_queries = task
    window = pl.ds(first * BLK, n * BLK)
    d_keys[0, window, :] += dot(ds, q, 1, 0) * SCALE
    d_keys[1, window, :] += dot(p, do, 1, 0)
    dq = (dot(k.T, ds, 1, 0) * SCALE).astype(BF16)
    for j in range(dq.shape[1] // BLK):
        d_queries[:, j * HD : (j + 1) * HD] = dq[:, j * BLK : (j + 1) * BLK].T


def pair_grads(a, b, d_keys):
    pa = products(a)
    wa = weigh(a, *pa)
    pb = products(b)
    gather(a, d_keys, *wa)
    wb = weigh(b, *pb)
    gather(b, d_keys, *wb)


def loose_grads(reach, first_block, slot, visible, query, d_out, keys, d_query, d_keys):
    group = 4
    steps = query.shape[3] // (group * HD)
    seen_rows = (reach + 1) * BLK

    def step(i, carried):
        b, g = i // steps, lax.rem(i, steps)
        tokens = rows(first_block + b)
        window = rows(b + REACH - reach, reach + 1)
        columns = [lanes(g * group + j) for j in range(group)]
        q = jnp.concatenate([query[0, slot, tokens, c] for c in columns], axis=0)
        do = jnp.concatenate([d_out[0, slot, tokens, c] for c in columns], axis=0)
        k, v = keys[0, window, :], keys[1, window, :]
        count = jnp.where(b == 0, visible[0], visible[1])
        place = lax.broadcasted_iota(jnp.int32, (seen_rows, BLK), 0)
        token = lax.broadcasted_iota(jnp.int32, (seen_rows, BLK), 1)
        seen = (place >= (reach + 1 - count) * BLK) & (place - reach * BLK <= token)
        hide = jnp.where(seen, 0.0, -jnp.inf)
        s, dp = dot(k, q, 1, 1), dot(v, do, 1, 1)
        p, ds = weigh_all(s + jnp.concatenate([hide] * group, axis=1), dp)
        d_keys[0, window, :] += dot(ds, q, 1, 0) * SCALE
        d_keys[1, window, :] += dot(p, do, 1, 0)
        dq = (dot(k.T, ds, 1, 0) * SCALE).astype(BF16)
        for j, c in enumerate(columns):
            d_query[rows(b), c] = dq[:, j * BLK : (j + 1) * BLK].T
        return carried

    lax.fori_loop(0, 2 * steps, step, 0)


def span_part(fast, reach, first_block, per_span, half, doc_start, query, d_out, keys, d_query, d_keys):
    slot = slot_of(half)
    d_keys[...] = jnp.zeros_like(d_keys)
    spot = lax.broadcasted_iota(jnp.int32, doc_start.shape, 1)
    marks = doc_start[...].astype(F32)
    visible = []
    for b in range(2):
        block = span_of(half) * per_span + first_block + b
        mark = jnp.sum(jnp.where(spot == block, 2 * marks, jnp.where(spot == block - 1, marks, 0.0)))
        visible.append(jnp.where(mark > 1.5, 1, jnp.where(mark > 0.5, 2, 3)))

    def task(b, n):
        tokens = pl.ds((first_block + b) * BLK, BLK)
        return (
            n,
            b + REACH + 1 - n,
            query.at[0, slot, tokens, :],
            d_out.at[0, slot, tokens, :],
            keys,
            d_query.at[pl.ds(b * BLK, BLK), :],
        )

    common = [(n, then) for n in range(1, REACH + 2) for then in (1, n + 1) if then <= REACH + 1]
    common = [case for case in common if case in fast]
    chosen = False
    for n, then in common:
        here = (visible[0] == n) & (visible[1] == then)
        chosen = here | chosen

        @pl.when(here)
        def _(n=n, then=then):
            pair_grads(task(0, n), task(1, then), d_keys)

    @pl.when(jnp.logical_not(chosen))
    def _():
        loose_grads(reach, first_block, slot, visible, query, d_out, keys, d_query, d_keys)


def late_blocks(per_span, half, doc_start, query, d_out, keys, d_query, d_keys):
    span_part(LATE, REACH, REACH, per_span, half, doc_start, query, d_out, keys, d_query, d_keys)


def early_blocks(per_span, half, doc_start, query, d_out, keys, other, incoming, d_query, d_own, d_rim, window, d_window):
    cut = REACH * BLK
    window[:, cut:, :] = keys[:, :cut, :]
    window[:, :cut, :] = incoming[...]
    if half == 1:

        @pl.when(is_last())
        def _():
            window[:, :cut, :] = other[:, (per_span - REACH) * BLK :, :]

    span_part(EARLY, REACH - 1, 0, per_span, half, doc_start, query, d_out, window, d_query, d_window)
    d_rim[...] = d_window[:, :cut, :].astype(BF16)
    d_own[...] = d_window[:, cut:, :]


def store_queries(reach, early_first, late_first, early_second, late_second, d_query, sems):
    pairs = []
    for half, parts in ((0, (early_first, late_first)), (1, (early_second, late_second))):
        for part, start in zip(parts, (0, reach * BLK)):
            pairs.append((part, d_query.at[0, slot_of(half), pl.ds(start, part.shape[0]), :]))
    carry(pairs, sems)


def pack_grads(heads, half, late, own, back, local, *refs):
    sends, total = refs[:-1], refs[-1]
    me = lax.axis_index("head")
    cut = REACH * BLK
    total[...] = late[...]
    total[:, :cut, :] += own[...]
    total[:, (heads - REACH) * BLK :, :] += back[...].astype(F32)
    if half == 0:

        @pl.when(is_last())
        def _():
            total[:, (heads - REACH) * BLK :, :] += local[...].astype(F32)

    for t in range(heads):
        sends[t][...] = total[:, rows(me ^ t), :].astype(BF16)


def join_grads(heads, half, *refs):
    parts, (d_key, d_value, sems) = refs[:heads], refs[-3:]
    me = lax.axis_index("head")
    pairs = []
    for t in range(heads):
        for i, array in enumerate((d_key, d_value)):
            pairs.append((parts[t].at[i], array.at[0, slot_of(half), :, lanes(me ^ t)]))
    carry(pairs, sems)


def per_device(query, key, value, d_out, doc_start):
    ctx_count, heads = lax.axis_size("ctx"), lax.axis_size("head")
    block = shape((2, BLK, HD))
    partners = range(1, heads)
    swap = lambda x, t: lax.ppermute(x, "head", [(i, i ^ t) for i in range(heads)])
    outer = [p for i in range(1, ctx_count - 1, 2) for p in ((i, i + 1), (i + 1, i))]
    inner = [p for i in range(0, ctx_count, 2) for p in ((i, i + 1), (i + 1, i))]
    to_outer = lambda x: lax.ppermute(x, "ctx", outer)
    to_inner = lambda x: lax.ppermute(x, "ctx", inner)

    key, value, query, d_out = (
        pltpu.with_memory_space_constraint(x, pltpu.HBM) for x in (key, value, query, d_out)
    )
    own, near, *sends = call(
        functools.partial(pack_keys, heads),
        (key, value),
        [shape((2, 2, BLK, HD))] * 2 + [block] * (2 * (heads - 2)),
        scratch=[pltpu.SemaphoreType.DMA((4 * heads,))],
        far=(0, 1),
    )
    near = swap(near, 1)
    parts = [
        [swap(sends[half * (heads - 2) + t - 2], t) for t in range(2, heads)] for half in range(2)
    ]
    starts = pltpu.with_memory_space_constraint(doc_start[None], pltpu.HBM)
    starts, query, d_out = call(
        functools.partial(load_queries),
        (starts, query, d_out),
        [shape(starts.shape, jnp.int32), shape(query.shape), shape(d_out.shape)],
        scratch=[pltpu.SemaphoreType.DMA((3,))],
        moved=4 * query.size,
        far=(0, 1, 2),
        after=(own,),
    )
    def join(half, after):
        return call(
            functools.partial(join_keys, heads, half),
            (own, near, *parts[half]),
            [shape((2, heads * BLK, HD)), shape((2, REACH * BLK, HD))],
            after=after,
        )

    keys = [None, None]
    keys[0], rim = join(0, (query,))
    rim_second = to_outer(rim)

    def late(half, after):
        return call(
            functools.partial(late_blocks, heads, half),
            (starts, query, d_out, keys[half]),
            [shape(((heads - REACH) * BLK, query.shape[3])), shape((2, heads * BLK, HD), F32)],
            limit=20,
            after=after,
        )

    def early(half, incoming, after):
        return call(
            functools.partial(early_blocks, heads, half),
            (starts, query, d_out, keys[half], keys[1 - half], incoming),
            [
                shape((REACH * BLK, query.shape[3])),
                shape((2, REACH * BLK, HD), F32),
                shape((2, REACH * BLK, HD)),
            ],
            scratch=[
                pltpu.VMEM((2, 2 * REACH * BLK, HD), BF16),
                pltpu.VMEM((2, 2 * REACH * BLK, HD), F32),
            ],
            limit=20,
            after=after,
        )

    dq_late_first, late_first = late(0, ())
    keys[1], rim = join(1, (late_first,))
    rim_first = to_inner(rim)
    dq_late_second, late_second = late(1, (late_first,))
    dq_early_second, own_second, edge_second = early(1, rim_second, (late_second,))
    back_first = to_outer(edge_second)
    dq_early_first, own_first, edge_first = early(0, rim_first, (edge_second,))
    back_second = to_inner(edge_first)
    d_query = call(
        functools.partial(store_queries, REACH),
        (dq_early_first, dq_late_first, dq_early_second, dq_late_second),
        [shape(query.shape)],
        scratch=[pltpu.SemaphoreType.DMA((4,))],
        out_spec=ANY,
    )[0]

    d_keys, packed = (), ()
    for half, late_part, own_part, back, local in (
        (0, late_first, own_first, back_first, edge_second),
        (1, late_second, own_second, back_second, edge_first),
    ):
        packed = call(
            functools.partial(pack_grads, heads, half),
            (late_part, own_part, back, local),
            [block] * heads,
            scratch=[pltpu.VMEM((2, heads * BLK, HD), F32)],
            after=packed[:1],
        )
        inputs = (packed[0], *[swap(packed[t], t) for t in partners], *d_keys)
        d_keys = call(
            functools.partial(join_grads, heads, half),
            inputs,
            [shape(key.shape), shape(value.shape)],
            scratch=[pltpu.SemaphoreType.DMA((2 * heads,))],
            far=range(heads, len(inputs)),
            out_spec=HBM,
            aliases={heads + i: i for i in range(len(d_keys))},
        )
    d_key, d_value = d_keys
    return d_query, d_key, d_value


def solution(mesh):
    tokens = P("ctx", None, "head", None)
    columns = P("ctx", None, None, "head")
    return jax.shard_map(
        per_device,
        mesh=mesh,
        in_specs=(columns, tokens, tokens, columns, P()),
        out_specs=(columns, tokens, tokens),
        check_vma=False,
    )
```

profile of v0, /device:TPU:0, one launch (start us, length us, event | category | flops | bytes accessed | tf_op | source)
XLA Modules:
  0.0 38.2 jit_solution(7270335610301649756)
XLA Ops:
  0.6 1.2 %pack_keys.1 = (bf16[2,2,128,128]{3,2,1,0:T(8,128)(2,1)S(1)}, bf16[2,2,128,128]{3,2,1,0:T(8,128)(2,1)S(1)}, bf16[2,128,128]{2,1,0:T(8,128)(2,1)S(1)}, bf16[2,128...) custom-call(bf16[1,2,128,512]{3,2,1,0:T(8,128)(2,1)} %refs_0_.1, ...), custom_call_target="tpu_custom_call" | custom-call | tf_op jit(solution)/shard_map/pack_keys/pallas_call | solution.py:34
  1.8 0.5 %collective-permute-start = (bf16[2,2,128,128]{3,2,1,0:T(8,128)(2,1)S(1)}, bf16[2,2,128,128]{3,2,1,0:T(8,128)(2,1)S(1)}, u32[]{:S(2)}, u32[]{:S(2)}) collective-permute-start(bf16[2,2,128,128]{3,2,1,0:T(8,128)(2,1)S(1)} %get-tuple-element.42), channel_id=1, source_target_pairs={{0,1},{1,0},{2,3},{3,2},{4,5},{5,4},{6,7},{7,6},{8,9},{9,8},{10,11... | collective-permute-start | bytes 393224 | tf_op jit(solution)/shard_map/ppermute | solution.py:288
  2.3 2.6 %collective-permute-start.1 = (bf16[2,128,128]{2,1,0:T(8,128)(2,1)S(1)}, bf16[2,128,128]{2,1,0:T(8,128)(2,1)S(1)}, u32[]{:S(2)}, u32[]{:S(2)}) collective-permute-start(bf16[2,128,128]{2,1,0:T(8,128)(2,1)S(1)} %get-tuple-element.43), channel_id=1, source_target_pairs={{0,2},{1,3},{2,0},{3,1},{4,6},{5,7},{6,4},{7,5},{8,10},{9,11},{10,... | collective-permute-start | bytes 196616 | tf_op jit(solution)/shard_map/ppermute | solution.py:288
  4.9 0.1 collective-permute-start.2
  5.0 1.7 %collective-permute-start.3 = (bf16[2,128,128]{2,1,0:T(8,128)(2,1)S(1)}, bf16[2,128,128]{2,1,0:T(8,128)(2,1)S(1)}, u32[]{:S(2)}, u32[]{:S(2)}) collective-permute-start(bf16[2,128,128]{2,1,0:T(8,128)(2,1)S(1)} %get-tuple-element.47), channel_id=1, source_target_pairs={{0,2},{1,3},{2,0},{3,1},{4,6},{5,7},{6,4},{7,5},{8,10},{9,11},{10,... | collective-permute-start | bytes 196616 | tf_op jit(solution)/shard_map/ppermute | solution.py:288
  6.7 0.0 collective-permute-start.4
  6.7 2.3 %load_queries.1 = (s32[1,64]{1,0:T(1,128)S(1)}, bf16[1,2,512,1024]{3,2,1,0:T(8,128)(2,1)S(1)}, bf16[1,2,512,1024]{3,2,1,0:T(8,128)(2,1)S(1)}) custom-call(bf16[2,2,128,128]{3,2,1,0:T(8,128)(2,1)S(1)} %get-tuple-element.38.refs_0_.refs_1_, s32[1,64]{1,0:T(1,128)} %bitcast.1, bf16[1,2,512,1024]{3,2,1,0:T(8,128)(2,1)} %refs_2_.1, bf16[1,2,512,1024]{3,2,1,0:T(8,128)(2,1)} %refs_3_.1), custom_call_target="tpu_custom_call" | custom-call | bytes 4194304 | tf_op jit(solution)/shard_map/load_queries/pallas_call | solution.py:34
  9.0 0.0 collective-permute-done.1.refs_3_
  9.0 0.0 collective-permute-done.2.refs_4_
  9.0 0.0 collective-permute-done.refs_2_
  9.1 0.7 %collective-permute-start.5 = (bf16[2,256,128]{2,1,0:T(8,128)(2,1)S(1)}, bf16[2,256,128]{2,1,0:T(8,128)(2,1)S(1)}, u32[]{:S(2)}, u32[]{:S(2)}) collective-permute-start(bf16[2,256,128]{2,1,0:T(8,128)(2,1)S(1)} %get-tuple-element.51), channel_id=1, source_target_pairs={{4,8},{8,4},{12,16},{16,12},{20,24},{24,20},{5,9},{9,5},{13,17},{1... | collective-permute-start | bytes 393224 | tf_op jit(solution)/shard_map/ppermute | solution.py:291
  9.7 1.8 %late_blocks.2 = (bf16[256,1024]{1,0:T(8,128)(2,1)S(1)}, f32[2,512,128]{2,1,0:T(8,128)S(1)}) custom-call(s32[1,64]{1,0:T(1,128)S(1)} %get-tuple-element.39.refs_0_.refs_1_, bf16[1,2,512,1024]{3,2,1,0:T(8,128)(2,1)S(1)} %get-tuple-element.40.refs_0_.refs_1_.refs_2_, bf16[1,2,512,1024]{3,2,1,0:T(8,128)(2,1)S(1)} %get-tuple-element.41.refs_2_.refs_3_, ...), custom_call_target="tpu_custom_call" | custom-call | tf_op jit(solution)/shard_map/late_blocks/pallas_call | solution.py:34
  11.6 0.0 collective-permute-done.3.refs_3_
  11.6 0.2 collective-permute-done.4.refs_4_
  11.8 3.9 %collective-permute-start.6 = (bf16[2,256,128]{2,1,0:T(8,128)(2,1)S(1)}, bf16[2,256,128]{2,1,0:T(8,128)(2,1)S(1)}, u32[]{:S(2)}, u32[]{:S(2)}) collective-permute-start(bf16[2,256,128]{2,1,0:T(8,128)(2,1)S(1)} %get-tuple-element.53), channel_id=1, source_target_pairs={{0,4},{4,0},{8,12},{12,8},{16,20},{20,16},{24,28},{28,24},{1,5},{5... | collective-permute-start | bytes 393224 | tf_op jit(solution)/shard_map/ppermute | solution.py:292
  15.7 2.5 %late_blocks.3 = (bf16[256,1024]{1,0:T(8,128)(2,1)S(1)}, f32[2,512,128]{2,1,0:T(8,128)S(1)}) custom-call(f32[2,512,128]{2,1,0:T(8,128)S(1)} %get-tuple-element.46.refs_0_, s32[1,64]{1,0:T(1,128)S(1)} %get-tuple-element.39.refs_0_.refs_1_, bf16[1,2,512,1024]{3,2,1,0:T(8,128)(2,1)S(1)} %get-tuple-element.40.refs_0_.refs_1_.refs_2_, ...), custom_call_target="tpu_custom_call" | custom-call | tf_op jit(solution)/shard_map/late_blocks/pallas_call | solution.py:34
  18.1 0.0 collective-permute-done.5.refs_6_
  18.1 3.5 %early_blocks.2 = (bf16[256,1024]{1,0:T(8,128)(2,1)S(1)}, f32[2,256,128]{2,1,0:T(8,128)S(1)}, bf16[2,256,128]{2,1,0:T(8,128)(2,1)S(1)}) custom-call(f32[2,512,128]{2,1,0:T(8,128)S(1)} %get-tuple-element.50.refs_0_.refs_1_, s32[1,64]{1,0:T(1,128)S(1)} %get-tuple-element.39.refs_0_.refs_1_, ...), custom_call_target="tpu_custom_call" | custom-call | tf_op jit(solution)/shard_map/early_blocks/pallas_call | solution.py:34
  21.7 0.7 %collective-permute-start.7 = (bf16[2,256,128]{2,1,0:T(8,128)(2,1)S(1)}, bf16[2,256,128]{2,1,0:T(8,128)(2,1)S(1)}, u32[]{:S(2)}, u32[]{:S(2)}) collective-permute-start(bf16[2,256,128]{2,1,0:T(8,128)(2,1)S(1)} %get-tuple-element.52.refs_0_.refs_3_), channel_id=1, source_target_pairs={{4,8},{8,4},{12,16},{16,12},{20,24},{24,20},{5,9},{9,5},{13,17},{1... | collective-permute-start | bytes 393224 | tf_op jit(solution)/shard_map/ppermute | solution.py:291
  22.4 0.0 collective-permute-done.6.refs_6_
  22.4 2.5 %early_blocks.3 = (bf16[256,1024]{1,0:T(8,128)(2,1)S(1)}, f32[2,256,128]{2,1,0:T(8,128)S(1)}, bf16[2,256,128]{2,1,0:T(8,128)(2,1)S(1)}) custom-call(bf16[2,256,128]{2,1,0:T(8,128)(2,1)S(1)} %get-tuple-element.52.refs_0_.refs_3_, s32[1,64]{1,0:T(1,128)S(1)} %get-tuple-element.39.refs_0_.refs_1_, ...), custom_call_target="tpu_custom_call" | custom-call | tf_op jit(solution)/shard_map/early_blocks/pallas_call | solution.py:34
  24.9 3.6 %collective-permute-start.8 = (bf16[2,256,128]{2,1,0:T(8,128)(2,1)S(1)}, bf16[2,256,128]{2,1,0:T(8,128)(2,1)S(1)}, u32[]{:S(2)}, u32[]{:S(2)}) collective-permute-start(bf16[2,256,128]{2,1,0:T(8,128)(2,1)S(1)} %get-tuple-element.61.refs_4_), channel_id=1, source_target_pairs={{0,4},{4,0},{8,12},{12,8},{16,20},{20,16},{24,28},{28,24},{1,5},{5... | collective-permute-start | bytes 393224 | tf_op jit(solution)/shard_map/ppermute | solution.py:292
  28.5 0.0 collective-permute-done.7.refs_2_
  28.5 0.1 pack_grads.2
  28.6 0.1 collective-permute-start.12
  28.7 1.6 %collective-permute-start.13 = (bf16[2,128,128]{2,1,0:T(8,128)(2,1)S(1)}, bf16[2,128,128]{2,1,0:T(8,128)(2,1)S(1)}, u32[]{:S(2)}, u32[]{:S(2)}) collective-permute-start(bf16[2,128,128]{2,1,0:T(8,128)(2,1)S(1)} %get-tuple-element.67), channel_id=1, source_target_pairs={{0,2},{1,3},{2,0},{3,1},{4,6},{5,7},{6,4},{7,5},{8,10},{9,11},{10,... | collective-permute-start | bytes 196616 | tf_op jit(solution)/shard_map/ppermute | solution.py:288
  30.2 0.3 collective-permute-start.14
  30.5 0.9 %collective-permute-done.8.refs_3_ = bf16[2,256,128]{2,1,0:T(8,128)(2,1)S(1)} collective-permute-done((bf16[2,256,128]{2,1,0:T(8,128)(2,1)S(1)}, bf16[2,256,128]{2,1,0:T(8,128)(2,1)S(1)}, u32[]{:S(2)}, u32[]{:S(2)}) %collective-permute-start.8) | collective-permute-done | bytes 131104 | tf_op jit(solution)/shard_map/ppermute | solution.py:292
  31.5 0.1 pack_grads.3
  31.6 0.1 collective-permute-start.9
  31.6 1.6 %collective-permute-start.10 = (bf16[2,128,128]{2,1,0:T(8,128)(2,1)S(1)}, bf16[2,128,128]{2,1,0:T(8,128)(2,1)S(1)}, u32[]{:S(2)}, u32[]{:S(2)}) collective-permute-start(bf16[2,128,128]{2,1,0:T(8,128)(2,1)S(1)} %get-tuple-element.64), channel_id=1, source_target_pairs={{0,2},{1,3},{2,0},{3,1},{4,6},{5,7},{6,4},{7,5},{8,10},{9,11},{10,... | collective-permute-start | bytes 196616 | tf_op jit(solution)/shard_map/ppermute | solution.py:288
  33.2 0.0 collective-permute-done.12.refs_1_
  33.2 0.3 collective-permute-start.11
  33.5 1.3 %store_queries.1 = bf16[1,2,512,1024]{3,2,1,0:T(8,128)(2,1)} custom-call(bf16[256,1024]{1,0:T(8,128)(2,1)S(1)} %get-tuple-element.54.refs_0_, bf16[256,1024]{1,0:T(8,128)(2,1)S(1)} %get-tuple-element.55.refs_1_, bf16[256,1024]{1,0:T(8,128)(2,1)S(1)} %get-tuple-element.56.refs_2_, bf16[256,1024]{1,0:T(8,128)(2,1)S(1)} %get-tuple-element.57.refs_3_), custom_call_target="tpu_custom_call" | custom-call | tf_op jit(solution)/shard_map/store_queries/pallas_call | solution.py:34
  34.9 0.0 collective-permute-done.13.refs_2_
  34.9 0.0 collective-permute-done.14.refs_3_
  34.9 0.8 %join_grads.2 = (bf16[1,2,128,512]{3,2,1,0:T(8,128)(2,1)}, bf16[1,2,128,512]{3,2,1,0:T(8,128)(2,1)}) custom-call(bf16[2,128,128]{2,1,0:T(8,128)(2,1)S(1)} %get-tuple-element.59.refs_0_, bf16[2,128,128]{2,1,0:T(8,128)(2,1)S(1)} %collective-permute-done.12.refs_1_, bf16[2,128,128]{2,1,0:T(8,128)(2,1)S(1)} %collective-permute-done.13.refs_2_, ...), custom_call_target="tpu_custom_call" | custom-call | tf_op jit(solution)/shard_map/join_grads/pallas_call | solution.py:34
  35.7 0.0 collective-permute-done.9.refs_1_
  35.7 0.5 %collective-permute-done.10.refs_2_ = bf16[2,128,128]{2,1,0:T(8,128)(2,1)S(1)} collective-permute-done((bf16[2,128,128]{2,1,0:T(8,128)(2,1)S(1)}, bf16[2,128,128]{2,1,0:T(8,128)(2,1)S(1)}, u32[]{:S(2)}, u32[]{:S(2)}) %collective-permute-start.10) | collective-permute-done | bytes 65568 | tf_op jit(solution)/shard_map/ppermute | solution.py:288
  36.1 1.1 %collective-permute-done.11.refs_3_ = bf16[2,128,128]{2,1,0:T(8,128)(2,1)S(1)} collective-permute-done((bf16[2,128,128]{2,1,0:T(8,128)(2,1)S(1)}, bf16[2,128,128]{2,1,0:T(8,128)(2,1)S(1)}, u32[]{:S(2)}, u32[]{:S(2)}) %collective-permute-start.11) | collective-permute-done | bytes 65568 | tf_op jit(solution)/shard_map/ppermute | solution.py:288
  37.3 0.8 %join_grads.3 = (bf16[1,2,128,512]{3,2,1,0:T(8,128)(2,1)}, bf16[1,2,128,512]{3,2,1,0:T(8,128)(2,1)}) custom-call(bf16[2,128,128]{2,1,0:T(8,128)(2,1)S(1)} %get-tuple-element.62.refs_0_, bf16[2,128,128]{2,1,0:T(8,128)(2,1)S(1)} %collective-permute-done.9.refs_1_, ...), custom_call_target="tpu_custom_call", output_to_operand_aliasing={{0}: (4, {}), {1}: (5, {})} | custom-call | tf_op jit(solution)/shard_map/join_grads/pallas_call | solution.py:34
  (2 shorter events, 0.1 us)
Async XLA Ops:
  1.8 7.2 %collective-permute-start = (bf16[2,2,128,128]{3,2,1,0:T(8,128)(2,1)S(1)}, bf16[2,2,128,128]{3,2,1,0:T(8,128)(2,1)S(1)}, u32[]{:S(2)}, u32[]{:S(2)}) collective-permute-start(bf16[2,2,128,128]{3,2,1,0:T(8,128)(2,1)S(1)} %get-tuple-element.42), channel_id=1, source_target_pairs={{0,1},{1,0},{2,3},{3,2},{4,5},{5,4},{6,7},{7,6},{8,9},{9,8},{10,11... | collective-permute-start | bytes 393224 | tf_op jit(solution)/shard_map/ppermute | solution.py:288
  2.3 6.7 %collective-permute-start.1 = (bf16[2,128,128]{2,1,0:T(8,128)(2,1)S(1)}, bf16[2,128,128]{2,1,0:T(8,128)(2,1)S(1)}, u32[]{:S(2)}, u32[]{:S(2)}) collective-permute-start(bf16[2,128,128]{2,1,0:T(8,128)(2,1)S(1)} %get-tuple-element.43), channel_id=1, source_target_pairs={{0,2},{1,3},{2,0},{3,1},{4,6},{5,7},{6,4},{7,5},{8,10},{9,11},{10,... | collective-permute-start | bytes 196616 | tf_op jit(solution)/shard_map/ppermute | solution.py:288
  4.9 4.1 %collective-permute-start.2 = (bf16[2,128,128]{2,1,0:T(8,128)(2,1)S(1)}, bf16[2,128,128]{2,1,0:T(8,128)(2,1)S(1)}, u32[]{:S(2)}, u32[]{:S(2)}) collective-permute-start(bf16[2,128,128]{2,1,0:T(8,128)(2,1)S(1)} %get-tuple-element.44), channel_id=1, source_target_pairs={{0,3},{1,2},{2,1},{3,0},{4,7},{5,6},{6,5},{7,4},{8,11},{9,10},{10,... | collective-permute-start | bytes 196616 | tf_op jit(solution)/shard_map/ppermute | solution.py:288
  5.0 6.6 %collective-permute-start.3 = (bf16[2,128,128]{2,1,0:T(8,128)(2,1)S(1)}, bf16[2,128,128]{2,1,0:T(8,128)(2,1)S(1)}, u32[]{:S(2)}, u32[]{:S(2)}) collective-permute-start(bf16[2,128,128]{2,1,0:T(8,128)(2,1)S(1)} %get-tuple-element.47), channel_id=1, source_target_pairs={{0,2},{1,3},{2,0},{3,1},{4,6},{5,7},{6,4},{7,5},{8,10},{9,11},{10,... | collective-permute-start | bytes 196616 | tf_op jit(solution)/shard_map/ppermute | solution.py:288
  6.7 5.0 %collective-permute-start.4 = (bf16[2,128,128]{2,1,0:T(8,128)(2,1)S(1)}, bf16[2,128,128]{2,1,0:T(8,128)(2,1)S(1)}, u32[]{:S(2)}, u32[]{:S(2)}) collective-permute-start(bf16[2,128,128]{2,1,0:T(8,128)(2,1)S(1)} %get-tuple-element.48), channel_id=1, source_target_pairs={{0,3},{1,2},{2,1},{3,0},{4,7},{5,6},{6,5},{7,4},{8,11},{9,10},{10,... | collective-permute-start | bytes 196616 | tf_op jit(solution)/shard_map/ppermute | solution.py:288
  9.1 9.1 %collective-permute-start.5 = (bf16[2,256,128]{2,1,0:T(8,128)(2,1)S(1)}, bf16[2,256,128]{2,1,0:T(8,128)(2,1)S(1)}, u32[]{:S(2)}, u32[]{:S(2)}) collective-permute-start(bf16[2,256,128]{2,1,0:T(8,128)(2,1)S(1)} %get-tuple-element.51), channel_id=1, source_target_pairs={{4,8},{8,4},{12,16},{16,12},{20,24},{24,20},{5,9},{9,5},{13,17},{1... | collective-permute-start | bytes 393224 | tf_op jit(solution)/shard_map/ppermute | solution.py:291
  11.8 10.6 %collective-permute-start.6 = (bf16[2,256,128]{2,1,0:T(8,128)(2,1)S(1)}, bf16[2,256,128]{2,1,0:T(8,128)(2,1)S(1)}, u32[]{:S(2)}, u32[]{:S(2)}) collective-permute-start(bf16[2,256,128]{2,1,0:T(8,128)(2,1)S(1)} %get-tuple-element.53), channel_id=1, source_target_pairs={{0,4},{4,0},{8,12},{12,8},{16,20},{20,16},{24,28},{28,24},{1,5},{5... | collective-permute-start | bytes 393224 | tf_op jit(solution)/shard_map/ppermute | solution.py:292
  21.7 6.8 %collective-permute-start.7 = (bf16[2,256,128]{2,1,0:T(8,128)(2,1)S(1)}, bf16[2,256,128]{2,1,0:T(8,128)(2,1)S(1)}, u32[]{:S(2)}, u32[]{:S(2)}) collective-permute-start(bf16[2,256,128]{2,1,0:T(8,128)(2,1)S(1)} %get-tuple-element.52.refs_0_.refs_3_), channel_id=1, source_target_pairs={{4,8},{8,4},{12,16},{16,12},{20,24},{24,20},{5,9},{9,5},{13,17},{1... | collective-permute-start | bytes 393224 | tf_op jit(solution)/shard_map/ppermute | solution.py:291
  24.9 6.6 %collective-permute-start.8 = (bf16[2,256,128]{2,1,0:T(8,128)(2,1)S(1)}, bf16[2,256,128]{2,1,0:T(8,128)(2,1)S(1)}, u32[]{:S(2)}, u32[]{:S(2)}) collective-permute-start(bf16[2,256,128]{2,1,0:T(8,128)(2,1)S(1)} %get-tuple-element.61.refs_4_), channel_id=1, source_target_pairs={{0,4},{4,0},{8,12},{12,8},{16,20},{20,16},{24,28},{28,24},{1,5},{5... | collective-permute-start | bytes 393224 | tf_op jit(solution)/shard_map/ppermute | solution.py:292
  28.6 4.6 %collective-permute-start.12 = (bf16[2,128,128]{2,1,0:T(8,128)(2,1)S(1)}, bf16[2,128,128]{2,1,0:T(8,128)(2,1)S(1)}, u32[]{:S(2)}, u32[]{:S(2)}) collective-permute-start(bf16[2,128,128]{2,1,0:T(8,128)(2,1)S(1)} %get-tuple-element.66), channel_id=1, source_target_pairs={{0,1},{1,0},{2,3},{3,2},{4,5},{5,4},{6,7},{7,6},{8,9},{9,8},{10,11... | collective-permute-start | bytes 196616 | tf_op jit(solution)/shard_map/ppermute | solution.py:288
  28.7 6.2 %collective-permute-start.13 = (bf16[2,128,128]{2,1,0:T(8,128)(2,1)S(1)}, bf16[2,128,128]{2,1,0:T(8,128)(2,1)S(1)}, u32[]{:S(2)}, u32[]{:S(2)}) collective-permute-start(bf16[2,128,128]{2,1,0:T(8,128)(2,1)S(1)} %get-tuple-element.67), channel_id=1, source_target_pairs={{0,2},{1,3},{2,0},{3,1},{4,6},{5,7},{6,4},{7,5},{8,10},{9,11},{10,... | collective-permute-start | bytes 196616 | tf_op jit(solution)/shard_map/ppermute | solution.py:288
  30.2 4.6 %collective-permute-start.14 = (bf16[2,128,128]{2,1,0:T(8,128)(2,1)S(1)}, bf16[2,128,128]{2,1,0:T(8,128)(2,1)S(1)}, u32[]{:S(2)}, u32[]{:S(2)}) collective-permute-start(bf16[2,128,128]{2,1,0:T(8,128)(2,1)S(1)} %get-tuple-element.68), channel_id=1, source_target_pairs={{0,3},{1,2},{2,1},{3,0},{4,7},{5,6},{6,5},{7,4},{8,11},{9,10},{10,... | collective-permute-start | bytes 196616 | tf_op jit(solution)/shard_map/ppermute | solution.py:288
  31.6 4.1 %collective-permute-start.9 = (bf16[2,128,128]{2,1,0:T(8,128)(2,1)S(1)}, bf16[2,128,128]{2,1,0:T(8,128)(2,1)S(1)}, u32[]{:S(2)}, u32[]{:S(2)}) collective-permute-start(bf16[2,128,128]{2,1,0:T(8,128)(2,1)S(1)} %get-tuple-element.63), channel_id=1, source_target_pairs={{0,1},{1,0},{2,3},{3,2},{4,5},{5,4},{6,7},{7,6},{8,9},{9,8},{10,11... | collective-permute-start | bytes 196616 | tf_op jit(solution)/shard_map/ppermute | solution.py:288
  31.6 4.5 %collective-permute-start.10 = (bf16[2,128,128]{2,1,0:T(8,128)(2,1)S(1)}, bf16[2,128,128]{2,1,0:T(8,128)(2,1)S(1)}, u32[]{:S(2)}, u32[]{:S(2)}) collective-permute-start(bf16[2,128,128]{2,1,0:T(8,128)(2,1)S(1)} %get-tuple-element.64), channel_id=1, source_target_pairs={{0,2},{1,3},{2,0},{3,1},{4,6},{5,7},{6,4},{7,5},{8,10},{9,11},{10,... | collective-permute-start | bytes 196616 | tf_op jit(solution)/shard_map/ppermute | solution.py:288
  33.2 4.0 %collective-permute-start.11 = (bf16[2,128,128]{2,1,0:T(8,128)(2,1)S(1)}, bf16[2,128,128]{2,1,0:T(8,128)(2,1)S(1)}, u32[]{:S(2)}, u32[]{:S(2)}) collective-permute-start(bf16[2,128,128]{2,1,0:T(8,128)(2,1)S(1)} %get-tuple-element.65), channel_id=1, source_target_pairs={{0,3},{1,2},{2,1},{3,0},{4,7},{5,6},{6,5},{7,4},{8,11},{9,10},{10,... | collective-permute-start | bytes 196616 | tf_op jit(solution)/shard_map/ppermute | solution.py:288
where the time goes:
time: 38.1 us; the launch traced here: 38.2 us
  starting transfers between devices  17.6 us (46%)
  Pallas kernels  16.8 us (44%)
  waiting for transfers between devices  2.72 us (7%)
  between operations  1.01 us (3%)
    pallas_call x13, Pallas kernels, call(): pl.pallas_call(lambda *refs: body(*refs[skip:]), out_shape=outs, in_specs...  16.8 us
    ppermute x11, starting transfers between devices, per_device(): lax.ppermute(x, 'head', [(i, i ^ t) for i in range(heads)])  8.76 us
    ppermute x2, starting transfers between devices, per_device(): to_inner = lambda x: lax.ppermute(x, 'ctx', inner)  7.52 us
    ppermute x11, waiting for transfers between devices, per_device(): lax.ppermute(x, 'head', [(i, i ^ t) for i in range(heads)])  1.78 us
    ppermute x2, starting transfers between devices, per_device(): to_outer = lambda x: lax.ppermute(x, 'ctx', outer)  1.34 us
    ppermute x2, waiting for transfers between devices, per_device(): to_inner = lambda x: lax.ppermute(x, 'ctx', inner)  0.94 us
  transfers between devices with their start and end apart: 15, of which 4 were waited for; matrix products, arithmetic and copies ran while one was open for 0% of the time, Pallas kernels for 39%

commit v1 on v0

--- a/solution.py
+++ b/solution.py
@@ -74,20 +74,57 @@
     return jnp.where(slot_of(half) == 0, ctx, 2 * lax.axis_size("ctx") - 1 - ctx)
 
 
-def pack_keys(heads, key, value, *refs):
-    own, near, sends, sems = refs[0], refs[1], refs[2:-1], refs[-1]
+def far_blocks(heads, half, key, value, sends):
     me = lax.axis_index("head")
-    pairs = []
-    for half in range(2):
-        for t in range(heads):
-            there = own.at[half] if t == 0 else near.at[half] if t == 1 else sends[half * (heads - 2) + t - 2]
+    return [
+        (array.at[0, slot_of(half), :, lanes(me ^ t)], sends[t - 2].at[i])
+        for t in range(2, heads)
+        for i, array in enumerate((key, value))
+    ]
+
+
+def pack_keys(heads, key, value, own, near, *refs):
+    sends, sems = refs[:-1], refs[-1]
+    me = lax.axis_index("head")
+    pairs = far_blocks(heads, 0, key, value, sends)
+    for t, there in enumerate((own, near)):
+        for half in range(2):
             for i, array in enumerate((key, value)):
-                pairs.append((array.at[0, slot_of(half), :, lanes(me ^ t)], there.at[i]))
+                pairs.append((array.at[0, slot_of(half), :, lanes(me ^ t)], there.at[half, i]))
     carry(pairs, sems)
 
 
-def load_queries(doc_start, query, d_out, starts_near, query_near, d_out_near, sems):
-    carry([(doc_start, starts_near), (query, query_near), (d_out, d_out_near)], sems)
+def fetch_rows(what, query, d_out, query_near, d_out_near, sems):
+    half, first_block = what
+    there = lambda array: array.at[0, slot_of(half), pl.ds(first_block * BLK, REACH * BLK), :]
+    return [
+        pltpu.make_async_copy(there(query), query_near, sems.at[0]),
+        pltpu.make_async_copy(there(d_out), d_out_near, sems.at[1]),
+    ]
+
+
+def load_queries(heads, what, doc_start, key, value, query, d_out, starts_near, query_near, d_out_near, *refs):
+    sends, sems = refs[:-1], refs[-1]
+    pairs = far_blocks(heads, 1, key, value, sends) + [(doc_start, starts_near)]
+    copies = fetch_rows(what, query, d_out, query_near, d_out_near, sems)
+    copies += [pltpu.make_async_copy(here, there, sems.at[2 + i]) for i, (here, there) in enumerate(pairs)]
+    for copy in copies:
+        copy.start()
+    for copy in copies:
+        copy.wait()
+
+
+def while_fetching(what, body, inputs, refs):
+    if what is None:
+        return body(*inputs, *refs)
+    query, d_out, *refs, sems = refs
+    outs, near, scratch = refs[: what[2]], refs[what[2] : what[2] + 2], refs[what[2] + 2 :]
+    copies = fetch_rows(what[:2], query, d_out, *near, sems)
+    for copy in copies:
+        copy.start()
+    body(*inputs, *outs, *scratch)
+    for copy in copies:
+        copy.wait()
 
 
 def join_keys(heads, half, own, near, *refs):
@@ -159,18 +196,17 @@
     gather(b, d_keys, *wb)
 
 
-def loose_grads(reach, first_block, slot, visible, query, d_out, keys, d_query, d_keys):
+def loose_grads(reach, visible, query, d_out, keys, d_query, d_keys):
     group = 4
-    steps = query.shape[3] // (group * HD)
+    steps = query.shape[1] // (group * HD)
     seen_rows = (reach + 1) * BLK
 
     def step(i, carried):
         b, g = i // steps, lax.rem(i, steps)
-        tokens = rows(first_block + b)
         window = rows(b + REACH - reach, reach + 1)
         columns = [lanes(g * group + j) for j in range(group)]
-        q = jnp.concatenate([query[0, slot, tokens, c] for c in columns], axis=0)
-        do = jnp.concatenate([d_out[0, slot, tokens, c] for c in columns], axis=0)
+        q = jnp.concatenate([query[rows(b), c] for c in columns], axis=0)
+        do = jnp.concatenate([d_out[rows(b), c] for c in columns], axis=0)
         k, v = keys[0, window, :], keys[1, window, :]
         count = jnp.where(b == 0, visible[0], visible[1])
         place = lax.broadcasted_iota(jnp.int32, (seen_rows, BLK), 0)
@@ -190,7 +226,6 @@
 
 
 def span_part(fast, reach, first_block, per_span, half, doc_start, query, d_out, keys, d_query, d_keys):
-    slot = slot_of(half)
     d_keys[...] = jnp.zeros_like(d_keys)
     spot = lax.broadcasted_iota(jnp.int32, doc_start.shape, 1)
     marks = doc_start[...].astype(F32)
@@ -201,12 +236,11 @@
         visible.append(jnp.where(mark > 1.5, 1, jnp.where(mark > 0.5, 2, 3)))
 
     def task(b, n):
-        tokens = pl.ds((first_block + b) * BLK, BLK)
         return (
             n,
             b + REACH + 1 - n,
-            query.at[0, slot, tokens, :],
-            d_out.at[0, slot, tokens, :],
+            query.at[pl.ds(b * BLK, BLK), :],
+            d_out.at[pl.ds(b * BLK, BLK), :],
             keys,
             d_query.at[pl.ds(b * BLK, BLK), :],
         )
@@ -224,26 +258,32 @@
 
     @pl.when(jnp.logical_not(chosen))
     def _():
-        loose_grads(reach, first_block, slot, visible, query, d_out, keys, d_query, d_keys)
-
-
-def late_blocks(per_span, half, doc_start, query, d_out, keys, d_query, d_keys):
-    span_part(LATE, REACH, REACH, per_span, half, doc_start, query, d_out, keys, d_query, d_keys)
-
-
-def early_blocks(per_span, half, doc_start, query, d_out, keys, other, incoming, d_query, d_own, d_rim, window, d_window):
-    cut = REACH * BLK
-    window[:, cut:, :] = keys[:, :cut, :]
-    window[:, :cut, :] = incoming[...]
-    if half == 1:
-
-        @pl.when(is_last())
-        def _():
-            window[:, :cut, :] = other[:, (per_span - REACH) * BLK :, :]
-
-    span_part(EARLY, REACH - 1, 0, per_span, half, doc_start, query, d_out, window, d_query, d_window)
-    d_rim[...] = d_window[:, :cut, :].astype(BF16)
-    d_own[...] = d_window[:, cut:, :]
+        loose_grads(reach, visible, query, d_out, keys, d_query, d_keys)
+
+
+def late_blocks(per_span, half, what, doc_start, query, d_out, keys, *refs):
+    def body(doc_start, query, d_out, keys, d_query, d_keys):
+        span_part(LATE, REACH, REACH, per_span, half, doc_start, query, d_out, keys, d_query, d_keys)
+
+    while_fetching(what, body, (doc_start, query, d_out, keys), refs)
+
+
+def early_blocks(per_span, half, what, doc_start, query, d_out, keys, other, incoming, *refs):
+    def body(doc_start, query, d_out, keys, other, incoming, d_query, d_own, d_rim, window, d_window):
+        cut = REACH * BLK
+        window[:, cut:, :] = keys[:, :cut, :]
+        window[:, :cut, :] = incoming[...]
+        if half == 1:
+
+            @pl.when(is_last())
+            def _():
+                window[:, :cut, :] = other[:, (per_span - REACH) * BLK :, :]
+
+        span_part(EARLY, REACH - 1, 0, per_span, half, doc_start, query, d_out, window, d_query, d_window)
+        d_rim[...] = d_window[:, :cut, :].astype(BF16)
+        d_own[...] = d_window[:, cut:, :]
+
+    while_fetching(what, body, (doc_start, query, d_out, keys, other, incoming), refs)
 
 
 def store_queries(reach, early_first, late_first, early_second, late_second, d_query, sems):
@@ -297,24 +337,26 @@
     own, near, *sends = call(
         functools.partial(pack_keys, heads),
         (key, value),
-        [shape((2, 2, BLK, HD))] * 2 + [block] * (2 * (heads - 2)),
-        scratch=[pltpu.SemaphoreType.DMA((4 * heads,))],
+        [shape((2, 2, BLK, HD))] * 2 + [block] * (heads - 2),
+        scratch=[pltpu.SemaphoreType.DMA((4 + 2 * heads,))],
         far=(0, 1),
     )
     near = swap(near, 1)
-    parts = [
-        [swap(sends[half * (heads - 2) + t - 2], t) for t in range(2, heads)] for half in range(2)
-    ]
+    parts = [[swap(sends[t - 2], t) for t in range(2, heads)]]
     starts = pltpu.with_memory_space_constraint(doc_start[None], pltpu.HBM)
-    starts, query, d_out = call(
-        functools.partial(load_queries),
-        (starts, query, d_out),
-        [shape(starts.shape, jnp.int32), shape(query.shape), shape(d_out.shape)],
-        scratch=[pltpu.SemaphoreType.DMA((3,))],
+    two_blocks = shape((REACH * BLK, query.shape[3]))
+    starts, *spans = call(
+        functools.partial(load_queries, heads, (0, REACH)),
+        (starts, key, value, query, d_out),
+        [shape(starts.shape, jnp.int32), two_blocks, two_blocks] + [block] * (heads - 2),
+        scratch=[pltpu.SemaphoreType.DMA((2 * heads - 1,))],
         moved=4 * query.size,
-        far=(0, 1, 2),
+        far=range(5),
         after=(own,),
     )
+    spans, sends = spans[:2], spans[2:]
+    parts.append([swap(sends[t - 2], t) for t in range(2, heads)])
+
     def join(half, after):
         return call(
             functools.partial(join_keys, heads, half),
@@ -324,42 +366,44 @@
         )
 
     keys = [None, None]
-    keys[0], rim = join(0, (query,))
+    keys[0], rim = join(0, (spans[0],))
     rim_second = to_outer(rim)
 
-    def late(half, after):
+    def grads(body, half, spans, more, outs, then, after, scratch=()):
+        inputs = (starts, *spans, keys[half], *more)
+        what = None
+        if then is not None:
+            what = (*then, len(outs))
+            far = (len(inputs), len(inputs) + 1)
+            inputs, outs = (*inputs, query, d_out), [*outs, two_blocks, two_blocks]
+            scratch = [*scratch, pltpu.SemaphoreType.DMA((2,))]
         return call(
-            functools.partial(late_blocks, heads, half),
-            (starts, query, d_out, keys[half]),
-            [shape(((heads - REACH) * BLK, query.shape[3])), shape((2, heads * BLK, HD), F32)],
+            functools.partial(body, heads, half, what),
+            inputs,
+            outs,
+            scratch=scratch,
+            far=() if what is None else far,
             limit=20,
             after=after,
         )
 
-    def early(half, incoming, after):
-        return call(
-            functools.partial(early_blocks, heads, half),
-            (starts, query, d_out, keys[half], keys[1 - half], incoming),
-            [
-                shape((REACH * BLK, query.shape[3])),
-                shape((2, REACH * BLK, HD), F32),
-                shape((2, REACH * BLK, HD)),
-            ],
-            scratch=[
-                pltpu.VMEM((2, 2 * REACH * BLK, HD), BF16),
-                pltpu.VMEM((2, 2 * REACH * BLK, HD), F32),
-            ],
-            limit=20,
-            after=after,
-        )
-
-    dq_late_first, late_first = late(0, ())
+    def late(half, spans, then, after):
+        outs = [two_blocks, shape((2, heads * BLK, HD), F32)]
+        return grads(late_blocks, half, spans, (), outs, then, after)
+
+    def early(half, spans, incoming, then, after):
+        outs = [two_blocks, shape((2, REACH * BLK, HD), F32), shape((2, REACH * BLK, HD))]
+        window = (2, 2 * REACH * BLK, HD)
+        scratch = [pltpu.VMEM(window, BF16), pltpu.VMEM(window, F32)]
+        return grads(early_blocks, half, spans, (keys[1 - half], incoming), outs, then, after, scratch)
+
+    dq_late_first, late_first, *spans = late(0, spans, (1, REACH), ())
     keys[1], rim = join(1, (late_first,))
     rim_first = to_inner(rim)
-    dq_late_second, late_second = late(1, (late_first,))
-    dq_early_second, own_second, edge_second = early(1, rim_second, (late_second,))
+    dq_late_second, late_second, *spans = late(1, spans, (1, 0), (late_first,))
+    dq_early_second, own_second, edge_second, *spans = early(1, spans, rim_second, (0, 0), (late_second,))
     back_first = to_outer(edge_second)
-    dq_early_first, own_first, edge_first = early(0, rim_first, (edge_second,))
+    dq_early_first, own_first, edge_first = early(0, spans, rim_first, None, (edge_second,))
     back_second = to_inner(edge_first)
     d_query = call(
         functools.partial(store_queries, REACH),

time: 38.1 us -> 37.7 us (0.990); the launches traced: 38.2 us -> 37 us
  starting transfers between devices: 17.6 us -> 14.7 us
  Pallas kernels: 16.8 us -> 18 us
  waiting for transfers between devices: 2.72 us -> 3.3 us
    ppermute x2, starting transfers between devices: 7.52 us -> 4.28 us  [per_device(): to_inner = lambda x: lax.ppermute(x, 'ctx', inner)]
    pallas_call x13, Pallas kernels: 16.8 us -> 18 us  [call(): pl.pallas_call(lambda *refs: body(*refs[skip:]), out_shape=outs, in_specs...]
    ppermute x11, waiting for transfers between devices: 1.78 us -> 2.36 us  [per_device(): lax.ppermute(x, 'head', [(i, i ^ t) for i in range(heads)])]
  transfers between devices with their start and end apart: 15 -> 15, of which waited for: 4 -> 4; matrix products, arithmetic and copies ran while one was open for 0% -> 0% of each run, Pallas kernels for 39% -> 44%
where the time goes in v1:
time: 37.7 us; the launch traced here: 37 us
  Pallas kernels  18 us (48%)
  starting transfers between devices  14.7 us (39%)
  waiting for transfers between devices  3.3 us (9%)
  between operations  0.98 us (3%)
    pallas_call x13, Pallas kernels, call(): pl.pallas_call(lambda *refs: body(*refs[skip:]), out_shape=outs, in_specs...  18 us
    ppermute x11, starting transfers between devices, per_device(): lax.ppermute(x, 'head', [(i, i ^ t) for i in range(heads)])  9.13 us
    ppermute x2, starting transfers between devices, per_device(): to_inner = lambda x: lax.ppermute(x, 'ctx', inner)  4.28 us
    ppermute x11, waiting for transfers between devices, per_device(): lax.ppermute(x, 'head', [(i, i ^ t) for i in range(heads)])  2.36 us
    ppermute x2, starting transfers between devices, per_device(): to_outer = lambda x: lax.ppermute(x, 'ctx', outer)  1.34 us
    ppermute x2, waiting for transfers between devices, per_device(): to_inner = lambda x: lax.ppermute(x, 'ctx', inner)  0.94 us
  transfers between devices with their start and end apart: 15, of which 4 were waited for; matrix products, arithmetic and copies ran while one was open for 0% of the time, Pallas kernels for 44%

profile of v1, /device:TPU:0, one launch (start us, length us, event | category | flops | bytes accessed | tf_op | source)
XLA Modules:
  0.0 37.0 jit_solution(13774719390402314038)
XLA Ops:
  0.6 1.1 %pack_keys.1 = (bf16[2,2,128,128]{3,2,1,0:T(8,128)(2,1)S(1)}, bf16[2,2,128,128]{3,2,1,0:T(8,128)(2,1)S(1)}, bf16[2,128,128]{2,1,0:T(8,128)(2,1)S(1)}, bf16[2,128,128]{2,1,0:T(8,128)(2,1)S(1)}) custom-call(bf16[1,2,128,512]{3,2,1,0:T(8,128)(2,1)} %refs_2_.1, bf16[1,2,128,512]{3,2,1,0:T(8,128)(2,1)} %refs_3_.1), custom_call_target="tpu_custom_call" | custom-call | tf_op jit(solution)/shard_map/pack_keys/pallas_call | solution.py:34
  1.7 0.5 %collective-permute-start = (bf16[2,2,128,128]{3,2,1,0:T(8,128)(2,1)S(1)}, bf16[2,2,128,128]{3,2,1,0:T(8,128)(2,1)S(1)}, u32[]{:S(2)}, u32[]{:S(2)}) collective-permute-start(bf16[2,2,128,128]{3,2,1,0:T(8,128)(2,1)S(1)} %get-tuple-element.48), channel_id=1, source_target_pairs={{0,1},{1,0},{2,3},{3,2},{4,5},{5,4},{6,7},{7,6},{8,9},{9,8},{10,11... | collective-permute-start | bytes 393224 | tf_op jit(solution)/shard_map/ppermute | solution.py:328
  2.2 2.6 %collective-permute-start.1 = (bf16[2,128,128]{2,1,0:T(8,128)(2,1)S(1)}, bf16[2,128,128]{2,1,0:T(8,128)(2,1)S(1)}, u32[]{:S(2)}, u32[]{:S(2)}) collective-permute-start(bf16[2,128,128]{2,1,0:T(8,128)(2,1)S(1)} %get-tuple-element.49), channel_id=1, source_target_pairs={{0,2},{1,3},{2,0},{3,1},{4,6},{5,7},{6,4},{7,5},{8,10},{9,11},{10,... | collective-permute-start | bytes 196616 | tf_op jit(solution)/shard_map/ppermute | solution.py:328
  4.8 0.1 collective-permute-start.2
  4.9 1.3 %load_queries.1 = (s32[1,64]{1,0:T(1,128)S(1)}, bf16[256,1024]{1,0:T(8,128)(2,1)S(1)}, bf16[256,1024]{1,0:T(8,128)(2,1)S(1)}, bf16[2,128,128]{2,1,0:T(8,128)(2,1)S(1)}, bf16[2,128,128]{2,1,0:T(8,128)(2,1)S(1)}) custom-call(bf16[2,2,128,128]{3,2,1,0:T(8,128)(2,1)S(1)} %get-tuple-element.44.refs_0_.refs_1_, s32[1,64]{1,0:T(1,128)} %bitcast.1, ...), custom_call_target="tpu_custom_call" | custom-call | bytes 4194304 | tf_op jit(solution)/shard_map/load_queries/pallas_call | solution.py:34
  6.1 1.8 %collective-permute-start.3 = (bf16[2,128,128]{2,1,0:T(8,128)(2,1)S(1)}, bf16[2,128,128]{2,1,0:T(8,128)(2,1)S(1)}, u32[]{:S(2)}, u32[]{:S(2)}) collective-permute-start(bf16[2,128,128]{2,1,0:T(8,128)(2,1)S(1)} %get-tuple-element.55), channel_id=1, source_target_pairs={{0,2},{1,3},{2,0},{3,1},{4,6},{5,7},{6,4},{7,5},{8,10},{9,11},{10,... | collective-permute-start | bytes 196616 | tf_op jit(solution)/shard_map/ppermute | solution.py:328
  7.9 0.0 collective-permute-start.4
  8.0 0.0 collective-permute-done.1.refs_3_
  8.0 0.9 %collective-permute-done.2.refs_4_ = bf16[2,128,128]{2,1,0:T(8,128)(2,1)S(1)} collective-permute-done((bf16[2,128,128]{2,1,0:T(8,128)(2,1)S(1)}, bf16[2,128,128]{2,1,0:T(8,128)(2,1)S(1)}, u32[]{:S(2)}, u32[]{:S(2)}) %collective-permute-start.2) | collective-permute-done | bytes 65568 | tf_op jit(solution)/shard_map/ppermute | solution.py:328
  8.8 0.0 collective-permute-done.refs_2_
  8.9 0.7 %collective-permute-start.5 = (bf16[2,256,128]{2,1,0:T(8,128)(2,1)S(1)}, bf16[2,256,128]{2,1,0:T(8,128)(2,1)S(1)}, u32[]{:S(2)}, u32[]{:S(2)}) collective-permute-start(bf16[2,256,128]{2,1,0:T(8,128)(2,1)S(1)} %get-tuple-element.61), channel_id=1, source_target_pairs={{4,8},{8,4},{12,16},{16,12},{20,24},{24,20},{5,9},{9,5},{13,17},{1... | collective-permute-start | bytes 393224 | tf_op jit(solution)/shard_map/ppermute | solution.py:331
  9.6 4.5 %late_blocks.2 = (bf16[256,1024]{1,0:T(8,128)(2,1)S(1)}, f32[2,512,128]{2,1,0:T(8,128)S(1)}, bf16[256,1024]{1,0:T(8,128)(2,1)S(1)}, bf16[256,1024]{1,0:T(8,128)(2,1)S(1)}) custom-call(s32[1,64]{1,0:T(1,128)S(1)} %get-tuple-element.45.refs_0_.refs_1_, bf16[256,1024]{1,0:T(8,128)(2,1)S(1)} %get-tuple-element.46.refs_0_.refs_1_, ...), custom_call_target="tpu_custom_call" | custom-call | tf_op jit(solution)/shard_map/late_blocks/pallas_call | solution.py:34
  14.1 0.0 collective-permute-done.3.refs_3_
  14.1 0.0 collective-permute-done.4.refs_4_
  14.1 1.6 %collective-permute-start.6 = (bf16[2,256,128]{2,1,0:T(8,128)(2,1)S(1)}, bf16[2,256,128]{2,1,0:T(8,128)(2,1)S(1)}, u32[]{:S(2)}, u32[]{:S(2)}) collective-permute-start(bf16[2,256,128]{2,1,0:T(8,128)(2,1)S(1)} %get-tuple-element.65), channel_id=1, source_target_pairs={{0,4},{4,0},{8,12},{12,8},{16,20},{20,16},{24,28},{28,24},{1,5},{5... | collective-permute-start | bytes 393224 | tf_op jit(solution)/shard_map/ppermute | solution.py:332
  15.8 2.0 %late_blocks.3 = (bf16[256,1024]{1,0:T(8,128)(2,1)S(1)}, f32[2,512,128]{2,1,0:T(8,128)S(1)}, bf16[256,1024]{1,0:T(8,128)(2,1)S(1)}, bf16[256,1024]{1,0:T(8,128)(2,1)S(1)}) custom-call(f32[2,512,128]{2,1,0:T(8,128)S(1)} %get-tuple-element.52.refs_0_, s32[1,64]{1,0:T(1,128)S(1)} %get-tuple-element.45.refs_0_.refs_1_, ...), custom_call_target="tpu_custom_call" | custom-call | tf_op jit(solution)/shard_map/late_blocks/pallas_call | solution.py:34
  17.7 0.0 collective-permute-done.5.refs_6_
  17.7 3.6 %early_blocks.2 = (bf16[256,1024]{1,0:T(8,128)(2,1)S(1)}, f32[2,256,128]{2,1,0:T(8,128)S(1)}, bf16[2,256,128]{2,1,0:T(8,128)(2,1)S(1)}, bf16[256,1024]{1,0:T(8,128)(2,1)S(1)}, bf16[256,1024]{1,0:T(8,128)(2,1)S(1)}) custom-call(f32[2,512,128]{2,1,0:T(8,128)S(1)} %get-tuple-element.58.refs_0_.refs_1_, s32[1,64]{1,0:T(1,128)S(1)} %get-tuple-element.45.refs_0_.refs_1_, ...), custom_call_target="tpu_custom_call" | custom-call | tf_op jit(solution)/shard_map/early_blocks/pallas_call | solution.py:34
  21.3 0.7 %collective-permute-start.7 = (bf16[2,256,128]{2,1,0:T(8,128)(2,1)S(1)}, bf16[2,256,128]{2,1,0:T(8,128)(2,1)S(1)}, u32[]{:S(2)}, u32[]{:S(2)}) collective-permute-start(bf16[2,256,128]{2,1,0:T(8,128)(2,1)S(1)} %get-tuple-element.62.refs_0_.refs_3_), channel_id=1, source_target_pairs={{4,8},{8,4},{12,16},{16,12},{20,24},{24,20},{5,9},{9,5},{13,17},{1... | collective-permute-start | bytes 393224 | tf_op jit(solution)/shard_map/ppermute | solution.py:331
  22.0 0.0 collective-permute-done.6.refs_6_
  22.0 2.5 %early_blocks.3 = (bf16[256,1024]{1,0:T(8,128)(2,1)S(1)}, f32[2,256,128]{2,1,0:T(8,128)S(1)}, bf16[2,256,128]{2,1,0:T(8,128)(2,1)S(1)}) custom-call(bf16[2,256,128]{2,1,0:T(8,128)(2,1)S(1)} %get-tuple-element.62.refs_0_.refs_3_, s32[1,64]{1,0:T(1,128)S(1)} %get-tuple-element.45.refs_0_.refs_1_, bf16[256,1024]{1,0:T(8,128)(2,1)S(1)} %get-tuple-element.63.refs_2_, ...), custom_call_target="tpu_custom_call" | custom-call | tf_op jit(solution)/shard_map/early_blocks/pallas_call | solution.py:34
  24.5 2.6 %collective-permute-start.8 = (bf16[2,256,128]{2,1,0:T(8,128)(2,1)S(1)}, bf16[2,256,128]{2,1,0:T(8,128)(2,1)S(1)}, u32[]{:S(2)}, u32[]{:S(2)}) collective-permute-start(bf16[2,256,128]{2,1,0:T(8,128)(2,1)S(1)} %get-tuple-element.73.refs_4_), channel_id=1, source_target_pairs={{0,4},{4,0},{8,12},{12,8},{16,20},{20,16},{24,28},{28,24},{1,5},{5... | collective-permute-start | bytes 393224 | tf_op jit(solution)/shard_map/ppermute | solution.py:332
  27.2 0.0 collective-permute-done.7.refs_2_
  27.2 0.1 pack_grads.2
  27.3 0.1 collective-permute-start.12
  27.3 1.5 %collective-permute-start.13 = (bf16[2,128,128]{2,1,0:T(8,128)(2,1)S(1)}, bf16[2,128,128]{2,1,0:T(8,128)(2,1)S(1)}, u32[]{:S(2)}, u32[]{:S(2)}) collective-permute-start(bf16[2,128,128]{2,1,0:T(8,128)(2,1)S(1)} %get-tuple-element.79), channel_id=1, source_target_pairs={{0,2},{1,3},{2,0},{3,1},{4,6},{5,7},{6,4},{7,5},{8,10},{9,11},{10,... | collective-permute-start | bytes 196616 | tf_op jit(solution)/shard_map/ppermute | solution.py:328
  28.9 0.3 collective-permute-start.14
  29.2 0.9 %collective-permute-done.8.refs_3_ = bf16[2,256,128]{2,1,0:T(8,128)(2,1)S(1)} collective-permute-done((bf16[2,256,128]{2,1,0:T(8,128)(2,1)S(1)}, bf16[2,256,128]{2,1,0:T(8,128)(2,1)S(1)}, u32[]{:S(2)}, u32[]{:S(2)}) %collective-permute-start.8) | collective-permute-done | bytes 131104 | tf_op jit(solution)/shard_map/ppermute | solution.py:332
  30.1 0.1 pack_grads.3
  30.2 1.5 %collective-permute-start.10 = (bf16[2,128,128]{2,1,0:T(8,128)(2,1)S(1)}, bf16[2,128,128]{2,1,0:T(8,128)(2,1)S(1)}, u32[]{:S(2)}, u32[]{:S(2)}) collective-permute-start(bf16[2,128,128]{2,1,0:T(8,128)(2,1)S(1)} %get-tuple-element.76), channel_id=1, source_target_pairs={{0,2},{1,3},{2,0},{3,1},{4,6},{5,7},{6,4},{7,5},{8,10},{9,11},{10,... | collective-permute-start | bytes 196616 | tf_op jit(solution)/shard_map/ppermute | solution.py:328
  31.7 0.0 collective-permute-start.11
  31.7 0.0 collective-permute-done.12.refs_1_
  31.7 0.7 %collective-permute-start.9 = (bf16[2,128,128]{2,1,0:T(8,128)(2,1)S(1)}, bf16[2,128,128]{2,1,0:T(8,128)(2,1)S(1)}, u32[]{:S(2)}, u32[]{:S(2)}) collective-permute-start(bf16[2,128,128]{2,1,0:T(8,128)(2,1)S(1)} %get-tuple-element.75), channel_id=1, source_target_pairs={{0,1},{1,0},{2,3},{3,2},{4,5},{5,4},{6,7},{7,6},{8,9},{9,8},{10,11... | collective-permute-start | bytes 196616 | tf_op jit(solution)/shard_map/ppermute | solution.py:328
  32.4 1.3 %store_queries.1 = bf16[1,2,512,1024]{3,2,1,0:T(8,128)(2,1)} custom-call(bf16[256,1024]{1,0:T(8,128)(2,1)S(1)} %get-tuple-element.66.refs_0_, bf16[256,1024]{1,0:T(8,128)(2,1)S(1)} %get-tuple-element.67.refs_1_, bf16[256,1024]{1,0:T(8,128)(2,1)S(1)} %get-tuple-element.68.refs_2_, bf16[256,1024]{1,0:T(8,128)(2,1)S(1)} %get-tuple-element.69.refs_3_), custom_call_target="tpu_custom_call" | custom-call | tf_op jit(solution)/shard_map/store_queries/pallas_call | solution.py:34
  33.8 0.0 collective-permute-done.13.refs_2_
  33.8 0.0 collective-permute-done.14.refs_3_
  33.8 0.8 %join_grads.2 = (bf16[1,2,128,512]{3,2,1,0:T(8,128)(2,1)}, bf16[1,2,128,512]{3,2,1,0:T(8,128)(2,1)}) custom-call(bf16[2,128,128]{2,1,0:T(8,128)(2,1)S(1)} %get-tuple-element.71.refs_0_, bf16[2,128,128]{2,1,0:T(8,128)(2,1)S(1)} %collective-permute-done.12.refs_1_, bf16[2,128,128]{2,1,0:T(8,128)(2,1)S(1)} %collective-permute-done.13.refs_2_, ...), custom_call_target="tpu_custom_call" | custom-call | tf_op jit(solution)/shard_map/join_grads/pallas_call | solution.py:34
  34.6 0.1 collective-permute-done.10.refs_2_
  34.6 1.4 %collective-permute-done.11.refs_3_ = bf16[2,128,128]{2,1,0:T(8,128)(2,1)S(1)} collective-permute-done((bf16[2,128,128]{2,1,0:T(8,128)(2,1)S(1)}, bf16[2,128,128]{2,1,0:T(8,128)(2,1)S(1)}, u32[]{:S(2)}, u32[]{:S(2)}) %collective-permute-start.11) | collective-permute-done | bytes 65568 | tf_op jit(solution)/shard_map/ppermute | solution.py:328
  36.1 0.0 collective-permute-done.9.refs_1_
  36.1 0.8 %join_grads.3 = (bf16[1,2,128,512]{3,2,1,0:T(8,128)(2,1)}, bf16[1,2,128,512]{3,2,1,0:T(8,128)(2,1)}) custom-call(bf16[2,128,128]{2,1,0:T(8,128)(2,1)S(1)} %get-tuple-element.74.refs_0_, bf16[2,128,128]{2,1,0:T(8,128)(2,1)S(1)} %collective-permute-done.9.refs_1_, ...), custom_call_target="tpu_custom_call", output_to_operand_aliasing={{0}: (4, {}), {1}: (5, {})} | custom-call | tf_op jit(solution)/shard_map/join_grads/pallas_call | solution.py:34
  (2 shorter events, 0.1 us)
Async XLA Ops:
  1.7 7.1 %collective-permute-start = (bf16[2,2,128,128]{3,2,1,0:T(8,128)(2,1)S(1)}, bf16[2,2,128,128]{3,2,1,0:T(8,128)(2,1)S(1)}, u32[]{:S(2)}, u32[]{:S(2)}) collective-permute-start(bf16[2,2,128,128]{3,2,1,0:T(8,128)(2,1)S(1)} %get-tuple-element.48), channel_id=1, source_target_pairs={{0,1},{1,0},{2,3},{3,2},{4,5},{5,4},{6,7},{7,6},{8,9},{9,8},{10,11... | collective-permute-start | bytes 393224 | tf_op jit(solution)/shard_map/ppermute | solution.py:328
  2.2 5.7 %collective-permute-start.1 = (bf16[2,128,128]{2,1,0:T(8,128)(2,1)S(1)}, bf16[2,128,128]{2,1,0:T(8,128)(2,1)S(1)}, u32[]{:S(2)}, u32[]{:S(2)}) collective-permute-start(bf16[2,128,128]{2,1,0:T(8,128)(2,1)S(1)} %get-tuple-element.49), channel_id=1, source_target_pairs={{0,2},{1,3},{2,0},{3,1},{4,6},{5,7},{6,4},{7,5},{8,10},{9,11},{10,... | collective-permute-start | bytes 196616 | tf_op jit(solution)/shard_map/ppermute | solution.py:328
  4.8 4.0 %collective-permute-start.2 = (bf16[2,128,128]{2,1,0:T(8,128)(2,1)S(1)}, bf16[2,128,128]{2,1,0:T(8,128)(2,1)S(1)}, u32[]{:S(2)}, u32[]{:S(2)}) collective-permute-start(bf16[2,128,128]{2,1,0:T(8,128)(2,1)S(1)} %get-tuple-element.50), channel_id=1, source_target_pairs={{0,3},{1,2},{2,1},{3,0},{4,7},{5,6},{6,5},{7,4},{8,11},{9,10},{10,... | collective-permute-start | bytes 196616 | tf_op jit(solution)/shard_map/ppermute | solution.py:328
  6.1 7.9 %collective-permute-start.3 = (bf16[2,128,128]{2,1,0:T(8,128)(2,1)S(1)}, bf16[2,128,128]{2,1,0:T(8,128)(2,1)S(1)}, u32[]{:S(2)}, u32[]{:S(2)}) collective-permute-start(bf16[2,128,128]{2,1,0:T(8,128)(2,1)S(1)} %get-tuple-element.55), channel_id=1, source_target_pairs={{0,2},{1,3},{2,0},{3,1},{4,6},{5,7},{6,4},{7,5},{8,10},{9,11},{10,... | collective-permute-start | bytes 196616 | tf_op jit(solution)/shard_map/ppermute | solution.py:328
  7.9 6.2 %collective-permute-start.4 = (bf16[2,128,128]{2,1,0:T(8,128)(2,1)S(1)}, bf16[2,128,128]{2,1,0:T(8,128)(2,1)S(1)}, u32[]{:S(2)}, u32[]{:S(2)}) collective-permute-start(bf16[2,128,128]{2,1,0:T(8,128)(2,1)S(1)} %get-tuple-element.56), channel_id=1, source_target_pairs={{0,3},{1,2},{2,1},{3,0},{4,7},{5,6},{6,5},{7,4},{8,11},{9,10},{10,... | collective-permute-start | bytes 196616 | tf_op jit(solution)/shard_map/ppermute | solution.py:328
  8.9 8.9 %collective-permute-start.5 = (bf16[2,256,128]{2,1,0:T(8,128)(2,1)S(1)}, bf16[2,256,128]{2,1,0:T(8,128)(2,1)S(1)}, u32[]{:S(2)}, u32[]{:S(2)}) collective-permute-start(bf16[2,256,128]{2,1,0:T(8,128)(2,1)S(1)} %get-tuple-element.61), channel_id=1, source_target_pairs={{4,8},{8,4},{12,16},{16,12},{20,24},{24,20},{5,9},{9,5},{13,17},{1... | collective-permute-start | bytes 393224 | tf_op jit(solution)/shard_map/ppermute | solution.py:331
  14.1 7.9 %collective-permute-start.6 = (bf16[2,256,128]{2,1,0:T(8,128)(2,1)S(1)}, bf16[2,256,128]{2,1,0:T(8,128)(2,1)S(1)}, u32[]{:S(2)}, u32[]{:S(2)}) collective-permute-start(bf16[2,256,128]{2,1,0:T(8,128)(2,1)S(1)} %get-tuple-element.65), channel_id=1, source_target_pairs={{0,4},{4,0},{8,12},{12,8},{16,20},{20,16},{24,28},{28,24},{1,5},{5... | collective-permute-start | bytes 393224 | tf_op jit(solution)/shard_map/ppermute | solution.py:332
  21.3 5.8 %collective-permute-start.7 = (bf16[2,256,128]{2,1,0:T(8,128)(2,1)S(1)}, bf16[2,256,128]{2,1,0:T(8,128)(2,1)S(1)}, u32[]{:S(2)}, u32[]{:S(2)}) collective-permute-start(bf16[2,256,128]{2,1,0:T(8,128)(2,1)S(1)} %get-tuple-element.62.refs_0_.refs_3_), channel_id=1, source_target_pairs={{4,8},{8,4},{12,16},{16,12},{20,24},{24,20},{5,9},{9,5},{13,17},{1... | collective-permute-start | bytes 393224 | tf_op jit(solution)/shard_map/ppermute | solution.py:331
  24.5 5.6 %collective-permute-start.8 = (bf16[2,256,128]{2,1,0:T(8,128)(2,1)S(1)}, bf16[2,256,128]{2,1,0:T(8,128)(2,1)S(1)}, u32[]{:S(2)}, u32[]{:S(2)}) collective-permute-start(bf16[2,256,128]{2,1,0:T(8,128)(2,1)S(1)} %get-tuple-element.73.refs_4_), channel_id=1, source_target_pairs={{0,4},{4,0},{8,12},{12,8},{16,20},{20,16},{24,28},{28,24},{1,5},{5... | collective-permute-start | bytes 393224 | tf_op jit(solution)/shard_map/ppermute | solution.py:332
  27.3 4.5 %collective-permute-start.12 = (bf16[2,128,128]{2,1,0:T(8,128)(2,1)S(1)}, bf16[2,128,128]{2,1,0:T(8,128)(2,1)S(1)}, u32[]{:S(2)}, u32[]{:S(2)}) collective-permute-start(bf16[2,128,128]{2,1,0:T(8,128)(2,1)S(1)} %get-tuple-element.78), channel_id=1, source_target_pairs={{0,1},{1,0},{2,3},{3,2},{4,5},{5,4},{6,7},{7,6},{8,9},{9,8},{10,11... | collective-permute-start | bytes 196616 | tf_op jit(solution)/shard_map/ppermute | solution.py:328
  27.3 6.4 %collective-permute-start.13 = (bf16[2,128,128]{2,1,0:T(8,128)(2,1)S(1)}, bf16[2,128,128]{2,1,0:T(8,128)(2,1)S(1)}, u32[]{:S(2)}, u32[]{:S(2)}) collective-permute-start(bf16[2,128,128]{2,1,0:T(8,128)(2,1)S(1)} %get-tuple-element.79), channel_id=1, source_target_pairs={{0,2},{1,3},{2,0},{3,1},{4,6},{5,7},{6,4},{7,5},{8,10},{9,11},{10,... | collective-permute-start | bytes 196616 | tf_op jit(solution)/shard_map/ppermute | solution.py:328
  28.9 4.9 %collective-permute-start.14 = (bf16[2,128,128]{2,1,0:T(8,128)(2,1)S(1)}, bf16[2,128,128]{2,1,0:T(8,128)(2,1)S(1)}, u32[]{:S(2)}, u32[]{:S(2)}) collective-permute-start(bf16[2,128,128]{2,1,0:T(8,128)(2,1)S(1)} %get-tuple-element.80), channel_id=1, source_target_pairs={{0,3},{1,2},{2,1},{3,0},{4,7},{5,6},{6,5},{7,4},{8,11},{9,10},{10,... | collective-permute-start | bytes 196616 | tf_op jit(solution)/shard_map/ppermute | solution.py:328
  30.2 4.4 %collective-permute-start.10 = (bf16[2,128,128]{2,1,0:T(8,128)(2,1)S(1)}, bf16[2,128,128]{2,1,0:T(8,128)(2,1)S(1)}, u32[]{:S(2)}, u32[]{:S(2)}) collective-permute-start(bf16[2,128,128]{2,1,0:T(8,128)(2,1)S(1)} %get-tuple-element.76), channel_id=1, source_target_pairs={{0,2},{1,3},{2,0},{3,1},{4,6},{5,7},{6,4},{7,5},{8,10},{9,11},{10,... | collective-permute-start | bytes 196616 | tf_op jit(solution)/shard_map/ppermute | solution.py:328
  31.7 4.3 %collective-permute-start.11 = (bf16[2,128,128]{2,1,0:T(8,128)(2,1)S(1)}, bf16[2,128,128]{2,1,0:T(8,128)(2,1)S(1)}, u32[]{:S(2)}, u32[]{:S(2)}) collective-permute-start(bf16[2,128,128]{2,1,0:T(8,128)(2,1)S(1)} %get-tuple-element.77), channel_id=1, source_target_pairs={{0,3},{1,2},{2,1},{3,0},{4,7},{5,6},{6,5},{7,4},{8,11},{9,10},{10,... | collective-permute-start | bytes 196616 | tf_op jit(solution)/shard_map/ppermute | solution.py:328
  31.7 4.3 %collective-permute-start.9 = (bf16[2,128,128]{2,1,0:T(8,128)(2,1)S(1)}, bf16[2,128,128]{2,1,0:T(8,128)(2,1)S(1)}, u32[]{:S(2)}, u32[]{:S(2)}) collective-permute-start(bf16[2,128,128]{2,1,0:T(8,128)(2,1)S(1)} %get-tuple-element.75), channel_id=1, source_target_pairs={{0,1},{1,0},{2,3},{3,2},{4,5},{5,4},{6,7},{7,6},{8,9},{9,8},{10,11... | collective-permute-start | bytes 196616 | tf_op jit(solution)/shard_map/ppermute | solution.py:328

commit v2 on v1

--- a/solution.py
+++ b/solution.py
@@ -142,7 +142,7 @@
 
 
 def products(task):
-    n, first, queries, grads, keys, d_queries = task
+    n, first, queries, grads, keys, put = task
     count = queries.shape[1] // HD
     window = pl.ds(first * BLK, n * BLK)
     k, v = keys[0, window, :], keys[1, window, :]
@@ -177,14 +177,22 @@
     return p.astype(BF16), (p * (dp - delta)).astype(BF16)
 
 
+def turn_back(k, ds):
+    return (dot(k.T, ds, 1, 0) * SCALE).astype(BF16)
+
+
+def put_queries(d_queries, k, ds):
+    dq = turn_back(k, ds)
+    for j in range(dq.shape[1] // BLK):
+        d_queries[:, j * HD : (j + 1) * HD] = dq[:, j * BLK : (j + 1) * BLK].T
+
+
 def gather(task, d_keys, k, q, do, p, ds):
-    n, first, queries, grads, keys, d_queries = task
+    n, first, queries, grads, keys, put = task
     window = pl.ds(first * BLK, n * BLK)
     d_keys[0, window, :] += dot(ds, q, 1, 0) * SCALE
     d_keys[1, window, :] += dot(p, do, 1, 0)
-    dq = (dot(k.T, ds, 1, 0) * SCALE).astype(BF16)
-    for j in range(dq.shape[1] // BLK):
-        d_queries[:, j * HD : (j + 1) * HD] = dq[:, j * BLK : (j + 1) * BLK].T
+    put(k, ds)
 
 
 def pair_grads(a, b, d_keys):
@@ -196,7 +204,7 @@
     gather(b, d_keys, *wb)
 
 
-def loose_grads(reach, visible, query, d_out, keys, d_query, d_keys):
+def loose_grads(reach, visible, query, d_out, keys, put_loose, d_keys):
     group = 4
     steps = query.shape[1] // (group * HD)
     seen_rows = (reach + 1) * BLK
@@ -217,16 +225,13 @@
         p, ds = weigh_all(s + jnp.concatenate([hide] * group, axis=1), dp)
         d_keys[0, window, :] += dot(ds, q, 1, 0) * SCALE
         d_keys[1, window, :] += dot(p, do, 1, 0)
-        dq = (dot(k.T, ds, 1, 0) * SCALE).astype(BF16)
-        for j, c in enumerate(columns):
-            d_query[rows(b), c] = dq[:, j * BLK : (j + 1) * BLK].T
+        put_loose(b, columns, k, ds)
         return carried
 
     lax.fori_loop(0, 2 * steps, step, 0)
 
 
-def span_part(fast, reach, first_block, per_span, half, doc_start, query, d_out, keys, d_query, d_keys):
-    d_keys[...] = jnp.zeros_like(d_keys)
+def visible_counts(per_span, half, first_block, doc_start):
     spot = lax.broadcasted_iota(jnp.int32, doc_start.shape, 1)
     marks = doc_start[...].astype(F32)
     visible = []
@@ -234,6 +239,12 @@
         block = span_of(half) * per_span + first_block + b
         mark = jnp.sum(jnp.where(spot == block, 2 * marks, jnp.where(spot == block - 1, marks, 0.0)))
         visible.append(jnp.where(mark > 1.5, 1, jnp.where(mark > 0.5, 2, 3)))
+    return visible
+
+
+def span_part(fast, reach, first_block, per_span, half, doc_start, query, d_out, keys, put, put_loose, d_keys):
+    d_keys[...] = jnp.zeros_like(d_keys)
+    visible = visible_counts(per_span, half, first_block, doc_start)
 
     def task(b, n):
         return (
@@ -242,7 +253,7 @@
             query.at[pl.ds(b * BLK, BLK), :],
             d_out.at[pl.ds(b * BLK, BLK), :],
             keys,
-            d_query.at[pl.ds(b * BLK, BLK), :],
+            put(b),
         )
 
     common = [(n, then) for n in range(1, REACH + 2) for then in (1, n + 1) if then <= REACH + 1]
@@ -258,32 +269,71 @@
 
     @pl.when(jnp.logical_not(chosen))
     def _():
-        loose_grads(reach, visible, query, d_out, keys, d_query, d_keys)
+        loose_grads(reach, visible, query, d_out, keys, put_loose, d_keys)
 
 
 def late_blocks(per_span, half, what, doc_start, query, d_out, keys, *refs):
     def body(doc_start, query, d_out, keys, d_query, d_keys):
-        span_part(LATE, REACH, REACH, per_span, half, doc_start, query, d_out, keys, d_query, d_keys)
+        def put(b):
+            return functools.partial(put_queries, d_query.at[pl.ds(b * BLK, BLK), :])
+
+        def put_loose(b, columns, k, ds):
+            dq = turn_back(k, ds)
+            for j, c in enumerate(columns):
+                d_query[rows(b), c] = dq[:, j * BLK : (j + 1) * BLK].T
+
+        span_part(LATE, REACH, REACH, per_span, half, doc_start, query, d_out, keys, put, put_loose, d_keys)
 
     while_fetching(what, body, (doc_start, query, d_out, keys), refs)
 
 
+def fill_window(per_span, half, window, keys, other, incoming):
+    cut = REACH * BLK
+    window[:, cut:, :] = keys[:, :cut, :]
+    window[:, :cut, :] = incoming[...]
+    if half == 1:
+
+        @pl.when(is_last())
+        def _():
+            window[:, :cut, :] = other[:, (per_span - REACH) * BLK :, :]
+
+
 def early_blocks(per_span, half, what, doc_start, query, d_out, keys, other, incoming, *refs):
-    def body(doc_start, query, d_out, keys, other, incoming, d_query, d_own, d_rim, window, d_window):
+    def body(doc_start, query, d_out, keys, other, incoming, dscores, d_own, d_rim, window, d_window):
+        def put(b):
+            def store(k, ds):
+                dscores[b, : ds.shape[0], :] = ds
+
+            return store
+
+        def put_loose(b, columns, k, ds):
+            for j, c in enumerate(columns):
+                dscores[b, : ds.shape[0], c] = ds[:, j * BLK : (j + 1) * BLK]
+
         cut = REACH * BLK
-        window[:, cut:, :] = keys[:, :cut, :]
-        window[:, :cut, :] = incoming[...]
-        if half == 1:
-
-            @pl.when(is_last())
-            def _():
-                window[:, :cut, :] = other[:, (per_span - REACH) * BLK :, :]
-
-        span_part(EARLY, REACH - 1, 0, per_span, half, doc_start, query, d_out, window, d_query, d_window)
+        fill_window(per_span, half, window, keys, other, incoming)
+        span_part(EARLY, REACH - 1, 0, per_span, half, doc_start, query, d_out, window, put, put_loose, d_window)
         d_rim[...] = d_window[:, :cut, :].astype(BF16)
         d_own[...] = d_window[:, cut:, :]
 
     while_fetching(what, body, (doc_start, query, d_out, keys, other, incoming), refs)
+
+
+def early_queries(per_span, half, doc_start, keys, other, incoming, dscores, d_query, window):
+    visible = visible_counts(per_span, half, 0, doc_start)
+    fill_window(per_span, half, window, keys, other, incoming)
+
+    def put(counts):
+        for b, n in enumerate(counts):
+            k = window[0, (b + REACH + 1 - n) * BLK : (b + REACH + 1) * BLK, :]
+            put_queries(d_query.at[pl.ds(b * BLK, BLK), :], k, dscores[b, : n * BLK, :])
+
+    chosen = False
+    for case in EARLY:
+        here = (visible[0] == case[0]) & (visible[1] == case[1])
+        chosen = here | chosen
+        pl.when(here)(functools.partial(put, case))
+    pl.when(jnp.logical_not(chosen))(functools.partial(put, (REACH, REACH)))
 
 
 def store_queries(reach, early_first, late_first, early_second, late_second, d_query, sems):
@@ -392,7 +442,8 @@
         return grads(late_blocks, half, spans, (), outs, then, after)
 
     def early(half, spans, incoming, then, after):
-        outs = [two_blocks, shape((2, REACH * BLK, HD), F32), shape((2, REACH * BLK, HD))]
+        dscores = shape((2, (REACH + 1) * BLK, query.shape[3]))
+        outs = [dscores, shape((2, REACH * BLK, HD), F32), shape((2, REACH * BLK, HD))]
         window = (2, 2 * REACH * BLK, HD)
         scratch = [pltpu.VMEM(window, BF16), pltpu.VMEM(window, F32)]
         return grads(early_blocks, half, spans, (keys[1 - half], incoming), outs, then, after, scratch)
@@ -401,10 +452,23 @@
     keys[1], rim = join(1, (late_first,))
     rim_first = to_inner(rim)
     dq_late_second, late_second, *spans = late(1, spans, (1, 0), (late_first,))
-    dq_early_second, own_second, edge_second, *spans = early(1, spans, rim_second, (0, 0), (late_second,))
+    ds_second, own_second, edge_second, *spans = early(1, spans, rim_second, (0, 0), (late_second,))
     back_first = to_outer(edge_second)
-    dq_early_first, own_first, edge_first = early(0, spans, rim_first, None, (edge_second,))
+    ds_first, own_first, edge_first = early(0, spans, rim_first, None, (edge_second,))
     back_second = to_inner(edge_first)
+
+    def queries_of(half, incoming, dscores, after):
+        return call(
+            functools.partial(early_queries, heads, half),
+            (starts, keys[half], keys[1 - half], incoming, dscores),
+            [two_blocks],
+            scratch=[pltpu.VMEM((2, 2 * REACH * BLK, HD), BF16)],
+            limit=20,
+            after=after,
+        )[0]
+
+    dq_early_second = queries_of(1, rim_second, ds_second, (edge_first,))
+    dq_early_first = queries_of(0, rim_first, ds_first, (dq_early_second,))
     d_query = call(
         functools.partial(store_queries, REACH),
         (dq_early_first, dq_late_first, dq_early_second, dq_late_second),

time: 37.7 us -> 36.8 us (0.976); the launches traced: 37 us -> 36.8 us
  Pallas kernels: 18 us -> 16.4 us
  starting transfers between devices: 14.7 us -> 16.2 us
    pallas_call x13 -> x15, Pallas kernels: 18 us -> 16.4 us  [call(): pl.pallas_call(lambda *refs: body(*refs[skip:]), out_shape=outs, in_specs...]
    ppermute x2, starting transfers between devices: 4.28 us -> 5.71 us  [per_device(): to_inner = lambda x: lax.ppermute(x, 'ctx', inner)]
  transfers between devices with their start and end apart: 15 -> 15, of which waited for: 4 -> 4; matrix products, arithmetic and copies ran while one was open for 0% -> 0% of each run, Pallas kernels for 44% -> 40%
where the time goes in v2:
time: 36.8 us
  Pallas kernels  16.4 us (45%)
  starting transfers between devices  16.2 us (44%)
  waiting for transfers between devices  3.22 us (9%)
  between operations  0.99 us (3%)
    pallas_call x15, Pallas kernels, call(): pl.pallas_call(lambda *refs: body(*refs[skip:]), out_shape=outs, in_specs...  16.4 us
    ppermute x11, starting transfers between devices, per_device(): lax.ppermute(x, 'head', [(i, i ^ t) for i in range(heads)])  9.13 us
    ppermute x2, starting transfers between devices, per_device(): to_inner = lambda x: lax.ppermute(x, 'ctx', inner)  5.71 us
    ppermute x11, waiting for transfers between devices, per_device(): lax.ppermute(x, 'head', [(i, i ^ t) for i in range(heads)])  2.22 us
    ppermute x2, starting transfers between devices, per_device(): to_outer = lambda x: lax.ppermute(x, 'ctx', outer)  1.34 us
    ppermute x2, waiting for transfers between devices, per_device(): to_inner = lambda x: lax.ppermute(x, 'ctx', inner)  1 us
  transfers between devices with their start and end apart: 15, of which 4 were waited for; matrix products, arithmetic and copies ran while one was open for 0% of the time, Pallas kernels for 40%

profile of v2, /device:TPU:0, one launch (start us, length us, event | category | flops | bytes accessed | tf_op | source)
XLA Modules:
  0.0 36.8 jit_solution(10742441664288491377)
XLA Ops:
  0.6 1.1 %pack_keys.1 = (bf16[2,2,128,128]{3,2,1,0:T(8,128)(2,1)S(1)}, bf16[2,2,128,128]{3,2,1,0:T(8,128)(2,1)S(1)}, bf16[2,128,128]{2,1,0:T(8,128)(2,1)S(1)}, bf16[2,128,128]{2,1,0:T(8,128)(2,1)S(1)}) custom-call(bf16[1,2,128,512]{3,2,1,0:T(8,128)(2,1)} %refs_2_.1, bf16[1,2,128,512]{3,2,1,0:T(8,128)(2,1)} %refs_3_.1), custom_call_target="tpu_custom_call" | custom-call | tf_op jit(solution)/shard_map/pack_keys/pallas_call | solution.py:34
  1.7 0.5 %collective-permute-start = (bf16[2,2,128,128]{3,2,1,0:T(8,128)(2,1)S(1)}, bf16[2,2,128,128]{3,2,1,0:T(8,128)(2,1)S(1)}, u32[]{:S(2)}, u32[]{:S(2)}) collective-permute-start(bf16[2,2,128,128]{3,2,1,0:T(8,128)(2,1)S(1)} %get-tuple-element.48), channel_id=1, source_target_pairs={{0,1},{1,0},{2,3},{3,2},{4,5},{5,4},{6,7},{7,6},{8,9},{9,8},{10,11... | collective-permute-start | bytes 393224 | tf_op jit(solution)/shard_map/ppermute | solution.py:378
  2.2 2.6 %collective-permute-start.1 = (bf16[2,128,128]{2,1,0:T(8,128)(2,1)S(1)}, bf16[2,128,128]{2,1,0:T(8,128)(2,1)S(1)}, u32[]{:S(2)}, u32[]{:S(2)}) collective-permute-start(bf16[2,128,128]{2,1,0:T(8,128)(2,1)S(1)} %get-tuple-element.49), channel_id=1, source_target_pairs={{0,2},{1,3},{2,0},{3,1},{4,6},{5,7},{6,4},{7,5},{8,10},{9,11},{10,... | collective-permute-start | bytes 196616 | tf_op jit(solution)/shard_map/ppermute | solution.py:378
  4.8 0.1 collective-permute-start.2
  4.9 1.3 %load_queries.1 = (s32[1,64]{1,0:T(1,128)S(1)}, bf16[256,1024]{1,0:T(8,128)(2,1)S(1)}, bf16[256,1024]{1,0:T(8,128)(2,1)S(1)}, bf16[2,128,128]{2,1,0:T(8,128)(2,1)S(1)}, bf16[2,128,128]{2,1,0:T(8,128)(2,1)S(1)}) custom-call(bf16[2,2,128,128]{3,2,1,0:T(8,128)(2,1)S(1)} %get-tuple-element.44.refs_0_.refs_1_, s32[1,64]{1,0:T(1,128)} %bitcast.1, ...), custom_call_target="tpu_custom_call" | custom-call | bytes 4194304 | tf_op jit(solution)/shard_map/load_queries/pallas_call | solution.py:34
  6.1 1.8 %collective-permute-start.3 = (bf16[2,128,128]{2,1,0:T(8,128)(2,1)S(1)}, bf16[2,128,128]{2,1,0:T(8,128)(2,1)S(1)}, u32[]{:S(2)}, u32[]{:S(2)}) collective-permute-start(bf16[2,128,128]{2,1,0:T(8,128)(2,1)S(1)} %get-tuple-element.55), channel_id=1, source_target_pairs={{0,2},{1,3},{2,0},{3,1},{4,6},{5,7},{6,4},{7,5},{8,10},{9,11},{10,... | collective-permute-start | bytes 196616 | tf_op jit(solution)/shard_map/ppermute | solution.py:378
  7.9 0.0 collective-permute-start.4
  8.0 0.0 collective-permute-done.1.refs_3_
  8.0 0.9 %collective-permute-done.2.refs_4_ = bf16[2,128,128]{2,1,0:T(8,128)(2,1)S(1)} collective-permute-done((bf16[2,128,128]{2,1,0:T(8,128)(2,1)S(1)}, bf16[2,128,128]{2,1,0:T(8,128)(2,1)S(1)}, u32[]{:S(2)}, u32[]{:S(2)}) %collective-permute-start.2) | collective-permute-done | bytes 65568 | tf_op jit(solution)/shard_map/ppermute | solution.py:378
  8.8 0.0 collective-permute-done.refs_2_
  8.9 0.7 %collective-permute-start.5 = (bf16[2,256,128]{2,1,0:T(8,128)(2,1)S(1)}, bf16[2,256,128]{2,1,0:T(8,128)(2,1)S(1)}, u32[]{:S(2)}, u32[]{:S(2)}) collective-permute-start(bf16[2,256,128]{2,1,0:T(8,128)(2,1)S(1)} %get-tuple-element.61), channel_id=1, source_target_pairs={{4,8},{8,4},{12,16},{16,12},{20,24},{24,20},{5,9},{9,5},{13,17},{1... | collective-permute-start | bytes 393224 | tf_op jit(solution)/shard_map/ppermute | solution.py:381
  9.6 1.4 %late_blocks.2 = (bf16[256,1024]{1,0:T(8,128)(2,1)S(1)}, f32[2,512,128]{2,1,0:T(8,128)S(1)}, bf16[256,1024]{1,0:T(8,128)(2,1)S(1)}, bf16[256,1024]{1,0:T(8,128)(2,1)S(1)}) custom-call(s32[1,64]{1,0:T(1,128)S(1)} %get-tuple-element.45.refs_0_.refs_1_, bf16[256,1024]{1,0:T(8,128)(2,1)S(1)} %get-tuple-element.46.refs_0_.refs_1_, ...), custom_call_target="tpu_custom_call" | custom-call | tf_op jit(solution)/shard_map/late_blocks/pallas_call | solution.py:34
  10.9 0.0 collective-permute-done.3.refs_3_
  10.9 1.1 %collective-permute-done.4.refs_4_ = bf16[2,128,128]{2,1,0:T(8,128)(2,1)S(1)} collective-permute-done((bf16[2,128,128]{2,1,0:T(8,128)(2,1)S(1)}, bf16[2,128,128]{2,1,0:T(8,128)(2,1)S(1)}, u32[]{:S(2)}, u32[]{:S(2)}) %collective-permute-start.4) | collective-permute-done | bytes 65568 | tf_op jit(solution)/shard_map/ppermute | solution.py:378
  12.1 3.7 %collective-permute-start.6 = (bf16[2,256,128]{2,1,0:T(8,128)(2,1)S(1)}, bf16[2,256,128]{2,1,0:T(8,128)(2,1)S(1)}, u32[]{:S(2)}, u32[]{:S(2)}) collective-permute-start(bf16[2,256,128]{2,1,0:T(8,128)(2,1)S(1)} %get-tuple-element.65), channel_id=1, source_target_pairs={{0,4},{4,0},{8,12},{12,8},{16,20},{20,16},{24,28},{28,24},{1,5},{5... | collective-permute-start | bytes 393224 | tf_op jit(solution)/shard_map/ppermute | solution.py:382
  15.8 2.5 %late_blocks.3 = (bf16[256,1024]{1,0:T(8,128)(2,1)S(1)}, f32[2,512,128]{2,1,0:T(8,128)S(1)}, bf16[256,1024]{1,0:T(8,128)(2,1)S(1)}, bf16[256,1024]{1,0:T(8,128)(2,1)S(1)}) custom-call(f32[2,512,128]{2,1,0:T(8,128)S(1)} %get-tuple-element.52.refs_0_, s32[1,64]{1,0:T(1,128)S(1)} %get-tuple-element.45.refs_0_.refs_1_, ...), custom_call_target="tpu_custom_call" | custom-call | tf_op jit(solution)/shard_map/late_blocks/pallas_call | solution.py:34
  18.3 0.0 collective-permute-done.5.refs_6_.refs_4_
  18.3 3.3 %early_blocks.2 = (bf16[2,384,1024]{2,1,0:T(8,128)(2,1)S(1)}, f32[2,256,128]{2,1,0:T(8,128)S(1)}, bf16[2,256,128]{2,1,0:T(8,128)(2,1)S(1)}, bf16[256,1024]{1,0:T(8,128)(2,1)S(1)}, bf16[256,1024]{1,0:T(8,128)(2,1)S(1)}) custom-call(f32[2,512,128]{2,1,0:T(8,128)S(1)} %get-tuple-element.58.refs_0_.refs_1_, s32[1,64]{1,0:T(1,128)S(1)} %get-tuple-element.45.refs_0_.refs_1_, ...), custom_call_target="tpu_custom_call" | custom-call | tf_op jit(solution)/shard_map/early_blocks/pallas_call | solution.py:34
  21.6 0.7 %collective-permute-start.7 = (bf16[2,256,128]{2,1,0:T(8,128)(2,1)S(1)}, bf16[2,256,128]{2,1,0:T(8,128)(2,1)S(1)}, u32[]{:S(2)}, u32[]{:S(2)}) collective-permute-start(bf16[2,256,128]{2,1,0:T(8,128)(2,1)S(1)} %get-tuple-element.62.refs_0_.refs_3_), channel_id=1, source_target_pairs={{4,8},{8,4},{12,16},{16,12},{20,24},{24,20},{5,9},{9,5},{13,17},{1... | collective-permute-start | bytes 393224 | tf_op jit(solution)/shard_map/ppermute | solution.py:381
  22.3 0.0 collective-permute-done.6.refs_6_.refs_4_
  22.3 2.5 %early_blocks.3 = (bf16[2,384,1024]{2,1,0:T(8,128)(2,1)S(1)}, f32[2,256,128]{2,1,0:T(8,128)S(1)}, bf16[2,256,128]{2,1,0:T(8,128)(2,1)S(1)}) custom-call(bf16[2,256,128]{2,1,0:T(8,128)(2,1)S(1)} %get-tuple-element.62.refs_0_.refs_3_, s32[1,64]{1,0:T(1,128)S(1)} %get-tuple-element.45.refs_0_.refs_1_, bf16[256,1024]{1,0:T(8,128)(2,1)S(1)} %get-tuple-element.63.refs_2_, ...), custom_call_target="tpu_custom_call" | custom-call | tf_op jit(solution)/shard_map/early_blocks/pallas_call | solution.py:34
  24.9 2.1 %collective-permute-start.8 = (bf16[2,256,128]{2,1,0:T(8,128)(2,1)S(1)}, bf16[2,256,128]{2,1,0:T(8,128)(2,1)S(1)}, u32[]{:S(2)}, u32[]{:S(2)}) collective-permute-start(bf16[2,256,128]{2,1,0:T(8,128)(2,1)S(1)} %get-tuple-element.66.refs_0_.refs_4_), channel_id=1, source_target_pairs={{0,4},{4,0},{8,12},{12,8},{16,20},{20,16},{24,28},{28,24},{1,5},{5... | collective-permute-start | bytes 393224 | tf_op jit(solution)/shard_map/ppermute | solution.py:382
  26.9 0.0 collective-permute-done.7.refs_2_
  26.9 0.1 pack_grads.2
  27.0 0.1 collective-permute-start.12
  27.1 1.5 %collective-permute-start.13 = (bf16[2,128,128]{2,1,0:T(8,128)(2,1)S(1)}, bf16[2,128,128]{2,1,0:T(8,128)(2,1)S(1)}, u32[]{:S(2)}, u32[]{:S(2)}) collective-permute-start(bf16[2,128,128]{2,1,0:T(8,128)(2,1)S(1)} %get-tuple-element.79), channel_id=1, source_target_pairs={{0,2},{1,3},{2,0},{3,1},{4,6},{5,7},{6,4},{7,5},{8,10},{9,11},{10,... | collective-permute-start | bytes 196616 | tf_op jit(solution)/shard_map/ppermute | solution.py:378
  28.6 0.4 collective-permute-start.14
  29.0 1.0 %collective-permute-done.8.refs_3_ = bf16[2,256,128]{2,1,0:T(8,128)(2,1)S(1)} collective-permute-done((bf16[2,256,128]{2,1,0:T(8,128)(2,1)S(1)}, bf16[2,256,128]{2,1,0:T(8,128)(2,1)S(1)}, u32[]{:S(2)}, u32[]{:S(2)}) %collective-permute-start.8) | collective-permute-done | bytes 131104 | tf_op jit(solution)/shard_map/ppermute | solution.py:382
  30.0 0.1 pack_grads.3
  30.0 1.5 %collective-permute-start.10 = (bf16[2,128,128]{2,1,0:T(8,128)(2,1)S(1)}, bf16[2,128,128]{2,1,0:T(8,128)(2,1)S(1)}, u32[]{:S(2)}, u32[]{:S(2)}) collective-permute-start(bf16[2,128,128]{2,1,0:T(8,128)(2,1)S(1)} %get-tuple-element.76), channel_id=1, source_target_pairs={{0,2},{1,3},{2,0},{3,1},{4,6},{5,7},{6,4},{7,5},{8,10},{9,11},{10,... | collective-permute-start | bytes 196616 | tf_op jit(solution)/shard_map/ppermute | solution.py:378
  31.6 0.0 collective-permute-start.11
  31.6 0.0 collective-permute-done.12.refs_1_
  31.6 0.7 %collective-permute-start.9 = (bf16[2,128,128]{2,1,0:T(8,128)(2,1)S(1)}, bf16[2,128,128]{2,1,0:T(8,128)(2,1)S(1)}, u32[]{:S(2)}, u32[]{:S(2)}) collective-permute-start(bf16[2,128,128]{2,1,0:T(8,128)(2,1)S(1)} %get-tuple-element.75), channel_id=1, source_target_pairs={{0,1},{1,0},{2,3},{3,2},{4,5},{5,4},{6,7},{7,6},{8,9},{9,8},{10,11... | collective-permute-start | bytes 196616 | tf_op jit(solution)/shard_map/ppermute | solution.py:378
  32.2 0.5 %early_queries.2.refs_0_.refs_2_ = bf16[256,1024]{1,0:T(8,128)(2,1)S(1)} custom-call(bf16[2,256,128]{2,1,0:T(8,128)(2,1)S(1)} %get-tuple-element.66.refs_0_.refs_4_, s32[1,64]{1,0:T(1,128)S(1)} %get-tuple-element.45.refs_0_.refs_1_, bf16[2,512,128]{2,1,0:T(8,128)(2,1)S(1)} %get-tuple-element.57.refs_4_.refs_5_.refs_2_.refs_3_, ...), custom_call_target="tpu_custom_call" | custom-call | tf_op jit(solution)/shard_map/early_queries/pallas_call | solution.py:34
  32.8 0.6 %early_queries.3.refs_0_ = bf16[256,1024]{1,0:T(8,128)(2,1)S(1)} custom-call(bf16[256,1024]{1,0:T(8,128)(2,1)S(1)} %early_queries.2.refs_0_.refs_2_, s32[1,64]{1,0:T(1,128)S(1)} %get-tuple-element.45.refs_0_.refs_1_, bf16[2,512,128]{2,1,0:T(8,128)(2,1)S(1)} %get-tuple-element.51.refs_3_.refs_5_.refs_4_.refs_2_, ...), custom_call_target="tpu_custom_call" | custom-call | tf_op jit(solution)/shard_map/early_queries/pallas_call | solution.py:34
  33.4 1.4 %store_queries.1 = bf16[1,2,512,1024]{3,2,1,0:T(8,128)(2,1)} custom-call(bf16[256,1024]{1,0:T(8,128)(2,1)S(1)} %early_queries.3.refs_0_, bf16[256,1024]{1,0:T(8,128)(2,1)S(1)} %get-tuple-element.69.refs_1_, bf16[256,1024]{1,0:T(8,128)(2,1)S(1)} %early_queries.2.refs_0_.refs_2_, bf16[256,1024]{1,0:T(8,128)(2,1)S(1)} %get-tuple-element.70.refs_3_), custom_call_target="tpu_custom_call" | custom-call | tf_op jit(solution)/shard_map/store_queries/pallas_call | solution.py:34
  34.8 0.0 collective-permute-done.13.refs_2_
  34.8 0.0 collective-permute-done.14.refs_3_
  34.8 0.8 %join_grads.2 = (bf16[1,2,128,512]{3,2,1,0:T(8,128)(2,1)}, bf16[1,2,128,512]{3,2,1,0:T(8,128)(2,1)}) custom-call(bf16[2,128,128]{2,1,0:T(8,128)(2,1)S(1)} %get-tuple-element.72.refs_0_, bf16[2,128,128]{2,1,0:T(8,128)(2,1)S(1)} %collective-permute-done.12.refs_1_, bf16[2,128,128]{2,1,0:T(8,128)(2,1)S(1)} %collective-permute-done.13.refs_2_, ...), custom_call_target="tpu_custom_call" | custom-call | tf_op jit(solution)/shard_map/join_grads/pallas_call | solution.py:34
  35.6 0.0 collective-permute-done.10.refs_2_
  35.6 0.2 collective-permute-done.11.refs_3_
  35.8 0.0 collective-permute-done.9.refs_1_
  35.8 0.8 %join_grads.3 = (bf16[1,2,128,512]{3,2,1,0:T(8,128)(2,1)}, bf16[1,2,128,512]{3,2,1,0:T(8,128)(2,1)}) custom-call(bf16[2,128,128]{2,1,0:T(8,128)(2,1)S(1)} %get-tuple-element.74.refs_0_, bf16[2,128,128]{2,1,0:T(8,128)(2,1)S(1)} %collective-permute-done.9.refs_1_, ...), custom_call_target="tpu_custom_call", output_to_operand_aliasing={{0}: (4, {}), {1}: (5, {})} | custom-call | tf_op jit(solution)/shard_map/join_grads/pallas_call | solution.py:34
  (2 shorter events, 0.1 us)
Async XLA Ops:
  1.7 7.1 %collective-permute-start = (bf16[2,2,128,128]{3,2,1,0:T(8,128)(2,1)S(1)}, bf16[2,2,128,128]{3,2,1,0:T(8,128)(2,1)S(1)}, u32[]{:S(2)}, u32[]{:S(2)}) collective-permute-start(bf16[2,2,128,128]{3,2,1,0:T(8,128)(2,1)S(1)} %get-tuple-element.48), channel_id=1, source_target_pairs={{0,1},{1,0},{2,3},{3,2},{4,5},{5,4},{6,7},{7,6},{8,9},{9,8},{10,11... | collective-permute-start | bytes 393224 | tf_op jit(solution)/shard_map/ppermute | solution.py:378
  2.2 5.7 %collective-permute-start.1 = (bf16[2,128,128]{2,1,0:T(8,128)(2,1)S(1)}, bf16[2,128,128]{2,1,0:T(8,128)(2,1)S(1)}, u32[]{:S(2)}, u32[]{:S(2)}) collective-permute-start(bf16[2,128,128]{2,1,0:T(8,128)(2,1)S(1)} %get-tuple-element.49), channel_id=1, source_target_pairs={{0,2},{1,3},{2,0},{3,1},{4,6},{5,7},{6,4},{7,5},{8,10},{9,11},{10,... | collective-permute-start | bytes 196616 | tf_op jit(solution)/shard_map/ppermute | solution.py:378
  4.8 4.0 %collective-permute-start.2 = (bf16[2,128,128]{2,1,0:T(8,128)(2,1)S(1)}, bf16[2,128,128]{2,1,0:T(8,128)(2,1)S(1)}, u32[]{:S(2)}, u32[]{:S(2)}) collective-permute-start(bf16[2,128,128]{2,1,0:T(8,128)(2,1)S(1)} %get-tuple-element.50), channel_id=1, source_target_pairs={{0,3},{1,2},{2,1},{3,0},{4,7},{5,6},{6,5},{7,4},{8,11},{9,10},{10,... | collective-permute-start | bytes 196616 | tf_op jit(solution)/shard_map/ppermute | solution.py:378
  6.1 4.8 %collective-permute-start.3 = (bf16[2,128,128]{2,1,0:T(8,128)(2,1)S(1)}, bf16[2,128,128]{2,1,0:T(8,128)(2,1)S(1)}, u32[]{:S(2)}, u32[]{:S(2)}) collective-permute-start(bf16[2,128,128]{2,1,0:T(8,128)(2,1)S(1)} %get-tuple-element.55), channel_id=1, source_target_pairs={{0,2},{1,3},{2,0},{3,1},{4,6},{5,7},{6,4},{7,5},{8,10},{9,11},{10,... | collective-permute-start | bytes 196616 | tf_op jit(solution)/shard_map/ppermute | solution.py:378
  7.9 4.1 %collective-permute-start.4 = (bf16[2,128,128]{2,1,0:T(8,128)(2,1)S(1)}, bf16[2,128,128]{2,1,0:T(8,128)(2,1)S(1)}, u32[]{:S(2)}, u32[]{:S(2)}) collective-permute-start(bf16[2,128,128]{2,1,0:T(8,128)(2,1)S(1)} %get-tuple-element.56), channel_id=1, source_target_pairs={{0,3},{1,2},{2,1},{3,0},{4,7},{5,6},{6,5},{7,4},{8,11},{9,10},{10,... | collective-permute-start | bytes 196616 | tf_op jit(solution)/shard_map/ppermute | solution.py:378
  8.9 9.4 %collective-permute-start.5 = (bf16[2,256,128]{2,1,0:T(8,128)(2,1)S(1)}, bf16[2,256,128]{2,1,0:T(8,128)(2,1)S(1)}, u32[]{:S(2)}, u32[]{:S(2)}) collective-permute-start(bf16[2,256,128]{2,1,0:T(8,128)(2,1)S(1)} %get-tuple-element.61), channel_id=1, source_target_pairs={{4,8},{8,4},{12,16},{16,12},{20,24},{24,20},{5,9},{9,5},{13,17},{1... | collective-permute-start | bytes 393224 | tf_op jit(solution)/shard_map/ppermute | solution.py:381
  12.1 10.2 %collective-permute-start.6 = (bf16[2,256,128]{2,1,0:T(8,128)(2,1)S(1)}, bf16[2,256,128]{2,1,0:T(8,128)(2,1)S(1)}, u32[]{:S(2)}, u32[]{:S(2)}) collective-permute-start(bf16[2,256,128]{2,1,0:T(8,128)(2,1)S(1)} %get-tuple-element.65), channel_id=1, source_target_pairs={{0,4},{4,0},{8,12},{12,8},{16,20},{20,16},{24,28},{28,24},{1,5},{5... | collective-permute-start | bytes 393224 | tf_op jit(solution)/shard_map/ppermute | solution.py:382
  21.6 5.3 %collective-permute-start.7 = (bf16[2,256,128]{2,1,0:T(8,128)(2,1)S(1)}, bf16[2,256,128]{2,1,0:T(8,128)(2,1)S(1)}, u32[]{:S(2)}, u32[]{:S(2)}) collective-permute-start(bf16[2,256,128]{2,1,0:T(8,128)(2,1)S(1)} %get-tuple-element.62.refs_0_.refs_3_), channel_id=1, source_target_pairs={{4,8},{8,4},{12,16},{16,12},{20,24},{24,20},{5,9},{9,5},{13,17},{1... | collective-permute-start | bytes 393224 | tf_op jit(solution)/shard_map/ppermute | solution.py:381
  24.9 5.1 %collective-permute-start.8 = (bf16[2,256,128]{2,1,0:T(8,128)(2,1)S(1)}, bf16[2,256,128]{2,1,0:T(8,128)(2,1)S(1)}, u32[]{:S(2)}, u32[]{:S(2)}) collective-permute-start(bf16[2,256,128]{2,1,0:T(8,128)(2,1)S(1)} %get-tuple-element.66.refs_0_.refs_4_), channel_id=1, source_target_pairs={{0,4},{4,0},{8,12},{12,8},{16,20},{20,16},{24,28},{28,24},{1,5},{5... | collective-permute-start | bytes 393224 | tf_op jit(solution)/shard_map/ppermute | solution.py:382
  27.0 4.6 %collective-permute-start.12 = (bf16[2,128,128]{2,1,0:T(8,128)(2,1)S(1)}, bf16[2,128,128]{2,1,0:T(8,128)(2,1)S(1)}, u32[]{:S(2)}, u32[]{:S(2)}) collective-permute-start(bf16[2,128,128]{2,1,0:T(8,128)(2,1)S(1)} %get-tuple-element.78), channel_id=1, source_target_pairs={{0,1},{1,0},{2,3},{3,2},{4,5},{5,4},{6,7},{7,6},{8,9},{9,8},{10,11... | collective-permute-start | bytes 196616 | tf_op jit(solution)/shard_map/ppermute | solution.py:378
  27.1 7.7 %collective-permute-start.13 = (bf16[2,128,128]{2,1,0:T(8,128)(2,1)S(1)}, bf16[2,128,128]{2,1,0:T(8,128)(2,1)S(1)}, u32[]{:S(2)}, u32[]{:S(2)}) collective-permute-start(bf16[2,128,128]{2,1,0:T(8,128)(2,1)S(1)} %get-tuple-element.79), channel_id=1, source_target_pairs={{0,2},{1,3},{2,0},{3,1},{4,6},{5,7},{6,4},{7,5},{8,10},{9,11},{10,... | collective-permute-start | bytes 196616 | tf_op jit(solution)/shard_map/ppermute | solution.py:378
  28.6 6.2 %collective-permute-start.14 = (bf16[2,128,128]{2,1,0:T(8,128)(2,1)S(1)}, bf16[2,128,128]{2,1,0:T(8,128)(2,1)S(1)}, u32[]{:S(2)}, u32[]{:S(2)}) collective-permute-start(bf16[2,128,128]{2,1,0:T(8,128)(2,1)S(1)} %get-tuple-element.80), channel_id=1, source_target_pairs={{0,3},{1,2},{2,1},{3,0},{4,7},{5,6},{6,5},{7,4},{8,11},{9,10},{10,... | collective-permute-start | bytes 196616 | tf_op jit(solution)/shard_map/ppermute | solution.py:378
  30.0 5.6 %collective-permute-start.10 = (bf16[2,128,128]{2,1,0:T(8,128)(2,1)S(1)}, bf16[2,128,128]{2,1,0:T(8,128)(2,1)S(1)}, u32[]{:S(2)}, u32[]{:S(2)}) collective-permute-start(bf16[2,128,128]{2,1,0:T(8,128)(2,1)S(1)} %get-tuple-element.76), channel_id=1, source_target_pairs={{0,2},{1,3},{2,0},{3,1},{4,6},{5,7},{6,4},{7,5},{8,10},{9,11},{10,... | collective-permute-start | bytes 196616 | tf_op jit(solution)/shard_map/ppermute | solution.py:378
  31.6 4.3 %collective-permute-start.11 = (bf16[2,128,128]{2,1,0:T(8,128)(2,1)S(1)}, bf16[2,128,128]{2,1,0:T(8,128)(2,1)S(1)}, u32[]{:S(2)}, u32[]{:S(2)}) collective-permute-start(bf16[2,128,128]{2,1,0:T(8,128)(2,1)S(1)} %get-tuple-element.77), channel_id=1, source_target_pairs={{0,3},{1,2},{2,1},{3,0},{4,7},{5,6},{6,5},{7,4},{8,11},{9,10},{10,... | collective-permute-start | bytes 196616 | tf_op jit(solution)/shard_map/ppermute | solution.py:378
  31.6 4.3 %collective-permute-start.9 = (bf16[2,128,128]{2,1,0:T(8,128)(2,1)S(1)}, bf16[2,128,128]{2,1,0:T(8,128)(2,1)S(1)}, u32[]{:S(2)}, u32[]{:S(2)}) collective-permute-start(bf16[2,128,128]{2,1,0:T(8,128)(2,1)S(1)} %get-tuple-element.75), channel_id=1, source_target_pairs={{0,1},{1,0},{2,3},{3,2},{4,5},{5,4},{6,7},{7,6},{8,9},{9,8},{10,11... | collective-permute-start | bytes 196616 | tf_op jit(solution)/shard_map/ppermute | solution.py:378

commit v3 on v2

--- a/solution.py
+++ b/solution.py
@@ -272,17 +272,32 @@
         loose_grads(reach, visible, query, d_out, keys, put_loose, d_keys)
 
 
+def keepers(dscores):
+    def put(b):
+        def store(k, ds):
+            dscores[b, : ds.shape[0], :] = ds
+
+        return store
+
+    def put_loose(b, columns, k, ds):
+        for j, c in enumerate(columns):
+            dscores[b, : ds.shape[0], c] = ds[:, j * BLK : (j + 1) * BLK]
+
+    return put, put_loose
+
+
 def late_blocks(per_span, half, what, doc_start, query, d_out, keys, *refs):
-    def body(doc_start, query, d_out, keys, d_query, d_keys):
+    def body(doc_start, query, d_out, keys, kept, d_keys):
         def put(b):
-            return functools.partial(put_queries, d_query.at[pl.ds(b * BLK, BLK), :])
+            return functools.partial(put_queries, kept.at[pl.ds(b * BLK, BLK), :])
 
         def put_loose(b, columns, k, ds):
             dq = turn_back(k, ds)
             for j, c in enumerate(columns):
-                d_query[rows(b), c] = dq[:, j * BLK : (j + 1) * BLK].T
-
-        span_part(LATE, REACH, REACH, per_span, half, doc_start, query, d_out, keys, put, put_loose, d_keys)
+                kept[rows(b), c] = dq[:, j * BLK : (j + 1) * BLK].T
+
+        writers = (put, put_loose) if half == 0 else keepers(kept)
+        span_part(LATE, REACH, REACH, per_span, half, doc_start, query, d_out, keys, *writers, d_keys)
 
     while_fetching(what, body, (doc_start, query, d_out, keys), refs)
 
@@ -300,48 +315,48 @@
 
 def early_blocks(per_span, half, what, doc_start, query, d_out, keys, other, incoming, *refs):
     def body(doc_start, query, d_out, keys, other, incoming, dscores, d_own, d_rim, window, d_window):
-        def put(b):
-            def store(k, ds):
-                dscores[b, : ds.shape[0], :] = ds
-
-            return store
-
-        def put_loose(b, columns, k, ds):
-            for j, c in enumerate(columns):
-                dscores[b, : ds.shape[0], c] = ds[:, j * BLK : (j + 1) * BLK]
-
         cut = REACH * BLK
         fill_window(per_span, half, window, keys, other, incoming)
-        span_part(EARLY, REACH - 1, 0, per_span, half, doc_start, query, d_out, window, put, put_loose, d_window)
+        span_part(EARLY, REACH - 1, 0, per_span, half, doc_start, query, d_out, window, *keepers(dscores), d_window)
         d_rim[...] = d_window[:, :cut, :].astype(BF16)
         d_own[...] = d_window[:, cut:, :]
 
     while_fetching(what, body, (doc_start, query, d_out, keys, other, incoming), refs)
 
 
-def early_queries(per_span, half, doc_start, keys, other, incoming, dscores, d_query, window):
-    visible = visible_counts(per_span, half, 0, doc_start)
-    fill_window(per_span, half, window, keys, other, incoming)
-
-    def put(counts):
-        for b, n in enumerate(counts):
-            k = window[0, (b + REACH + 1 - n) * BLK : (b + REACH + 1) * BLK, :]
-            put_queries(d_query.at[pl.ds(b * BLK, BLK), :], k, dscores[b, : n * BLK, :])
-
-    chosen = False
-    for case in EARLY:
-        here = (visible[0] == case[0]) & (visible[1] == case[1])
-        chosen = here | chosen
-        pl.when(here)(functools.partial(put, case))
-    pl.when(jnp.logical_not(chosen))(functools.partial(put, (REACH, REACH)))
-
-
-def store_queries(reach, early_first, late_first, early_second, late_second, d_query, sems):
-    pairs = []
-    for half, parts in ((0, (early_first, late_first)), (1, (early_second, late_second))):
-        for part, start in zip(parts, (0, reach * BLK)):
-            pairs.append((part, d_query.at[0, slot_of(half), pl.ds(start, part.shape[0]), :]))
-    carry(pairs, sems)
+def finish_queries(per_span, doc_start, late_first, keys_0, keys_1, rim_second, rim_first, *refs):
+    ds_late, ds_second, ds_first, d_query, part_late, part_second, part_first, window, sems = refs
+    copies = []
+
+    def send(part, half, first_block):
+        there = d_query.at[0, slot_of(half), pl.ds(first_block * BLK, REACH * BLK), :]
+        copies.append(pltpu.make_async_copy(part, there, sems.at[len(copies)]))
+        copies[-1].start()
+
+    def work_out(fast, reach, half, first_block, keys, dscores, part):
+        visible = visible_counts(per_span, half, first_block, doc_start)
+
+        def put(counts):
+            for b, n in enumerate(counts):
+                k = keys[0, (b + REACH + 1 - n) * BLK : (b + REACH + 1) * BLK, :]
+                put_queries(part.at[pl.ds(b * BLK, BLK), :], k, dscores[b, : n * BLK, :])
+
+        chosen = False
+        for case in fast:
+            here = (visible[0] == case[0]) & (visible[1] == case[1])
+            chosen = here | chosen
+            pl.when(here)(functools.partial(put, case))
+        pl.when(jnp.logical_not(chosen))(functools.partial(put, (reach + 1, reach + 1)))
+        send(part, half, first_block)
+
+    send(late_first, 0, REACH)
+    work_out(LATE, REACH, 1, REACH, keys_1, ds_late, part_late)
+    fill_window(per_span, 1, window, keys_1, keys_0, rim_second)
+    work_out(EARLY, REACH - 1, 1, 0, window, ds_second, part_second)
+    fill_window(per_span, 0, window, keys_0, keys_1, rim_first)
+    work_out(EARLY, REACH - 1, 0, 0, window, ds_first, part_first)
+    for copy in copies:
+        copy.wait()
 
 
 def pack_grads(heads, half, late, own, back, local, *refs):
@@ -437,12 +452,13 @@
             after=after,
         )
 
+    dscores = shape((2, (REACH + 1) * BLK, query.shape[3]))
+
     def late(half, spans, then, after):
-        outs = [two_blocks, shape((2, heads * BLK, HD), F32)]
+        outs = [two_blocks if half == 0 else dscores, shape((2, heads * BLK, HD), F32)]
         return grads(late_blocks, half, spans, (), outs, then, after)
 
     def early(half, spans, incoming, then, after):
-        dscores = shape((2, (REACH + 1) * BLK, query.shape[3]))
         outs = [dscores, shape((2, REACH * BLK, HD), F32), shape((2, REACH * BLK, HD))]
         window = (2, 2 * REACH * BLK, HD)
         scratch = [pltpu.VMEM(window, BF16), pltpu.VMEM(window, F32)]
@@ -451,30 +467,20 @@
     dq_late_first, late_first, *spans = late(0, spans, (1, REACH), ())
     keys[1], rim = join(1, (late_first,))
     rim_first = to_inner(rim)
-    dq_late_second, late_second, *spans = late(1, spans, (1, 0), (late_first,))
+    ds_late, late_second, *spans = late(1, spans, (1, 0), (late_first,))
     ds_second, own_second, edge_second, *spans = early(1, spans, rim_second, (0, 0), (late_second,))
     back_first = to_outer(edge_second)
     ds_first, own_first, edge_first = early(0, spans, rim_first, None, (edge_second,))
     back_second = to_inner(edge_first)
 
-    def queries_of(half, incoming, dscores, after):
-        return call(
-            functools.partial(early_queries, heads, half),
-            (starts, keys[half], keys[1 - half], incoming, dscores),
-            [two_blocks],
-            scratch=[pltpu.VMEM((2, 2 * REACH * BLK, HD), BF16)],
-            limit=20,
-            after=after,
-        )[0]
-
-    dq_early_second = queries_of(1, rim_second, ds_second, (edge_first,))
-    dq_early_first = queries_of(0, rim_first, ds_first, (dq_early_second,))
+    part = pltpu.VMEM(two_blocks.shape, BF16)
     d_query = call(
-        functools.partial(store_queries, REACH),
-        (dq_early_first, dq_late_first, dq_early_second, dq_late_second),
+        functools.partial(finish_queries, heads),
+        (starts, dq_late_first, *keys, rim_second, rim_first, ds_late, ds_second, ds_first),
         [shape(query.shape)],
-        scratch=[pltpu.SemaphoreType.DMA((4,))],
-        out_spec=ANY,
+        scratch=[part] * 3 + [pltpu.VMEM((2, 2 * REACH * BLK, HD), BF16), pltpu.SemaphoreType.DMA((4,))],
+        limit=20,
+        out_spec=HBM,
     )[0]
 
     d_keys, packed = (), ()

time: 36.8 us -> 36.8 us (level)
  starting transfers between devices: 16.2 us -> 16.8 us
  waiting for transfers between devices: 3.22 us -> 2.62 us
    ppermute x2, starting transfers between devices: 5.71 us -> 6.39 us  [per_device(): to_inner = lambda x: lax.ppermute(x, 'ctx', inner)]
    pallas_call x15 -> x13, Pallas kernels: 16.4 us -> 16.1 us  [call(): pl.pallas_call(lambda *refs: body(*refs[skip:]), out_shape=outs, in_specs...]
  transfers between devices with their start and end apart: 15 -> 15, of which waited for: 4 -> 4; matrix products, arithmetic and copies ran while one was open for 0% -> 0% of each run, Pallas kernels for 40% -> 39%
where the time goes in v3:
time: 36.8 us; the launch traced here: 36.5 us
  starting transfers between devices  16.8 us (46%)
  Pallas kernels  16.1 us (44%)
  waiting for transfers between devices  2.62 us (7%)
  between operations  0.98 us (3%)
    pallas_call x13, Pallas kernels, call(): pl.pallas_call(lambda *refs: body(*refs[skip:]), out_shape=outs, in_specs...  16.1 us
    ppermute x11, starting transfers between devices, per_device(): lax.ppermute(x, 'head', [(i, i ^ t) for i in range(heads)])  9.13 us
    ppermute x2, starting transfers between devices, per_device(): to_inner = lambda x: lax.ppermute(x, 'ctx', inner)  6.39 us
    ppermute x11, waiting for transfers between devices, per_device(): lax.ppermute(x, 'head', [(i, i ^ t) for i in range(heads)])  1.91 us
    ppermute x2, starting transfers between devices, per_device(): to_outer = lambda x: lax.ppermute(x, 'ctx', outer)  1.34 us
  transfers between devices with their start and end apart: 15, of which 4 were waited for; matrix products, arithmetic and copies ran while one was open for 0% of the time, Pallas kernels for 39%

profile of v3, /device:TPU:0, one launch (start us, length us, event | category | flops | bytes accessed | tf_op | source)
XLA Modules:
  0.0 36.5 jit_solution(10562694195496073602)
XLA Ops:
  0.6 1.1 %pack_keys.1 = (bf16[2,2,128,128]{3,2,1,0:T(8,128)(2,1)S(1)}, bf16[2,2,128,128]{3,2,1,0:T(8,128)(2,1)S(1)}, bf16[2,128,128]{2,1,0:T(8,128)(2,1)S(1)}, bf16[2,128,128]{2,1,0:T(8,128)(2,1)S(1)}) custom-call(bf16[1,2,128,512]{3,2,1,0:T(8,128)(2,1)} %refs_2_.1, bf16[1,2,128,512]{3,2,1,0:T(8,128)(2,1)} %refs_3_.1), custom_call_target="tpu_custom_call" | custom-call | tf_op jit(solution)/shard_map/pack_keys/pallas_call | solution.py:34
  1.7 0.5 %collective-permute-start = (bf16[2,2,128,128]{3,2,1,0:T(8,128)(2,1)S(1)}, bf16[2,2,128,128]{3,2,1,0:T(8,128)(2,1)S(1)}, u32[]{:S(2)}, u32[]{:S(2)}) collective-permute-start(bf16[2,2,128,128]{3,2,1,0:T(8,128)(2,1)S(1)} %get-tuple-element.48), channel_id=1, source_target_pairs={{0,1},{1,0},{2,3},{3,2},{4,5},{5,4},{6,7},{7,6},{8,9},{9,8},{10,11... | collective-permute-start | bytes 393224 | tf_op jit(solution)/shard_map/ppermute | solution.py:393
  2.2 2.6 %collective-permute-start.1 = (bf16[2,128,128]{2,1,0:T(8,128)(2,1)S(1)}, bf16[2,128,128]{2,1,0:T(8,128)(2,1)S(1)}, u32[]{:S(2)}, u32[]{:S(2)}) collective-permute-start(bf16[2,128,128]{2,1,0:T(8,128)(2,1)S(1)} %get-tuple-element.49), channel_id=1, source_target_pairs={{0,2},{1,3},{2,0},{3,1},{4,6},{5,7},{6,4},{7,5},{8,10},{9,11},{10,... | collective-permute-start | bytes 196616 | tf_op jit(solution)/shard_map/ppermute | solution.py:393
  4.8 0.1 collective-permute-start.2
  4.9 1.3 %load_queries.1 = (s32[1,64]{1,0:T(1,128)S(1)}, bf16[256,1024]{1,0:T(8,128)(2,1)S(1)}, bf16[256,1024]{1,0:T(8,128)(2,1)S(1)}, bf16[2,128,128]{2,1,0:T(8,128)(2,1)S(1)}, bf16[2,128,128]{2,1,0:T(8,128)(2,1)S(1)}) custom-call(bf16[2,2,128,128]{3,2,1,0:T(8,128)(2,1)S(1)} %get-tuple-element.44.refs_0_.refs_1_, s32[1,64]{1,0:T(1,128)} %bitcast.1, ...), custom_call_target="tpu_custom_call" | custom-call | bytes 4194304 | tf_op jit(solution)/shard_map/load_queries/pallas_call | solution.py:34
  6.1 1.8 %collective-permute-start.3 = (bf16[2,128,128]{2,1,0:T(8,128)(2,1)S(1)}, bf16[2,128,128]{2,1,0:T(8,128)(2,1)S(1)}, u32[]{:S(2)}, u32[]{:S(2)}) collective-permute-start(bf16[2,128,128]{2,1,0:T(8,128)(2,1)S(1)} %get-tuple-element.54), channel_id=1, source_target_pairs={{0,2},{1,3},{2,0},{3,1},{4,6},{5,7},{6,4},{7,5},{8,10},{9,11},{10,... | collective-permute-start | bytes 196616 | tf_op jit(solution)/shard_map/ppermute | solution.py:393
  7.9 0.0 collective-permute-start.4
  8.0 0.0 collective-permute-done.1.refs_3_
  8.0 0.9 %collective-permute-done.2.refs_4_ = bf16[2,128,128]{2,1,0:T(8,128)(2,1)S(1)} collective-permute-done((bf16[2,128,128]{2,1,0:T(8,128)(2,1)S(1)}, bf16[2,128,128]{2,1,0:T(8,128)(2,1)S(1)}, u32[]{:S(2)}, u32[]{:S(2)}) %collective-permute-start.2) | collective-permute-done | bytes 65568 | tf_op jit(solution)/shard_map/ppermute | solution.py:393
  8.8 0.0 collective-permute-done.refs_2_
  8.9 0.7 %collective-permute-start.5 = (bf16[2,256,128]{2,1,0:T(8,128)(2,1)S(1)}, bf16[2,256,128]{2,1,0:T(8,128)(2,1)S(1)}, u32[]{:S(2)}, u32[]{:S(2)}) collective-permute-start(bf16[2,256,128]{2,1,0:T(8,128)(2,1)S(1)} %get-tuple-element.57), channel_id=1, source_target_pairs={{4,8},{8,4},{12,16},{16,12},{20,24},{24,20},{5,9},{9,5},{13,17},{1... | collective-permute-start | bytes 393224 | tf_op jit(solution)/shard_map/ppermute | solution.py:396
  9.6 1.8 %late_blocks.2 = (bf16[256,1024]{1,0:T(8,128)(2,1)S(1)}, f32[2,512,128]{2,1,0:T(8,128)S(1)}, bf16[256,1024]{1,0:T(8,128)(2,1)S(1)}, bf16[256,1024]{1,0:T(8,128)(2,1)S(1)}) custom-call(s32[1,64]{1,0:T(1,128)S(1)} %get-tuple-element.45.refs_0_.refs_1_, bf16[256,1024]{1,0:T(8,128)(2,1)S(1)} %get-tuple-element.46.refs_0_.refs_1_, ...), custom_call_target="tpu_custom_call" | custom-call | tf_op jit(solution)/shard_map/late_blocks/pallas_call | solution.py:34
  11.3 0.0 collective-permute-done.3.refs_3_
  11.4 0.7 %collective-permute-done.4.refs_4_ = bf16[2,128,128]{2,1,0:T(8,128)(2,1)S(1)} collective-permute-done((bf16[2,128,128]{2,1,0:T(8,128)(2,1)S(1)}, bf16[2,128,128]{2,1,0:T(8,128)(2,1)S(1)}, u32[]{:S(2)}, u32[]{:S(2)}) %collective-permute-start.4) | collective-permute-done | bytes 65568 | tf_op jit(solution)/shard_map/ppermute | solution.py:393
  12.1 3.2 %collective-permute-start.6 = (bf16[2,256,128]{2,1,0:T(8,128)(2,1)S(1)}, bf16[2,256,128]{2,1,0:T(8,128)(2,1)S(1)}, u32[]{:S(2)}, u32[]{:S(2)}) collective-permute-start(bf16[2,256,128]{2,1,0:T(8,128)(2,1)S(1)} %get-tuple-element.58), channel_id=1, source_target_pairs={{0,4},{4,0},{8,12},{12,8},{16,20},{20,16},{24,28},{28,24},{1,5},{5... | collective-permute-start | bytes 393224 | tf_op jit(solution)/shard_map/ppermute | solution.py:397
  15.3 1.8 %late_blocks.3 = (bf16[2,384,1024]{2,1,0:T(8,128)(2,1)S(1)}, f32[2,512,128]{2,1,0:T(8,128)S(1)}, bf16[256,1024]{1,0:T(8,128)(2,1)S(1)}, bf16[256,1024]{1,0:T(8,128)(2,1)S(1)}) custom-call(f32[2,512,128]{2,1,0:T(8,128)S(1)} %get-tuple-element.53.refs_0_, s32[1,64]{1,0:T(1,128)S(1)} %get-tuple-element.45.refs_0_.refs_1_, ...), custom_call_target="tpu_custom_call" | custom-call | tf_op jit(solution)/shard_map/late_blocks/pallas_call | solution.py:34
  17.1 0.0 collective-permute-done.5.refs_6_.refs_4_
  17.1 3.4 %early_blocks.2 = (bf16[2,384,1024]{2,1,0:T(8,128)(2,1)S(1)}, f32[2,256,128]{2,1,0:T(8,128)S(1)}, bf16[2,256,128]{2,1,0:T(8,128)(2,1)S(1)}, bf16[256,1024]{1,0:T(8,128)(2,1)S(1)}, bf16[256,1024]{1,0:T(8,128)(2,1)S(1)}) custom-call(f32[2,512,128]{2,1,0:T(8,128)S(1)} %get-tuple-element.62.refs_0_.refs_1_, s32[1,64]{1,0:T(1,128)S(1)} %get-tuple-element.45.refs_0_.refs_1_, ...), custom_call_target="tpu_custom_call" | custom-call | tf_op jit(solution)/shard_map/early_blocks/pallas_call | solution.py:34
  20.5 0.7 %collective-permute-start.7 = (bf16[2,256,128]{2,1,0:T(8,128)(2,1)S(1)}, bf16[2,256,128]{2,1,0:T(8,128)(2,1)S(1)}, u32[]{:S(2)}, u32[]{:S(2)}) collective-permute-start(bf16[2,256,128]{2,1,0:T(8,128)(2,1)S(1)} %get-tuple-element.66.refs_0_.refs_3_), channel_id=1, source_target_pairs={{4,8},{8,4},{12,16},{16,12},{20,24},{24,20},{5,9},{9,5},{13,17},{1... | collective-permute-start | bytes 393224 | tf_op jit(solution)/shard_map/ppermute | solution.py:396
  21.2 0.0 collective-permute-done.6.refs_6_.refs_5_
  21.2 2.3 %early_blocks.3 = (bf16[2,384,1024]{2,1,0:T(8,128)(2,1)S(1)}, f32[2,256,128]{2,1,0:T(8,128)S(1)}, bf16[2,256,128]{2,1,0:T(8,128)(2,1)S(1)}) custom-call(bf16[2,256,128]{2,1,0:T(8,128)(2,1)S(1)} %get-tuple-element.66.refs_0_.refs_3_, s32[1,64]{1,0:T(1,128)S(1)} %get-tuple-element.45.refs_0_.refs_1_, bf16[256,1024]{1,0:T(8,128)(2,1)S(1)} %get-tuple-element.67.refs_2_, ...), custom_call_target="tpu_custom_call" | custom-call | tf_op jit(solution)/shard_map/early_blocks/pallas_call | solution.py:34
  23.5 3.2 %collective-permute-start.8 = (bf16[2,256,128]{2,1,0:T(8,128)(2,1)S(1)}, bf16[2,256,128]{2,1,0:T(8,128)(2,1)S(1)}, u32[]{:S(2)}, u32[]{:S(2)}) collective-permute-start(bf16[2,256,128]{2,1,0:T(8,128)(2,1)S(1)} %get-tuple-element.73.refs_4_), channel_id=1, source_target_pairs={{0,4},{4,0},{8,12},{12,8},{16,20},{20,16},{24,28},{28,24},{1,5},{5... | collective-permute-start | bytes 393224 | tf_op jit(solution)/shard_map/ppermute | solution.py:397
  26.7 0.0 collective-permute-done.7.refs_2_
  26.7 0.3 pack_grads.2
  27.0 0.1 collective-permute-start.12
  27.1 1.5 %collective-permute-start.13 = (bf16[2,128,128]{2,1,0:T(8,128)(2,1)S(1)}, bf16[2,128,128]{2,1,0:T(8,128)(2,1)S(1)}, u32[]{:S(2)}, u32[]{:S(2)}) collective-permute-start(bf16[2,128,128]{2,1,0:T(8,128)(2,1)S(1)} %get-tuple-element.79), channel_id=1, source_target_pairs={{0,2},{1,3},{2,0},{3,1},{4,6},{5,7},{6,4},{7,5},{8,10},{9,11},{10,... | collective-permute-start | bytes 196616 | tf_op jit(solution)/shard_map/ppermute | solution.py:393
  28.6 0.3 collective-permute-start.14
  28.9 0.7 %collective-permute-done.8.refs_3_ = bf16[2,256,128]{2,1,0:T(8,128)(2,1)S(1)} collective-permute-done((bf16[2,256,128]{2,1,0:T(8,128)(2,1)S(1)}, bf16[2,256,128]{2,1,0:T(8,128)(2,1)S(1)}, u32[]{:S(2)}, u32[]{:S(2)}) %collective-permute-start.8) | collective-permute-done | bytes 131104 | tf_op jit(solution)/shard_map/ppermute | solution.py:397
  29.6 0.1 pack_grads.3
  29.7 1.5 %collective-permute-start.10 = (bf16[2,128,128]{2,1,0:T(8,128)(2,1)S(1)}, bf16[2,128,128]{2,1,0:T(8,128)(2,1)S(1)}, u32[]{:S(2)}, u32[]{:S(2)}) collective-permute-start(bf16[2,128,128]{2,1,0:T(8,128)(2,1)S(1)} %get-tuple-element.76), channel_id=1, source_target_pairs={{0,2},{1,3},{2,0},{3,1},{4,6},{5,7},{6,4},{7,5},{8,10},{9,11},{10,... | collective-permute-start | bytes 196616 | tf_op jit(solution)/shard_map/ppermute | solution.py:393
  31.2 0.0 collective-permute-start.11
  31.2 0.0 collective-permute-done.12.refs_1_
  31.2 0.7 %collective-permute-start.9 = (bf16[2,128,128]{2,1,0:T(8,128)(2,1)S(1)}, bf16[2,128,128]{2,1,0:T(8,128)(2,1)S(1)}, u32[]{:S(2)}, u32[]{:S(2)}) collective-permute-start(bf16[2,128,128]{2,1,0:T(8,128)(2,1)S(1)} %get-tuple-element.75), channel_id=1, source_target_pairs={{0,1},{1,0},{2,3},{3,2},{4,5},{5,4},{6,7},{7,6},{8,9},{9,8},{10,11... | collective-permute-start | bytes 196616 | tf_op jit(solution)/shard_map/ppermute | solution.py:393
  31.9 2.5 %finish_queries.1 = bf16[1,2,512,1024]{3,2,1,0:T(8,128)(2,1)} custom-call(s32[1,64]{1,0:T(1,128)S(1)} %get-tuple-element.45.refs_0_.refs_1_, bf16[256,1024]{1,0:T(8,128)(2,1)S(1)} %get-tuple-element.52.refs_1_, bf16[2,512,128]{2,1,0:T(8,128)(2,1)S(1)} %get-tuple-element.51.refs_3_.refs_5_.refs_4_.refs_2_, ...), custom_call_target="tpu_custom_call" | custom-call | tf_op jit(solution)/shard_map/finish_queries/pallas_call | solution.py:34
  34.5 0.0 collective-permute-done.13.refs_2_
  34.5 0.0 collective-permute-done.14.refs_3_
  34.5 0.8 %join_grads.2 = (bf16[1,2,128,512]{3,2,1,0:T(8,128)(2,1)}, bf16[1,2,128,512]{3,2,1,0:T(8,128)(2,1)}) custom-call(bf16[2,128,128]{2,1,0:T(8,128)(2,1)S(1)} %get-tuple-element.71.refs_0_, bf16[2,128,128]{2,1,0:T(8,128)(2,1)S(1)} %collective-permute-done.12.refs_1_, bf16[2,128,128]{2,1,0:T(8,128)(2,1)S(1)} %collective-permute-done.13.refs_2_, ...), custom_call_target="tpu_custom_call" | custom-call | tf_op jit(solution)/shard_map/join_grads/pallas_call | solution.py:34
  35.3 0.0 collective-permute-done.10.refs_2_
  35.3 0.3 collective-permute-done.11.refs_3_
  35.6 0.0 collective-permute-done.9.refs_1_
  35.6 0.8 %join_grads.3 = (bf16[1,2,128,512]{3,2,1,0:T(8,128)(2,1)}, bf16[1,2,128,512]{3,2,1,0:T(8,128)(2,1)}) custom-call(bf16[2,128,128]{2,1,0:T(8,128)(2,1)S(1)} %get-tuple-element.74.refs_0_, bf16[2,128,128]{2,1,0:T(8,128)(2,1)S(1)} %collective-permute-done.9.refs_1_, ...), custom_call_target="tpu_custom_call", output_to_operand_aliasing={{0}: (4, {}), {1}: (5, {})} | custom-call | tf_op jit(solution)/shard_map/join_grads/pallas_call | solution.py:34
  (2 shorter events, 0.1 us)
Async XLA Ops:
  1.7 7.1 %collective-permute-start = (bf16[2,2,128,128]{3,2,1,0:T(8,128)(2,1)S(1)}, bf16[2,2,128,128]{3,2,1,0:T(8,128)(2,1)S(1)}, u32[]{:S(2)}, u32[]{:S(2)}) collective-permute-start(bf16[2,2,128,128]{3,2,1,0:T(8,128)(2,1)S(1)} %get-tuple-element.48), channel_id=1, source_target_pairs={{0,1},{1,0},{2,3},{3,2},{4,5},{5,4},{6,7},{7,6},{8,9},{9,8},{10,11... | collective-permute-start | bytes 393224 | tf_op jit(solution)/shard_map/ppermute | solution.py:393
  2.2 5.7 %collective-permute-start.1 = (bf16[2,128,128]{2,1,0:T(8,128)(2,1)S(1)}, bf16[2,128,128]{2,1,0:T(8,128)(2,1)S(1)}, u32[]{:S(2)}, u32[]{:S(2)}) collective-permute-start(bf16[2,128,128]{2,1,0:T(8,128)(2,1)S(1)} %get-tuple-element.49), channel_id=1, source_target_pairs={{0,2},{1,3},{2,0},{3,1},{4,6},{5,7},{6,4},{7,5},{8,10},{9,11},{10,... | collective-permute-start | bytes 196616 | tf_op jit(solution)/shard_map/ppermute | solution.py:393
  4.8 4.0 %collective-permute-start.2 = (bf16[2,128,128]{2,1,0:T(8,128)(2,1)S(1)}, bf16[2,128,128]{2,1,0:T(8,128)(2,1)S(1)}, u32[]{:S(2)}, u32[]{:S(2)}) collective-permute-start(bf16[2,128,128]{2,1,0:T(8,128)(2,1)S(1)} %get-tuple-element.50), channel_id=1, source_target_pairs={{0,3},{1,2},{2,1},{3,0},{4,7},{5,6},{6,5},{7,4},{8,11},{9,10},{10,... | collective-permute-start | bytes 196616 | tf_op jit(solution)/shard_map/ppermute | solution.py:393
  6.1 5.2 %collective-permute-start.3 = (bf16[2,128,128]{2,1,0:T(8,128)(2,1)S(1)}, bf16[2,128,128]{2,1,0:T(8,128)(2,1)S(1)}, u32[]{:S(2)}, u32[]{:S(2)}) collective-permute-start(bf16[2,128,128]{2,1,0:T(8,128)(2,1)S(1)} %get-tuple-element.54), channel_id=1, source_target_pairs={{0,2},{1,3},{2,0},{3,1},{4,6},{5,7},{6,4},{7,5},{8,10},{9,11},{10,... | collective-permute-start | bytes 196616 | tf_op jit(solution)/shard_map/ppermute | solution.py:393
  7.9 4.1 %collective-permute-start.4 = (bf16[2,128,128]{2,1,0:T(8,128)(2,1)S(1)}, bf16[2,128,128]{2,1,0:T(8,128)(2,1)S(1)}, u32[]{:S(2)}, u32[]{:S(2)}) collective-permute-start(bf16[2,128,128]{2,1,0:T(8,128)(2,1)S(1)} %get-tuple-element.55), channel_id=1, source_target_pairs={{0,3},{1,2},{2,1},{3,0},{4,7},{5,6},{6,5},{7,4},{8,11},{9,10},{10,... | collective-permute-start | bytes 196616 | tf_op jit(solution)/shard_map/ppermute | solution.py:393
  8.9 8.3 %collective-permute-start.5 = (bf16[2,256,128]{2,1,0:T(8,128)(2,1)S(1)}, bf16[2,256,128]{2,1,0:T(8,128)(2,1)S(1)}, u32[]{:S(2)}, u32[]{:S(2)}) collective-permute-start(bf16[2,256,128]{2,1,0:T(8,128)(2,1)S(1)} %get-tuple-element.57), channel_id=1, source_target_pairs={{4,8},{8,4},{12,16},{16,12},{20,24},{24,20},{5,9},{9,5},{13,17},{1... | collective-permute-start | bytes 393224 | tf_op jit(solution)/shard_map/ppermute | solution.py:396
  12.1 9.1 %collective-permute-start.6 = (bf16[2,256,128]{2,1,0:T(8,128)(2,1)S(1)}, bf16[2,256,128]{2,1,0:T(8,128)(2,1)S(1)}, u32[]{:S(2)}, u32[]{:S(2)}) collective-permute-start(bf16[2,256,128]{2,1,0:T(8,128)(2,1)S(1)} %get-tuple-element.58), channel_id=1, source_target_pairs={{0,4},{4,0},{8,12},{12,8},{16,20},{20,16},{24,28},{28,24},{1,5},{5... | collective-permute-start | bytes 393224 | tf_op jit(solution)/shard_map/ppermute | solution.py:397
  20.5 6.2 %collective-permute-start.7 = (bf16[2,256,128]{2,1,0:T(8,128)(2,1)S(1)}, bf16[2,256,128]{2,1,0:T(8,128)(2,1)S(1)}, u32[]{:S(2)}, u32[]{:S(2)}) collective-permute-start(bf16[2,256,128]{2,1,0:T(8,128)(2,1)S(1)} %get-tuple-element.66.refs_0_.refs_3_), channel_id=1, source_target_pairs={{4,8},{8,4},{12,16},{16,12},{20,24},{24,20},{5,9},{9,5},{13,17},{1... | collective-permute-start | bytes 393224 | tf_op jit(solution)/shard_map/ppermute | solution.py:396
  23.5 6.1 %collective-permute-start.8 = (bf16[2,256,128]{2,1,0:T(8,128)(2,1)S(1)}, bf16[2,256,128]{2,1,0:T(8,128)(2,1)S(1)}, u32[]{:S(2)}, u32[]{:S(2)}) collective-permute-start(bf16[2,256,128]{2,1,0:T(8,128)(2,1)S(1)} %get-tuple-element.73.refs_4_), channel_id=1, source_target_pairs={{0,4},{4,0},{8,12},{12,8},{16,20},{20,16},{24,28},{28,24},{1,5},{5... | collective-permute-start | bytes 393224 | tf_op jit(solution)/shard_map/ppermute | solution.py:397
  27.0 4.2 %collective-permute-start.12 = (bf16[2,128,128]{2,1,0:T(8,128)(2,1)S(1)}, bf16[2,128,128]{2,1,0:T(8,128)(2,1)S(1)}, u32[]{:S(2)}, u32[]{:S(2)}) collective-permute-start(bf16[2,128,128]{2,1,0:T(8,128)(2,1)S(1)} %get-tuple-element.78), channel_id=1, source_target_pairs={{0,1},{1,0},{2,3},{3,2},{4,5},{5,4},{6,7},{7,6},{8,9},{9,8},{10,11... | collective-permute-start | bytes 196616 | tf_op jit(solution)/shard_map/ppermute | solution.py:393
  27.1 7.4 %collective-permute-start.13 = (bf16[2,128,128]{2,1,0:T(8,128)(2,1)S(1)}, bf16[2,128,128]{2,1,0:T(8,128)(2,1)S(1)}, u32[]{:S(2)}, u32[]{:S(2)}) collective-permute-start(bf16[2,128,128]{2,1,0:T(8,128)(2,1)S(1)} %get-tuple-element.79), channel_id=1, source_target_pairs={{0,2},{1,3},{2,0},{3,1},{4,6},{5,7},{6,4},{7,5},{8,10},{9,11},{10,... | collective-permute-start | bytes 196616 | tf_op jit(solution)/shard_map/ppermute | solution.py:393
  28.6 5.9 %collective-permute-start.14 = (bf16[2,128,128]{2,1,0:T(8,128)(2,1)S(1)}, bf16[2,128,128]{2,1,0:T(8,128)(2,1)S(1)}, u32[]{:S(2)}, u32[]{:S(2)}) collective-permute-start(bf16[2,128,128]{2,1,0:T(8,128)(2,1)S(1)} %get-tuple-element.80), channel_id=1, source_target_pairs={{0,3},{1,2},{2,1},{3,0},{4,7},{5,6},{6,5},{7,4},{8,11},{9,10},{10,... | collective-permute-start | bytes 196616 | tf_op jit(solution)/shard_map/ppermute | solution.py:393
  29.7 5.6 %collective-permute-start.10 = (bf16[2,128,128]{2,1,0:T(8,128)(2,1)S(1)}, bf16[2,128,128]{2,1,0:T(8,128)(2,1)S(1)}, u32[]{:S(2)}, u32[]{:S(2)}) collective-permute-start(bf16[2,128,128]{2,1,0:T(8,128)(2,1)S(1)} %get-tuple-element.76), channel_id=1, source_target_pairs={{0,2},{1,3},{2,0},{3,1},{4,6},{5,7},{6,4},{7,5},{8,10},{9,11},{10,... | collective-permute-start | bytes 196616 | tf_op jit(solution)/shard_map/ppermute | solution.py:393
  31.2 4.4 %collective-permute-start.11 = (bf16[2,128,128]{2,1,0:T(8,128)(2,1)S(1)}, bf16[2,128,128]{2,1,0:T(8,128)(2,1)S(1)}, u32[]{:S(2)}, u32[]{:S(2)}) collective-permute-start(bf16[2,128,128]{2,1,0:T(8,128)(2,1)S(1)} %get-tuple-element.77), channel_id=1, source_target_pairs={{0,3},{1,2},{2,1},{3,0},{4,7},{5,6},{6,5},{7,4},{8,11},{9,10},{10,... | collective-permute-start | bytes 196616 | tf_op jit(solution)/shard_map/ppermute | solution.py:393
  31.2 4.4 %collective-permute-start.9 = (bf16[2,128,128]{2,1,0:T(8,128)(2,1)S(1)}, bf16[2,128,128]{2,1,0:T(8,128)(2,1)S(1)}, u32[]{:S(2)}, u32[]{:S(2)}) collective-permute-start(bf16[2,128,128]{2,1,0:T(8,128)(2,1)S(1)} %get-tuple-element.75), channel_id=1, source_target_pairs={{0,1},{1,0},{2,3},{3,2},{4,5},{5,4},{6,7},{7,6},{8,9},{9,8},{10,11... | collective-permute-start | bytes 196616 | tf_op jit(solution)/shard_map/ppermute | solution.py:393

commit v4 on v3

--- a/solution.py
+++ b/solution.py
@@ -288,16 +288,7 @@
 
 def late_blocks(per_span, half, what, doc_start, query, d_out, keys, *refs):
     def body(doc_start, query, d_out, keys, kept, d_keys):
-        def put(b):
-            return functools.partial(put_queries, kept.at[pl.ds(b * BLK, BLK), :])
-
-        def put_loose(b, columns, k, ds):
-            dq = turn_back(k, ds)
-            for j, c in enumerate(columns):
-                kept[rows(b), c] = dq[:, j * BLK : (j + 1) * BLK].T
-
-        writers = (put, put_loose) if half == 0 else keepers(kept)
-        span_part(LATE, REACH, REACH, per_span, half, doc_start, query, d_out, keys, *writers, d_keys)
+        span_part(LATE, REACH, REACH, per_span, half, doc_start, query, d_out, keys, *keepers(kept), d_keys)
 
     while_fetching(what, body, (doc_start, query, d_out, keys), refs)
 
@@ -324,8 +315,9 @@
     while_fetching(what, body, (doc_start, query, d_out, keys, other, incoming), refs)
 
 
-def finish_queries(per_span, doc_start, late_first, keys_0, keys_1, rim_second, rim_first, *refs):
-    ds_late, ds_second, ds_first, d_query, part_late, part_second, part_first, window, sems = refs
+def finish_queries(per_span, doc_start, keys_0, keys_1, rim_second, rim_first, *refs):
+    ds_late_0, ds_late_1, ds_second, ds_first, d_query = refs[:5]
+    part_late_0, part_late_1, part_second, part_first, window, sems = refs[5:]
     copies = []
 
     def send(part, half, first_block):
@@ -349,8 +341,8 @@
         pl.when(jnp.logical_not(chosen))(functools.partial(put, (reach + 1, reach + 1)))
         send(part, half, first_block)
 
-    send(late_first, 0, REACH)
-    work_out(LATE, REACH, 1, REACH, keys_1, ds_late, part_late)
+    work_out(LATE, REACH, 0, REACH, keys_0, ds_late_0, part_late_0)
+    work_out(LATE, REACH, 1, REACH, keys_1, ds_late_1, part_late_1)
     fill_window(per_span, 1, window, keys_1, keys_0, rim_second)
     work_out(EARLY, REACH - 1, 1, 0, window, ds_second, part_second)
     fill_window(per_span, 0, window, keys_0, keys_1, rim_first)
@@ -455,7 +447,7 @@
     dscores = shape((2, (REACH + 1) * BLK, query.shape[3]))
 
     def late(half, spans, then, after):
-        outs = [two_blocks if half == 0 else dscores, shape((2, heads * BLK, HD), F32)]
+        outs = [dscores, shape((2, heads * BLK, HD), F32)]
         return grads(late_blocks, half, spans, (), outs, then, after)
 
     def early(half, spans, incoming, then, after):
@@ -464,10 +456,10 @@
         scratch = [pltpu.VMEM(window, BF16), pltpu.VMEM(window, F32)]
         return grads(early_blocks, half, spans, (keys[1 - half], incoming), outs, then, after, scratch)
 
-    dq_late_first, late_first, *spans = late(0, spans, (1, REACH), ())
+    ds_late_first, late_first, *spans = late(0, spans, (1, REACH), ())
     keys[1], rim = join(1, (late_first,))
     rim_first = to_inner(rim)
-    ds_late, late_second, *spans = late(1, spans, (1, 0), (late_first,))
+    ds_late_second, late_second, *spans = late(1, spans, (1, 0), (late_first,))
     ds_second, own_second, edge_second, *spans = early(1, spans, rim_second, (0, 0), (late_second,))
     back_first = to_outer(edge_second)
     ds_first, own_first, edge_first = early(0, spans, rim_first, None, (edge_second,))
@@ -476,9 +468,9 @@
     part = pltpu.VMEM(two_blocks.shape, BF16)
     d_query = call(
         functools.partial(finish_queries, heads),
-        (starts, dq_late_first, *keys, rim_second, rim_first, ds_late, ds_second, ds_first),
+        (starts, *keys, rim_second, rim_first, ds_late_first, ds_late_second, ds_second, ds_first),
         [shape(query.shape)],
-        scratch=[part] * 3 + [pltpu.VMEM((2, 2 * REACH * BLK, HD), BF16), pltpu.SemaphoreType.DMA((4,))],
+        scratch=[part] * 4 + [pltpu.VMEM((2, 2 * REACH * BLK, HD), BF16), pltpu.SemaphoreType.DMA((4,))],
         limit=20,
         out_spec=HBM,
     )[0]

time: 36.8 us -> 37.1 us (level)
  starting transfers between devices: 16.8 us -> 17.2 us
  transfers between devices with their start and end apart: 15 -> 15, of which waited for: 4 -> 3; matrix products, arithmetic and copies ran while one was open for 0% -> 0% of each run, Pallas kernels for 39% -> 39%
where the time goes in v4:
time: 37.1 us; the launch traced here: 36.8 us
  starting transfers between devices  17.2 us (46%)
  Pallas kernels  16.2 us (44%)
  waiting for transfers between devices  2.48 us (7%)
  between operations  0.99 us (3%)
    pallas_call x13, Pallas kernels, call(): pl.pallas_call(lambda *refs: body(*refs[skip:]), out_shape=outs, in_specs...  16.2 us
    ppermute x11, starting transfers between devices, per_device(): lax.ppermute(x, 'head', [(i, i ^ t) for i in range(heads)])  9.13 us
    ppermute x2, starting transfers between devices, per_device(): to_inner = lambda x: lax.ppermute(x, 'ctx', inner)  6.72 us
    ppermute x11, waiting for transfers between devices, per_device(): lax.ppermute(x, 'head', [(i, i ^ t) for i in range(heads)])  1.78 us
    ppermute x2, starting transfers between devices, per_device(): to_outer = lambda x: lax.ppermute(x, 'ctx', outer)  1.34 us
  transfers between devices with their start and end apart: 15, of which 3 were waited for; matrix products, arithmetic and copies ran while one was open for 0% of the time, Pallas kernels for 39%

profile of v4, /device:TPU:0, one launch (start us, length us, event | category | flops | bytes accessed | tf_op | source)
XLA Modules:
  0.0 36.8 jit_solution(3475238102534381331)
XLA Ops:
  0.6 1.1 %pack_keys.1 = (bf16[2,2,128,128]{3,2,1,0:T(8,128)(2,1)S(1)}, bf16[2,2,128,128]{3,2,1,0:T(8,128)(2,1)S(1)}, bf16[2,128,128]{2,1,0:T(8,128)(2,1)S(1)}, bf16[2,128,128]{2,1,0:T(8,128)(2,1)S(1)}) custom-call(bf16[1,2,128,512]{3,2,1,0:T(8,128)(2,1)} %refs_2_.1, bf16[1,2,128,512]{3,2,1,0:T(8,128)(2,1)} %refs_3_.1), custom_call_target="tpu_custom_call" | custom-call | tf_op jit(solution)/shard_map/pack_keys/pallas_call | solution.py:34
  1.7 0.5 %collective-permute-start = (bf16[2,2,128,128]{3,2,1,0:T(8,128)(2,1)S(1)}, bf16[2,2,128,128]{3,2,1,0:T(8,128)(2,1)S(1)}, u32[]{:S(2)}, u32[]{:S(2)}) collective-permute-start(bf16[2,2,128,128]{3,2,1,0:T(8,128)(2,1)S(1)} %get-tuple-element.47), channel_id=1, source_target_pairs={{0,1},{1,0},{2,3},{3,2},{4,5},{5,4},{6,7},{7,6},{8,9},{9,8},{10,11... | collective-permute-start | bytes 393224 | tf_op jit(solution)/shard_map/ppermute | solution.py:385
  2.2 2.6 %collective-permute-start.1 = (bf16[2,128,128]{2,1,0:T(8,128)(2,1)S(1)}, bf16[2,128,128]{2,1,0:T(8,128)(2,1)S(1)}, u32[]{:S(2)}, u32[]{:S(2)}) collective-permute-start(bf16[2,128,128]{2,1,0:T(8,128)(2,1)S(1)} %get-tuple-element.48), channel_id=1, source_target_pairs={{0,2},{1,3},{2,0},{3,1},{4,6},{5,7},{6,4},{7,5},{8,10},{9,11},{10,... | collective-permute-start | bytes 196616 | tf_op jit(solution)/shard_map/ppermute | solution.py:385
  4.8 0.1 collective-permute-start.2
  4.9 1.3 %load_queries.1 = (s32[1,64]{1,0:T(1,128)S(1)}, bf16[256,1024]{1,0:T(8,128)(2,1)S(1)}, bf16[256,1024]{1,0:T(8,128)(2,1)S(1)}, bf16[2,128,128]{2,1,0:T(8,128)(2,1)S(1)}, bf16[2,128,128]{2,1,0:T(8,128)(2,1)S(1)}) custom-call(bf16[2,2,128,128]{3,2,1,0:T(8,128)(2,1)S(1)} %get-tuple-element.44.refs_0_.refs_1_, s32[1,64]{1,0:T(1,128)} %bitcast.1, ...), custom_call_target="tpu_custom_call" | custom-call | bytes 4194304 | tf_op jit(solution)/shard_map/load_queries/pallas_call | solution.py:34
  6.1 1.8 %collective-permute-start.3 = (bf16[2,128,128]{2,1,0:T(8,128)(2,1)S(1)}, bf16[2,128,128]{2,1,0:T(8,128)(2,1)S(1)}, u32[]{:S(2)}, u32[]{:S(2)}) collective-permute-start(bf16[2,128,128]{2,1,0:T(8,128)(2,1)S(1)} %get-tuple-element.53), channel_id=1, source_target_pairs={{0,2},{1,3},{2,0},{3,1},{4,6},{5,7},{6,4},{7,5},{8,10},{9,11},{10,... | collective-permute-start | bytes 196616 | tf_op jit(solution)/shard_map/ppermute | solution.py:385
  7.9 0.0 collective-permute-start.4
  8.0 0.0 collective-permute-done.1.refs_3_
  8.0 0.9 %collective-permute-done.2.refs_4_ = bf16[2,128,128]{2,1,0:T(8,128)(2,1)S(1)} collective-permute-done((bf16[2,128,128]{2,1,0:T(8,128)(2,1)S(1)}, bf16[2,128,128]{2,1,0:T(8,128)(2,1)S(1)}, u32[]{:S(2)}, u32[]{:S(2)}) %collective-permute-start.2) | collective-permute-done | bytes 65568 | tf_op jit(solution)/shard_map/ppermute | solution.py:385
  8.8 0.0 collective-permute-done.refs_2_
  8.9 0.7 %collective-permute-start.5 = (bf16[2,256,128]{2,1,0:T(8,128)(2,1)S(1)}, bf16[2,256,128]{2,1,0:T(8,128)(2,1)S(1)}, u32[]{:S(2)}, u32[]{:S(2)}) collective-permute-start(bf16[2,256,128]{2,1,0:T(8,128)(2,1)S(1)} %get-tuple-element.56), channel_id=1, source_target_pairs={{4,8},{8,4},{12,16},{16,12},{20,24},{24,20},{5,9},{9,5},{13,17},{1... | collective-permute-start | bytes 393224 | tf_op jit(solution)/shard_map/ppermute | solution.py:388
  9.6 1.6 %late_blocks.2 = (bf16[2,384,1024]{2,1,0:T(8,128)(2,1)S(1)}, f32[2,512,128]{2,1,0:T(8,128)S(1)}, bf16[256,1024]{1,0:T(8,128)(2,1)S(1)}, bf16[256,1024]{1,0:T(8,128)(2,1)S(1)}) custom-call(s32[1,64]{1,0:T(1,128)S(1)} %get-tuple-element.45.refs_0_.refs_1_, bf16[256,1024]{1,0:T(8,128)(2,1)S(1)} %get-tuple-element.46.refs_0_.refs_1_, ...), custom_call_target="tpu_custom_call" | custom-call | tf_op jit(solution)/shard_map/late_blocks/pallas_call | solution.py:34
  11.2 0.0 collective-permute-done.3.refs_3_
  11.2 0.9 %collective-permute-done.4.refs_4_ = bf16[2,128,128]{2,1,0:T(8,128)(2,1)S(1)} collective-permute-done((bf16[2,128,128]{2,1,0:T(8,128)(2,1)S(1)}, bf16[2,128,128]{2,1,0:T(8,128)(2,1)S(1)}, u32[]{:S(2)}, u32[]{:S(2)}) %collective-permute-start.4) | collective-permute-done | bytes 65568 | tf_op jit(solution)/shard_map/ppermute | solution.py:385
  12.1 3.5 %collective-permute-start.6 = (bf16[2,256,128]{2,1,0:T(8,128)(2,1)S(1)}, bf16[2,256,128]{2,1,0:T(8,128)(2,1)S(1)}, u32[]{:S(2)}, u32[]{:S(2)}) collective-permute-start(bf16[2,256,128]{2,1,0:T(8,128)(2,1)S(1)} %get-tuple-element.57), channel_id=1, source_target_pairs={{0,4},{4,0},{8,12},{12,8},{16,20},{20,16},{24,28},{28,24},{1,5},{5... | collective-permute-start | bytes 393224 | tf_op jit(solution)/shard_map/ppermute | solution.py:389
  15.6 1.8 %late_blocks.3 = (bf16[2,384,1024]{2,1,0:T(8,128)(2,1)S(1)}, f32[2,512,128]{2,1,0:T(8,128)S(1)}, bf16[256,1024]{1,0:T(8,128)(2,1)S(1)}, bf16[256,1024]{1,0:T(8,128)(2,1)S(1)}) custom-call(f32[2,512,128]{2,1,0:T(8,128)S(1)} %get-tuple-element.52.refs_0_, s32[1,64]{1,0:T(1,128)S(1)} %get-tuple-element.45.refs_0_.refs_1_, ...), custom_call_target="tpu_custom_call" | custom-call | tf_op jit(solution)/shard_map/late_blocks/pallas_call | solution.py:34
  17.4 0.0 collective-permute-done.5.refs_6_.refs_3_
  17.4 3.3 %early_blocks.2 = (bf16[2,384,1024]{2,1,0:T(8,128)(2,1)S(1)}, f32[2,256,128]{2,1,0:T(8,128)S(1)}, bf16[2,256,128]{2,1,0:T(8,128)(2,1)S(1)}, bf16[256,1024]{1,0:T(8,128)(2,1)S(1)}, bf16[256,1024]{1,0:T(8,128)(2,1)S(1)}) custom-call(f32[2,512,128]{2,1,0:T(8,128)S(1)} %get-tuple-element.62.refs_0_.refs_1_, s32[1,64]{1,0:T(1,128)S(1)} %get-tuple-element.45.refs_0_.refs_1_, ...), custom_call_target="tpu_custom_call" | custom-call | tf_op jit(solution)/shard_map/early_blocks/pallas_call | solution.py:34
  20.8 0.7 %collective-permute-start.7 = (bf16[2,256,128]{2,1,0:T(8,128)(2,1)S(1)}, bf16[2,256,128]{2,1,0:T(8,128)(2,1)S(1)}, u32[]{:S(2)}, u32[]{:S(2)}) collective-permute-start(bf16[2,256,128]{2,1,0:T(8,128)(2,1)S(1)} %get-tuple-element.66.refs_0_.refs_3_), channel_id=1, source_target_pairs={{4,8},{8,4},{12,16},{16,12},{20,24},{24,20},{5,9},{9,5},{13,17},{1... | collective-permute-start | bytes 393224 | tf_op jit(solution)/shard_map/ppermute | solution.py:388
  21.5 0.0 collective-permute-done.6.refs_6_.refs_4_
  21.5 2.0 %early_blocks.3 = (bf16[2,384,1024]{2,1,0:T(8,128)(2,1)S(1)}, f32[2,256,128]{2,1,0:T(8,128)S(1)}, bf16[2,256,128]{2,1,0:T(8,128)(2,1)S(1)}) custom-call(bf16[2,256,128]{2,1,0:T(8,128)(2,1)S(1)} %get-tuple-element.66.refs_0_.refs_3_, s32[1,64]{1,0:T(1,128)S(1)} %get-tuple-element.45.refs_0_.refs_1_, bf16[256,1024]{1,0:T(8,128)(2,1)S(1)} %get-tuple-element.67.refs_2_, ...), custom_call_target="tpu_custom_call" | custom-call | tf_op jit(solution)/shard_map/early_blocks/pallas_call | solution.py:34
  23.4 3.3 %collective-permute-start.8 = (bf16[2,256,128]{2,1,0:T(8,128)(2,1)S(1)}, bf16[2,256,128]{2,1,0:T(8,128)(2,1)S(1)}, u32[]{:S(2)}, u32[]{:S(2)}) collective-permute-start(bf16[2,256,128]{2,1,0:T(8,128)(2,1)S(1)} %get-tuple-element.73.refs_4_), channel_id=1, source_target_pairs={{0,4},{4,0},{8,12},{12,8},{16,20},{20,16},{24,28},{28,24},{1,5},{5... | collective-permute-start | bytes 393224 | tf_op jit(solution)/shard_map/ppermute | solution.py:389
  26.7 0.0 collective-permute-done.7.refs_2_
  26.7 0.3 pack_grads.2
  27.0 0.1 collective-permute-start.12
  27.1 1.5 %collective-permute-start.13 = (bf16[2,128,128]{2,1,0:T(8,128)(2,1)S(1)}, bf16[2,128,128]{2,1,0:T(8,128)(2,1)S(1)}, u32[]{:S(2)}, u32[]{:S(2)}) collective-permute-start(bf16[2,128,128]{2,1,0:T(8,128)(2,1)S(1)} %get-tuple-element.79), channel_id=1, source_target_pairs={{0,2},{1,3},{2,0},{3,1},{4,6},{5,7},{6,4},{7,5},{8,10},{9,11},{10,... | collective-permute-start | bytes 196616 | tf_op jit(solution)/shard_map/ppermute | solution.py:385
  28.6 0.3 collective-permute-start.14
  29.0 0.7 %collective-permute-done.8.refs_3_ = bf16[2,256,128]{2,1,0:T(8,128)(2,1)S(1)} collective-permute-done((bf16[2,256,128]{2,1,0:T(8,128)(2,1)S(1)}, bf16[2,256,128]{2,1,0:T(8,128)(2,1)S(1)}, u32[]{:S(2)}, u32[]{:S(2)}) %collective-permute-start.8) | collective-permute-done | bytes 131104 | tf_op jit(solution)/shard_map/ppermute | solution.py:389
  29.7 0.1 pack_grads.3
  29.7 1.5 %collective-permute-start.10 = (bf16[2,128,128]{2,1,0:T(8,128)(2,1)S(1)}, bf16[2,128,128]{2,1,0:T(8,128)(2,1)S(1)}, u32[]{:S(2)}, u32[]{:S(2)}) collective-permute-start(bf16[2,128,128]{2,1,0:T(8,128)(2,1)S(1)} %get-tuple-element.76), channel_id=1, source_target_pairs={{0,2},{1,3},{2,0},{3,1},{4,6},{5,7},{6,4},{7,5},{8,10},{9,11},{10,... | collective-permute-start | bytes 196616 | tf_op jit(solution)/shard_map/ppermute | solution.py:385
  31.3 0.0 collective-permute-start.11
  31.3 0.0 collective-permute-done.12.refs_1_
  31.3 0.7 %collective-permute-start.9 = (bf16[2,128,128]{2,1,0:T(8,128)(2,1)S(1)}, bf16[2,128,128]{2,1,0:T(8,128)(2,1)S(1)}, u32[]{:S(2)}, u32[]{:S(2)}) collective-permute-start(bf16[2,128,128]{2,1,0:T(8,128)(2,1)S(1)} %get-tuple-element.75), channel_id=1, source_target_pairs={{0,1},{1,0},{2,3},{3,2},{4,5},{5,4},{6,7},{7,6},{8,9},{9,8},{10,11... | collective-permute-start | bytes 196616 | tf_op jit(solution)/shard_map/ppermute | solution.py:385
  32.0 3.1 %finish_queries.1 = bf16[1,2,512,1024]{3,2,1,0:T(8,128)(2,1)} custom-call(s32[1,64]{1,0:T(1,128)S(1)} %get-tuple-element.45.refs_0_.refs_1_, bf16[2,512,128]{2,1,0:T(8,128)(2,1)S(1)} %get-tuple-element.50.refs_3_.refs_5_.refs_4_.refs_1_, bf16[2,512,128]{2,1,0:T(8,128)(2,1)S(1)} %get-tuple-element.55.refs_4_.refs_5_.refs_2_, ...), custom_call_target="tpu_custom_call" | custom-call | tf_op jit(solution)/shard_map/finish_queries/pallas_call | solution.py:34
  35.0 0.0 collective-permute-done.13.refs_2_
  35.0 0.0 collective-permute-done.14.refs_3_
  35.1 0.8 %join_grads.2 = (bf16[1,2,128,512]{3,2,1,0:T(8,128)(2,1)}, bf16[1,2,128,512]{3,2,1,0:T(8,128)(2,1)}) custom-call(bf16[2,128,128]{2,1,0:T(8,128)(2,1)S(1)} %get-tuple-element.71.refs_0_, bf16[2,128,128]{2,1,0:T(8,128)(2,1)S(1)} %collective-permute-done.12.refs_1_, bf16[2,128,128]{2,1,0:T(8,128)(2,1)S(1)} %collective-permute-done.13.refs_2_, ...), custom_call_target="tpu_custom_call" | custom-call | tf_op jit(solution)/shard_map/join_grads/pallas_call | solution.py:34
  35.8 0.0 collective-permute-done.10.refs_2_
  35.8 0.0 collective-permute-done.11.refs_3_
  35.9 0.0 collective-permute-done.9.refs_1_
  35.9 0.8 %join_grads.3 = (bf16[1,2,128,512]{3,2,1,0:T(8,128)(2,1)}, bf16[1,2,128,512]{3,2,1,0:T(8,128)(2,1)}) custom-call(bf16[2,128,128]{2,1,0:T(8,128)(2,1)S(1)} %get-tuple-element.74.refs_0_, bf16[2,128,128]{2,1,0:T(8,128)(2,1)S(1)} %collective-permute-done.9.refs_1_, ...), custom_call_target="tpu_custom_call", output_to_operand_aliasing={{0}: (4, {}), {1}: (5, {})} | custom-call | tf_op jit(solution)/shard_map/join_grads/pallas_call | solution.py:34
  (2 shorter events, 0.1 us)
Async XLA Ops:
  1.7 7.1 %collective-permute-start = (bf16[2,2,128,128]{3,2,1,0:T(8,128)(2,1)S(1)}, bf16[2,2,128,128]{3,2,1,0:T(8,128)(2,1)S(1)}, u32[]{:S(2)}, u32[]{:S(2)}) collective-permute-start(bf16[2,2,128,128]{3,2,1,0:T(8,128)(2,1)S(1)} %get-tuple-element.47), channel_id=1, source_target_pairs={{0,1},{1,0},{2,3},{3,2},{4,5},{5,4},{6,7},{7,6},{8,9},{9,8},{10,11... | collective-permute-start | bytes 393224 | tf_op jit(solution)/shard_map/ppermute | solution.py:385
  2.2 5.7 %collective-permute-start.1 = (bf16[2,128,128]{2,1,0:T(8,128)(2,1)S(1)}, bf16[2,128,128]{2,1,0:T(8,128)(2,1)S(1)}, u32[]{:S(2)}, u32[]{:S(2)}) collective-permute-start(bf16[2,128,128]{2,1,0:T(8,128)(2,1)S(1)} %get-tuple-element.48), channel_id=1, source_target_pairs={{0,2},{1,3},{2,0},{3,1},{4,6},{5,7},{6,4},{7,5},{8,10},{9,11},{10,... | collective-permute-start | bytes 196616 | tf_op jit(solution)/shard_map/ppermute | solution.py:385
  4.8 4.0 %collective-permute-start.2 = (bf16[2,128,128]{2,1,0:T(8,128)(2,1)S(1)}, bf16[2,128,128]{2,1,0:T(8,128)(2,1)S(1)}, u32[]{:S(2)}, u32[]{:S(2)}) collective-permute-start(bf16[2,128,128]{2,1,0:T(8,128)(2,1)S(1)} %get-tuple-element.49), channel_id=1, source_target_pairs={{0,3},{1,2},{2,1},{3,0},{4,7},{5,6},{6,5},{7,4},{8,11},{9,10},{10,... | collective-permute-start | bytes 196616 | tf_op jit(solution)/shard_map/ppermute | solution.py:385
  6.1 5.0 %collective-permute-start.3 = (bf16[2,128,128]{2,1,0:T(8,128)(2,1)S(1)}, bf16[2,128,128]{2,1,0:T(8,128)(2,1)S(1)}, u32[]{:S(2)}, u32[]{:S(2)}) collective-permute-start(bf16[2,128,128]{2,1,0:T(8,128)(2,1)S(1)} %get-tuple-element.53), channel_id=1, source_target_pairs={{0,2},{1,3},{2,0},{3,1},{4,6},{5,7},{6,4},{7,5},{8,10},{9,11},{10,... | collective-permute-start | bytes 196616 | tf_op jit(solution)/shard_map/ppermute | solution.py:385
  7.9 4.1 %collective-permute-start.4 = (bf16[2,128,128]{2,1,0:T(8,128)(2,1)S(1)}, bf16[2,128,128]{2,1,0:T(8,128)(2,1)S(1)}, u32[]{:S(2)}, u32[]{:S(2)}) collective-permute-start(bf16[2,128,128]{2,1,0:T(8,128)(2,1)S(1)} %get-tuple-element.54), channel_id=1, source_target_pairs={{0,3},{1,2},{2,1},{3,0},{4,7},{5,6},{6,5},{7,4},{8,11},{9,10},{10,... | collective-permute-start | bytes 196616 | tf_op jit(solution)/shard_map/ppermute | solution.py:385
  8.9 8.6 %collective-permute-start.5 = (bf16[2,256,128]{2,1,0:T(8,128)(2,1)S(1)}, bf16[2,256,128]{2,1,0:T(8,128)(2,1)S(1)}, u32[]{:S(2)}, u32[]{:S(2)}) collective-permute-start(bf16[2,256,128]{2,1,0:T(8,128)(2,1)S(1)} %get-tuple-element.56), channel_id=1, source_target_pairs={{4,8},{8,4},{12,16},{16,12},{20,24},{24,20},{5,9},{9,5},{13,17},{1... | collective-permute-start | bytes 393224 | tf_op jit(solution)/shard_map/ppermute | solution.py:388
  12.1 9.3 %collective-permute-start.6 = (bf16[2,256,128]{2,1,0:T(8,128)(2,1)S(1)}, bf16[2,256,128]{2,1,0:T(8,128)(2,1)S(1)}, u32[]{:S(2)}, u32[]{:S(2)}) collective-permute-start(bf16[2,256,128]{2,1,0:T(8,128)(2,1)S(1)} %get-tuple-element.57), channel_id=1, source_target_pairs={{0,4},{4,0},{8,12},{12,8},{16,20},{20,16},{24,28},{28,24},{1,5},{5... | collective-permute-start | bytes 393224 | tf_op jit(solution)/shard_map/ppermute | solution.py:389
  20.8 5.9 %collective-permute-start.7 = (bf16[2,256,128]{2,1,0:T(8,128)(2,1)S(1)}, bf16[2,256,128]{2,1,0:T(8,128)(2,1)S(1)}, u32[]{:S(2)}, u32[]{:S(2)}) collective-permute-start(bf16[2,256,128]{2,1,0:T(8,128)(2,1)S(1)} %get-tuple-element.66.refs_0_.refs_3_), channel_id=1, source_target_pairs={{4,8},{8,4},{12,16},{16,12},{20,24},{24,20},{5,9},{9,5},{13,17},{1... | collective-permute-start | bytes 393224 | tf_op jit(solution)/shard_map/ppermute | solution.py:388
  23.4 6.2 %collective-permute-start.8 = (bf16[2,256,128]{2,1,0:T(8,128)(2,1)S(1)}, bf16[2,256,128]{2,1,0:T(8,128)(2,1)S(1)}, u32[]{:S(2)}, u32[]{:S(2)}) collective-permute-start(bf16[2,256,128]{2,1,0:T(8,128)(2,1)S(1)} %get-tuple-element.73.refs_4_), channel_id=1, source_target_pairs={{0,4},{4,0},{8,12},{12,8},{16,20},{20,16},{24,28},{28,24},{1,5},{5... | collective-permute-start | bytes 393224 | tf_op jit(solution)/shard_map/ppermute | solution.py:389
  27.0 4.2 %collective-permute-start.12 = (bf16[2,128,128]{2,1,0:T(8,128)(2,1)S(1)}, bf16[2,128,128]{2,1,0:T(8,128)(2,1)S(1)}, u32[]{:S(2)}, u32[]{:S(2)}) collective-permute-start(bf16[2,128,128]{2,1,0:T(8,128)(2,1)S(1)} %get-tuple-element.78), channel_id=1, source_target_pairs={{0,1},{1,0},{2,3},{3,2},{4,5},{5,4},{6,7},{7,6},{8,9},{9,8},{10,11... | collective-permute-start | bytes 196616 | tf_op jit(solution)/shard_map/ppermute | solution.py:385
  27.1 7.9 %collective-permute-start.13 = (bf16[2,128,128]{2,1,0:T(8,128)(2,1)S(1)}, bf16[2,128,128]{2,1,0:T(8,128)(2,1)S(1)}, u32[]{:S(2)}, u32[]{:S(2)}) collective-permute-start(bf16[2,128,128]{2,1,0:T(8,128)(2,1)S(1)} %get-tuple-element.79), channel_id=1, source_target_pairs={{0,2},{1,3},{2,0},{3,1},{4,6},{5,7},{6,4},{7,5},{8,10},{9,11},{10,... | collective-permute-start | bytes 196616 | tf_op jit(solution)/shard_map/ppermute | solution.py:385
  28.6 6.4 %collective-permute-start.14 = (bf16[2,128,128]{2,1,0:T(8,128)(2,1)S(1)}, bf16[2,128,128]{2,1,0:T(8,128)(2,1)S(1)}, u32[]{:S(2)}, u32[]{:S(2)}) collective-permute-start(bf16[2,128,128]{2,1,0:T(8,128)(2,1)S(1)} %get-tuple-element.80), channel_id=1, source_target_pairs={{0,3},{1,2},{2,1},{3,0},{4,7},{5,6},{6,5},{7,4},{8,11},{9,10},{10,... | collective-permute-start | bytes 196616 | tf_op jit(solution)/shard_map/ppermute | solution.py:385
  29.7 6.1 %collective-permute-start.10 = (bf16[2,128,128]{2,1,0:T(8,128)(2,1)S(1)}, bf16[2,128,128]{2,1,0:T(8,128)(2,1)S(1)}, u32[]{:S(2)}, u32[]{:S(2)}) collective-permute-start(bf16[2,128,128]{2,1,0:T(8,128)(2,1)S(1)} %get-tuple-element.76), channel_id=1, source_target_pairs={{0,2},{1,3},{2,0},{3,1},{4,6},{5,7},{6,4},{7,5},{8,10},{9,11},{10,... | collective-permute-start | bytes 196616 | tf_op jit(solution)/shard_map/ppermute | solution.py:385
  31.3 4.6 %collective-permute-start.11 = (bf16[2,128,128]{2,1,0:T(8,128)(2,1)S(1)}, bf16[2,128,128]{2,1,0:T(8,128)(2,1)S(1)}, u32[]{:S(2)}, u32[]{:S(2)}) collective-permute-start(bf16[2,128,128]{2,1,0:T(8,128)(2,1)S(1)} %get-tuple-element.77), channel_id=1, source_target_pairs={{0,3},{1,2},{2,1},{3,0},{4,7},{5,6},{6,5},{7,4},{8,11},{9,10},{10,... | collective-permute-start | bytes 196616 | tf_op jit(solution)/shard_map/ppermute | solution.py:385
  31.3 4.6 %collective-permute-start.9 = (bf16[2,128,128]{2,1,0:T(8,128)(2,1)S(1)}, bf16[2,128,128]{2,1,0:T(8,128)(2,1)S(1)}, u32[]{:S(2)}, u32[]{:S(2)}) collective-permute-start(bf16[2,128,128]{2,1,0:T(8,128)(2,1)S(1)} %get-tuple-element.75), channel_id=1, source_target_pairs={{0,1},{1,0},{2,3},{3,2},{4,5},{5,4},{6,7},{7,6},{8,9},{9,8},{10,11... | collective-permute-start | bytes 196616 | tf_op jit(solution)/shard_map/ppermute | solution.py:385

commit v5 on v3

--- a/solution.py
+++ b/solution.py
@@ -83,15 +83,18 @@
     ]
 
 
-def pack_keys(heads, key, value, own, near, *refs):
+def close_blocks(t, key, value, there):
+    me = lax.axis_index("head")
+    return [
+        (array.at[0, slot_of(half), :, lanes(me ^ t)], there.at[half, i])
+        for half in range(2)
+        for i, array in enumerate((key, value))
+    ]
+
+
+def pack_keys(heads, key, value, near, *refs):
     sends, sems = refs[:-1], refs[-1]
-    me = lax.axis_index("head")
-    pairs = far_blocks(heads, 0, key, value, sends)
-    for t, there in enumerate((own, near)):
-        for half in range(2):
-            for i, array in enumerate((key, value)):
-                pairs.append((array.at[0, slot_of(half), :, lanes(me ^ t)], there.at[half, i]))
-    carry(pairs, sems)
+    carry(far_blocks(heads, 0, key, value, sends) + close_blocks(1, key, value, near), sems)
 
 
 def fetch_rows(what, query, d_out, query_near, d_out_near, sems):
@@ -104,8 +107,9 @@
 
 
 def load_queries(heads, what, doc_start, key, value, query, d_out, starts_near, query_near, d_out_near, *refs):
-    sends, sems = refs[:-1], refs[-1]
-    pairs = far_blocks(heads, 1, key, value, sends) + [(doc_start, starts_near)]
+    own, *sends, sems = refs
+    pairs = far_blocks(heads, 1, key, value, sends) + close_blocks(0, key, value, own)
+    pairs.append((doc_start, starts_near))
     copies = fetch_rows(what, query, d_out, query_near, d_out_near, sems)
     copies += [pltpu.make_async_copy(here, there, sems.at[2 + i]) for i, (here, there) in enumerate(pairs)]
     for copy in copies:
@@ -399,27 +403,28 @@
     key, value, query, d_out = (
         pltpu.with_memory_space_constraint(x, pltpu.HBM) for x in (key, value, query, d_out)
     )
-    own, near, *sends = call(
+    both = shape((2, 2, BLK, HD))
+    ready, *sends = call(
         functools.partial(pack_keys, heads),
         (key, value),
-        [shape((2, 2, BLK, HD))] * 2 + [block] * (heads - 2),
-        scratch=[pltpu.SemaphoreType.DMA((4 + 2 * heads,))],
+        [both] + [block] * (heads - 2),
+        scratch=[pltpu.SemaphoreType.DMA((2 * heads,))],
         far=(0, 1),
     )
-    near = swap(near, 1)
+    near = swap(ready, 1)
     parts = [[swap(sends[t - 2], t) for t in range(2, heads)]]
     starts = pltpu.with_memory_space_constraint(doc_start[None], pltpu.HBM)
     two_blocks = shape((REACH * BLK, query.shape[3]))
     starts, *spans = call(
         functools.partial(load_queries, heads, (0, REACH)),
         (starts, key, value, query, d_out),
-        [shape(starts.shape, jnp.int32), two_blocks, two_blocks] + [block] * (heads - 2),
-        scratch=[pltpu.SemaphoreType.DMA((2 * heads - 1,))],
+        [shape(starts.shape, jnp.int32), two_blocks, two_blocks, both] + [block] * (heads - 2),
+        scratch=[pltpu.SemaphoreType.DMA((2 * heads + 3,))],
         moved=4 * query.size,
         far=range(5),
-        after=(own,),
+        after=(ready,),
     )
-    spans, sends = spans[:2], spans[2:]
+    spans, own, sends = spans[:2], spans[2], spans[3:]
     parts.append([swap(sends[t - 2], t) for t in range(2, heads)])
 
     def join(half, after):

time: 36.8 us -> 37 us (level)
  Pallas kernels: 16.1 us -> 15.7 us
  starting transfers between devices: 16.8 us -> 17.2 us
    pallas_call x13, Pallas kernels: 16.1 us -> 15.7 us  [call(): pl.pallas_call(lambda *refs: body(*refs[skip:]), out_shape=outs, in_specs...]
  transfers between devices with their start and end apart: 15 -> 15, of which waited for: 4 -> 4; matrix products, arithmetic and copies ran while one was open for 0% -> 0% of each run, Pallas kernels for 39% -> 38%
where the time goes in v5:
time: 37 us; the launch traced here: 36.5 us
  starting transfers between devices  17.2 us (46%)
  Pallas kernels  15.7 us (42%)
  waiting for transfers between devices  2.59 us (7%)
  between operations  0.98 us (3%)
    pallas_call x13, Pallas kernels, call(): pl.pallas_call(lambda *refs: body(*refs[skip:]), out_shape=outs, in_specs...  15.7 us
    ppermute x11, starting transfers between devices, per_device(): lax.ppermute(x, 'head', [(i, i ^ t) for i in range(heads)])  9.13 us
    ppermute x2, starting transfers between devices, per_device(): to_inner = lambda x: lax.ppermute(x, 'ctx', inner)  6.73 us
    ppermute x11, waiting for transfers between devices, per_device(): lax.ppermute(x, 'head', [(i, i ^ t) for i in range(heads)])  1.89 us
    ppermute x2, starting transfers between devices, per_device(): to_outer = lambda x: lax.ppermute(x, 'ctx', outer)  1.34 us
  transfers between devices with their start and end apart: 15, of which 4 were waited for; matrix products, arithmetic and copies ran while one was open for 0% of the time, Pallas kernels for 38%

profile of v5, /device:TPU:0, one launch (start us, length us, event | category | flops | bytes accessed | tf_op | source)
XLA Modules:
  0.0 36.5 jit_solution(2989434416161581507)
XLA Ops:
  0.6 1.0 %pack_keys.1 = (bf16[2,2,128,128]{3,2,1,0:T(8,128)(2,1)S(1)}, bf16[2,128,128]{2,1,0:T(8,128)(2,1)S(1)}, bf16[2,128,128]{2,1,0:T(8,128)(2,1)S(1)}) custom-call(bf16[1,2,128,512]{3,2,1,0:T(8,128)(2,1)} %refs_2_.1, bf16[1,2,128,512]{3,2,1,0:T(8,128)(2,1)} %refs_3_.1), custom_call_target="tpu_custom_call" | custom-call | tf_op jit(solution)/shard_map/pack_keys/pallas_call | solution.py:34
  1.6 0.5 %collective-permute-start = (bf16[2,2,128,128]{3,2,1,0:T(8,128)(2,1)S(1)}, bf16[2,2,128,128]{3,2,1,0:T(8,128)(2,1)S(1)}, u32[]{:S(2)}, u32[]{:S(2)}) collective-permute-start(bf16[2,2,128,128]{3,2,1,0:T(8,128)(2,1)S(1)} %get-tuple-element.44.refs_0_), channel_id=1, source_target_pairs={{0,1},{1,0},{2,3},{3,2},{4,5},{5,4},{6,7},{7,6},{8,9},{9,8},{10,11... | collective-permute-start | bytes 393224 | tf_op jit(solution)/shard_map/ppermute | solution.py:397
  2.1 2.6 %collective-permute-start.1 = (bf16[2,128,128]{2,1,0:T(8,128)(2,1)S(1)}, bf16[2,128,128]{2,1,0:T(8,128)(2,1)S(1)}, u32[]{:S(2)}, u32[]{:S(2)}) collective-permute-start(bf16[2,128,128]{2,1,0:T(8,128)(2,1)S(1)} %get-tuple-element.49), channel_id=1, source_target_pairs={{0,2},{1,3},{2,0},{3,1},{4,6},{5,7},{6,4},{7,5},{8,10},{9,11},{10,... | collective-permute-start | bytes 196616 | tf_op jit(solution)/shard_map/ppermute | solution.py:397
  4.7 0.1 collective-permute-start.2
  4.8 1.3 %load_queries.1 = (s32[1,64]{1,0:T(1,128)S(1)}, bf16[256,1024]{1,0:T(8,128)(2,1)S(1)}, bf16[256,1024]{1,0:T(8,128)(2,1)S(1)}, bf16[2,2,128,128]{3,2,1,0:T(8,128)...) custom-call(bf16[2,2,128,128]{3,2,1,0:T(8,128)(2,1)S(1)} %get-tuple-element.44.refs_0_, ...), custom_call_target="tpu_custom_call" | custom-call | bytes 4194304 | tf_op jit(solution)/shard_map/load_queries/pallas_call | solution.py:34
  6.1 1.8 %collective-permute-start.3 = (bf16[2,128,128]{2,1,0:T(8,128)(2,1)S(1)}, bf16[2,128,128]{2,1,0:T(8,128)(2,1)S(1)}, u32[]{:S(2)}, u32[]{:S(2)}) collective-permute-start(bf16[2,128,128]{2,1,0:T(8,128)(2,1)S(1)} %get-tuple-element.54), channel_id=1, source_target_pairs={{0,2},{1,3},{2,0},{3,1},{4,6},{5,7},{6,4},{7,5},{8,10},{9,11},{10,... | collective-permute-start | bytes 196616 | tf_op jit(solution)/shard_map/ppermute | solution.py:397
  7.9 0.0 collective-permute-start.4
  7.9 0.0 collective-permute-done.1.refs_3_
  7.9 0.8 %collective-permute-done.2.refs_4_ = bf16[2,128,128]{2,1,0:T(8,128)(2,1)S(1)} collective-permute-done((bf16[2,128,128]{2,1,0:T(8,128)(2,1)S(1)}, bf16[2,128,128]{2,1,0:T(8,128)(2,1)S(1)}, u32[]{:S(2)}, u32[]{:S(2)}) %collective-permute-start.2) | collective-permute-done | bytes 65568 | tf_op jit(solution)/shard_map/ppermute | solution.py:397
  8.7 0.0 collective-permute-done.refs_2_
  8.8 0.7 %collective-permute-start.5 = (bf16[2,256,128]{2,1,0:T(8,128)(2,1)S(1)}, bf16[2,256,128]{2,1,0:T(8,128)(2,1)S(1)}, u32[]{:S(2)}, u32[]{:S(2)}) collective-permute-start(bf16[2,256,128]{2,1,0:T(8,128)(2,1)S(1)} %get-tuple-element.57), channel_id=1, source_target_pairs={{4,8},{8,4},{12,16},{16,12},{20,24},{24,20},{5,9},{9,5},{13,17},{1... | collective-permute-start | bytes 393224 | tf_op jit(solution)/shard_map/ppermute | solution.py:400
  9.4 1.8 %late_blocks.2 = (bf16[256,1024]{1,0:T(8,128)(2,1)S(1)}, f32[2,512,128]{2,1,0:T(8,128)S(1)}, bf16[256,1024]{1,0:T(8,128)(2,1)S(1)}, bf16[256,1024]{1,0:T(8,128)(2,1)S(1)}) custom-call(s32[1,64]{1,0:T(1,128)S(1)} %get-tuple-element.45.refs_0_.refs_1_, bf16[256,1024]{1,0:T(8,128)(2,1)S(1)} %get-tuple-element.46.refs_0_.refs_1_, ...), custom_call_target="tpu_custom_call" | custom-call | tf_op jit(solution)/shard_map/late_blocks/pallas_call | solution.py:34
  11.3 0.0 collective-permute-done.3.refs_3_
  11.3 0.7 %collective-permute-done.4.refs_4_ = bf16[2,128,128]{2,1,0:T(8,128)(2,1)S(1)} collective-permute-done((bf16[2,128,128]{2,1,0:T(8,128)(2,1)S(1)}, bf16[2,128,128]{2,1,0:T(8,128)(2,1)S(1)}, u32[]{:S(2)}, u32[]{:S(2)}) %collective-permute-start.4) | collective-permute-done | bytes 65568 | tf_op jit(solution)/shard_map/ppermute | solution.py:397
  12.0 3.2 %collective-permute-start.6 = (bf16[2,256,128]{2,1,0:T(8,128)(2,1)S(1)}, bf16[2,256,128]{2,1,0:T(8,128)(2,1)S(1)}, u32[]{:S(2)}, u32[]{:S(2)}) collective-permute-start(bf16[2,256,128]{2,1,0:T(8,128)(2,1)S(1)} %get-tuple-element.58), channel_id=1, source_target_pairs={{0,4},{4,0},{8,12},{12,8},{16,20},{20,16},{24,28},{28,24},{1,5},{5... | collective-permute-start | bytes 393224 | tf_op jit(solution)/shard_map/ppermute | solution.py:401
  15.2 1.8 %late_blocks.3 = (bf16[2,384,1024]{2,1,0:T(8,128)(2,1)S(1)}, f32[2,512,128]{2,1,0:T(8,128)S(1)}, bf16[256,1024]{1,0:T(8,128)(2,1)S(1)}, bf16[256,1024]{1,0:T(8,128)(2,1)S(1)}) custom-call(f32[2,512,128]{2,1,0:T(8,128)S(1)} %get-tuple-element.53.refs_0_, s32[1,64]{1,0:T(1,128)S(1)} %get-tuple-element.45.refs_0_.refs_1_, ...), custom_call_target="tpu_custom_call" | custom-call | tf_op jit(solution)/shard_map/late_blocks/pallas_call | solution.py:34
  17.0 0.0 collective-permute-done.5.refs_6_.refs_4_
  17.0 3.3 %early_blocks.2 = (bf16[2,384,1024]{2,1,0:T(8,128)(2,1)S(1)}, f32[2,256,128]{2,1,0:T(8,128)S(1)}, bf16[2,256,128]{2,1,0:T(8,128)(2,1)S(1)}, bf16[256,1024]{1,0:T(8,128)(2,1)S(1)}, bf16[256,1024]{1,0:T(8,128)(2,1)S(1)}) custom-call(f32[2,512,128]{2,1,0:T(8,128)S(1)} %get-tuple-element.62.refs_0_.refs_1_, s32[1,64]{1,0:T(1,128)S(1)} %get-tuple-element.45.refs_0_.refs_1_, ...), custom_call_target="tpu_custom_call" | custom-call | tf_op jit(solution)/shard_map/early_blocks/pallas_call | solution.py:34
  20.4 0.7 %collective-permute-start.7 = (bf16[2,256,128]{2,1,0:T(8,128)(2,1)S(1)}, bf16[2,256,128]{2,1,0:T(8,128)(2,1)S(1)}, u32[]{:S(2)}, u32[]{:S(2)}) collective-permute-start(bf16[2,256,128]{2,1,0:T(8,128)(2,1)S(1)} %get-tuple-element.66.refs_0_.refs_3_), channel_id=1, source_target_pairs={{4,8},{8,4},{12,16},{16,12},{20,24},{24,20},{5,9},{9,5},{13,17},{1... | collective-permute-start | bytes 393224 | tf_op jit(solution)/shard_map/ppermute | solution.py:400
  21.0 0.0 collective-permute-done.6.refs_6_.refs_5_
  21.1 2.0 %early_blocks.3 = (bf16[2,384,1024]{2,1,0:T(8,128)(2,1)S(1)}, f32[2,256,128]{2,1,0:T(8,128)S(1)}, bf16[2,256,128]{2,1,0:T(8,128)(2,1)S(1)}) custom-call(bf16[2,256,128]{2,1,0:T(8,128)(2,1)S(1)} %get-tuple-element.66.refs_0_.refs_3_, s32[1,64]{1,0:T(1,128)S(1)} %get-tuple-element.45.refs_0_.refs_1_, bf16[256,1024]{1,0:T(8,128)(2,1)S(1)} %get-tuple-element.67.refs_2_, ...), custom_call_target="tpu_custom_call" | custom-call | tf_op jit(solution)/shard_map/early_blocks/pallas_call | solution.py:34
  23.0 3.5 %collective-permute-start.8 = (bf16[2,256,128]{2,1,0:T(8,128)(2,1)S(1)}, bf16[2,256,128]{2,1,0:T(8,128)(2,1)S(1)}, u32[]{:S(2)}, u32[]{:S(2)}) collective-permute-start(bf16[2,256,128]{2,1,0:T(8,128)(2,1)S(1)} %get-tuple-element.73.refs_4_), channel_id=1, source_target_pairs={{0,4},{4,0},{8,12},{12,8},{16,20},{20,16},{24,28},{28,24},{1,5},{5... | collective-permute-start | bytes 393224 | tf_op jit(solution)/shard_map/ppermute | solution.py:401
  26.6 0.0 collective-permute-done.7.refs_2_
  26.6 0.3 pack_grads.2
  26.9 0.1 collective-permute-start.12
  27.0 1.5 %collective-permute-start.13 = (bf16[2,128,128]{2,1,0:T(8,128)(2,1)S(1)}, bf16[2,128,128]{2,1,0:T(8,128)(2,1)S(1)}, u32[]{:S(2)}, u32[]{:S(2)}) collective-permute-start(bf16[2,128,128]{2,1,0:T(8,128)(2,1)S(1)} %get-tuple-element.79), channel_id=1, source_target_pairs={{0,2},{1,3},{2,0},{3,1},{4,6},{5,7},{6,4},{7,5},{8,10},{9,11},{10,... | collective-permute-start | bytes 196616 | tf_op jit(solution)/shard_map/ppermute | solution.py:397
  28.5 0.3 collective-permute-start.14
  28.8 0.7 %collective-permute-done.8.refs_3_ = bf16[2,256,128]{2,1,0:T(8,128)(2,1)S(1)} collective-permute-done((bf16[2,256,128]{2,1,0:T(8,128)(2,1)S(1)}, bf16[2,256,128]{2,1,0:T(8,128)(2,1)S(1)}, u32[]{:S(2)}, u32[]{:S(2)}) %collective-permute-start.8) | collective-permute-done | bytes 131104 | tf_op jit(solution)/shard_map/ppermute | solution.py:401
  29.5 0.1 pack_grads.3
  29.6 1.5 %collective-permute-start.10 = (bf16[2,128,128]{2,1,0:T(8,128)(2,1)S(1)}, bf16[2,128,128]{2,1,0:T(8,128)(2,1)S(1)}, u32[]{:S(2)}, u32[]{:S(2)}) collective-permute-start(bf16[2,128,128]{2,1,0:T(8,128)(2,1)S(1)} %get-tuple-element.76), channel_id=1, source_target_pairs={{0,2},{1,3},{2,0},{3,1},{4,6},{5,7},{6,4},{7,5},{8,10},{9,11},{10,... | collective-permute-start | bytes 196616 | tf_op jit(solution)/shard_map/ppermute | solution.py:397
  31.1 0.0 collective-permute-start.11
  31.1 0.0 collective-permute-done.12.refs_1_
  31.1 0.7 %collective-permute-start.9 = (bf16[2,128,128]{2,1,0:T(8,128)(2,1)S(1)}, bf16[2,128,128]{2,1,0:T(8,128)(2,1)S(1)}, u32[]{:S(2)}, u32[]{:S(2)}) collective-permute-start(bf16[2,128,128]{2,1,0:T(8,128)(2,1)S(1)} %get-tuple-element.75), channel_id=1, source_target_pairs={{0,1},{1,0},{2,3},{3,2},{4,5},{5,4},{6,7},{7,6},{8,9},{9,8},{10,11... | collective-permute-start | bytes 196616 | tf_op jit(solution)/shard_map/ppermute | solution.py:397
  31.8 2.5 %finish_queries.1 = bf16[1,2,512,1024]{3,2,1,0:T(8,128)(2,1)} custom-call(s32[1,64]{1,0:T(1,128)S(1)} %get-tuple-element.45.refs_0_.refs_1_, bf16[256,1024]{1,0:T(8,128)(2,1)S(1)} %get-tuple-element.52.refs_1_, bf16[2,512,128]{2,1,0:T(8,128)(2,1)S(1)} %get-tuple-element.51.refs_3_.refs_5_.refs_4_.refs_2_, ...), custom_call_target="tpu_custom_call" | custom-call | tf_op jit(solution)/shard_map/finish_queries/pallas_call | solution.py:34
  34.4 0.0 collective-permute-done.13.refs_2_
  34.4 0.0 collective-permute-done.14.refs_3_
  34.4 0.8 %join_grads.2 = (bf16[1,2,128,512]{3,2,1,0:T(8,128)(2,1)}, bf16[1,2,128,512]{3,2,1,0:T(8,128)(2,1)}) custom-call(bf16[2,128,128]{2,1,0:T(8,128)(2,1)S(1)} %get-tuple-element.71.refs_0_, bf16[2,128,128]{2,1,0:T(8,128)(2,1)S(1)} %collective-permute-done.12.refs_1_, bf16[2,128,128]{2,1,0:T(8,128)(2,1)S(1)} %collective-permute-done.13.refs_2_, ...), custom_call_target="tpu_custom_call" | custom-call | tf_op jit(solution)/shard_map/join_grads/pallas_call | solution.py:34
  35.2 0.0 collective-permute-done.10.refs_2_
  35.2 0.3 collective-permute-done.11.refs_3_
  35.5 0.0 collective-permute-done.9.refs_1_
  35.5 0.8 %join_grads.3 = (bf16[1,2,128,512]{3,2,1,0:T(8,128)(2,1)}, bf16[1,2,128,512]{3,2,1,0:T(8,128)(2,1)}) custom-call(bf16[2,128,128]{2,1,0:T(8,128)(2,1)S(1)} %get-tuple-element.74.refs_0_, bf16[2,128,128]{2,1,0:T(8,128)(2,1)S(1)} %collective-permute-done.9.refs_1_, ...), custom_call_target="tpu_custom_call", output_to_operand_aliasing={{0}: (4, {}), {1}: (5, {})} | custom-call | tf_op jit(solution)/shard_map/join_grads/pallas_call | solution.py:34
  (2 shorter events, 0.1 us)
Async XLA Ops:
  1.6 7.1 %collective-permute-start = (bf16[2,2,128,128]{3,2,1,0:T(8,128)(2,1)S(1)}, bf16[2,2,128,128]{3,2,1,0:T(8,128)(2,1)S(1)}, u32[]{:S(2)}, u32[]{:S(2)}) collective-permute-start(bf16[2,2,128,128]{3,2,1,0:T(8,128)(2,1)S(1)} %get-tuple-element.44.refs_0_), channel_id=1, source_target_pairs={{0,1},{1,0},{2,3},{3,2},{4,5},{5,4},{6,7},{7,6},{8,9},{9,8},{10,11... | collective-permute-start | bytes 393224 | tf_op jit(solution)/shard_map/ppermute | solution.py:397
  2.1 5.8 %collective-permute-start.1 = (bf16[2,128,128]{2,1,0:T(8,128)(2,1)S(1)}, bf16[2,128,128]{2,1,0:T(8,128)(2,1)S(1)}, u32[]{:S(2)}, u32[]{:S(2)}) collective-permute-start(bf16[2,128,128]{2,1,0:T(8,128)(2,1)S(1)} %get-tuple-element.49), channel_id=1, source_target_pairs={{0,2},{1,3},{2,0},{3,1},{4,6},{5,7},{6,4},{7,5},{8,10},{9,11},{10,... | collective-permute-start | bytes 196616 | tf_op jit(solution)/shard_map/ppermute | solution.py:397
  4.7 4.0 %collective-permute-start.2 = (bf16[2,128,128]{2,1,0:T(8,128)(2,1)S(1)}, bf16[2,128,128]{2,1,0:T(8,128)(2,1)S(1)}, u32[]{:S(2)}, u32[]{:S(2)}) collective-permute-start(bf16[2,128,128]{2,1,0:T(8,128)(2,1)S(1)} %get-tuple-element.50), channel_id=1, source_target_pairs={{0,3},{1,2},{2,1},{3,0},{4,7},{5,6},{6,5},{7,4},{8,11},{9,10},{10,... | collective-permute-start | bytes 196616 | tf_op jit(solution)/shard_map/ppermute | solution.py:397
  6.1 5.2 %collective-permute-start.3 = (bf16[2,128,128]{2,1,0:T(8,128)(2,1)S(1)}, bf16[2,128,128]{2,1,0:T(8,128)(2,1)S(1)}, u32[]{:S(2)}, u32[]{:S(2)}) collective-permute-start(bf16[2,128,128]{2,1,0:T(8,128)(2,1)S(1)} %get-tuple-element.54), channel_id=1, source_target_pairs={{0,2},{1,3},{2,0},{3,1},{4,6},{5,7},{6,4},{7,5},{8,10},{9,11},{10,... | collective-permute-start | bytes 196616 | tf_op jit(solution)/shard_map/ppermute | solution.py:397
  7.9 4.1 %collective-permute-start.4 = (bf16[2,128,128]{2,1,0:T(8,128)(2,1)S(1)}, bf16[2,128,128]{2,1,0:T(8,128)(2,1)S(1)}, u32[]{:S(2)}, u32[]{:S(2)}) collective-permute-start(bf16[2,128,128]{2,1,0:T(8,128)(2,1)S(1)} %get-tuple-element.55), channel_id=1, source_target_pairs={{0,3},{1,2},{2,1},{3,0},{4,7},{5,6},{6,5},{7,4},{8,11},{9,10},{10,... | collective-permute-start | bytes 196616 | tf_op jit(solution)/shard_map/ppermute | solution.py:397
  8.8 8.2 %collective-permute-start.5 = (bf16[2,256,128]{2,1,0:T(8,128)(2,1)S(1)}, bf16[2,256,128]{2,1,0:T(8,128)(2,1)S(1)}, u32[]{:S(2)}, u32[]{:S(2)}) collective-permute-start(bf16[2,256,128]{2,1,0:T(8,128)(2,1)S(1)} %get-tuple-element.57), channel_id=1, source_target_pairs={{4,8},{8,4},{12,16},{16,12},{20,24},{24,20},{5,9},{9,5},{13,17},{1... | collective-permute-start | bytes 393224 | tf_op jit(solution)/shard_map/ppermute | solution.py:400
  12.0 9.0 %collective-permute-start.6 = (bf16[2,256,128]{2,1,0:T(8,128)(2,1)S(1)}, bf16[2,256,128]{2,1,0:T(8,128)(2,1)S(1)}, u32[]{:S(2)}, u32[]{:S(2)}) collective-permute-start(bf16[2,256,128]{2,1,0:T(8,128)(2,1)S(1)} %get-tuple-element.58), channel_id=1, source_target_pairs={{0,4},{4,0},{8,12},{12,8},{16,20},{20,16},{24,28},{28,24},{1,5},{5... | collective-permute-start | bytes 393224 | tf_op jit(solution)/shard_map/ppermute | solution.py:401
  20.4 6.2 %collective-permute-start.7 = (bf16[2,256,128]{2,1,0:T(8,128)(2,1)S(1)}, bf16[2,256,128]{2,1,0:T(8,128)(2,1)S(1)}, u32[]{:S(2)}, u32[]{:S(2)}) collective-permute-start(bf16[2,256,128]{2,1,0:T(8,128)(2,1)S(1)} %get-tuple-element.66.refs_0_.refs_3_), channel_id=1, source_target_pairs={{4,8},{8,4},{12,16},{16,12},{20,24},{24,20},{5,9},{9,5},{13,17},{1... | collective-permute-start | bytes 393224 | tf_op jit(solution)/shard_map/ppermute | solution.py:400
  23.0 6.5 %collective-permute-start.8 = (bf16[2,256,128]{2,1,0:T(8,128)(2,1)S(1)}, bf16[2,256,128]{2,1,0:T(8,128)(2,1)S(1)}, u32[]{:S(2)}, u32[]{:S(2)}) collective-permute-start(bf16[2,256,128]{2,1,0:T(8,128)(2,1)S(1)} %get-tuple-element.73.refs_4_), channel_id=1, source_target_pairs={{0,4},{4,0},{8,12},{12,8},{16,20},{20,16},{24,28},{28,24},{1,5},{5... | collective-permute-start | bytes 393224 | tf_op jit(solution)/shard_map/ppermute | solution.py:401
  26.9 4.3 %collective-permute-start.12 = (bf16[2,128,128]{2,1,0:T(8,128)(2,1)S(1)}, bf16[2,128,128]{2,1,0:T(8,128)(2,1)S(1)}, u32[]{:S(2)}, u32[]{:S(2)}) collective-permute-start(bf16[2,128,128]{2,1,0:T(8,128)(2,1)S(1)} %get-tuple-element.78), channel_id=1, source_target_pairs={{0,1},{1,0},{2,3},{3,2},{4,5},{5,4},{6,7},{7,6},{8,9},{9,8},{10,11... | collective-permute-start | bytes 196616 | tf_op jit(solution)/shard_map/ppermute | solution.py:397
  27.0 7.4 %collective-permute-start.13 = (bf16[2,128,128]{2,1,0:T(8,128)(2,1)S(1)}, bf16[2,128,128]{2,1,0:T(8,128)(2,1)S(1)}, u32[]{:S(2)}, u32[]{:S(2)}) collective-permute-start(bf16[2,128,128]{2,1,0:T(8,128)(2,1)S(1)} %get-tuple-element.79), channel_id=1, source_target_pairs={{0,2},{1,3},{2,0},{3,1},{4,6},{5,7},{6,4},{7,5},{8,10},{9,11},{10,... | collective-permute-start | bytes 196616 | tf_op jit(solution)/shard_map/ppermute | solution.py:397
  28.5 5.9 %collective-permute-start.14 = (bf16[2,128,128]{2,1,0:T(8,128)(2,1)S(1)}, bf16[2,128,128]{2,1,0:T(8,128)(2,1)S(1)}, u32[]{:S(2)}, u32[]{:S(2)}) collective-permute-start(bf16[2,128,128]{2,1,0:T(8,128)(2,1)S(1)} %get-tuple-element.80), channel_id=1, source_target_pairs={{0,3},{1,2},{2,1},{3,0},{4,7},{5,6},{6,5},{7,4},{8,11},{9,10},{10,... | collective-permute-start | bytes 196616 | tf_op jit(solution)/shard_map/ppermute | solution.py:397
  29.6 5.6 %collective-permute-start.10 = (bf16[2,128,128]{2,1,0:T(8,128)(2,1)S(1)}, bf16[2,128,128]{2,1,0:T(8,128)(2,1)S(1)}, u32[]{:S(2)}, u32[]{:S(2)}) collective-permute-start(bf16[2,128,128]{2,1,0:T(8,128)(2,1)S(1)} %get-tuple-element.76), channel_id=1, source_target_pairs={{0,2},{1,3},{2,0},{3,1},{4,6},{5,7},{6,4},{7,5},{8,10},{9,11},{10,... | collective-permute-start | bytes 196616 | tf_op jit(solution)/shard_map/ppermute | solution.py:397
  31.1 4.4 %collective-permute-start.11 = (bf16[2,128,128]{2,1,0:T(8,128)(2,1)S(1)}, bf16[2,128,128]{2,1,0:T(8,128)(2,1)S(1)}, u32[]{:S(2)}, u32[]{:S(2)}) collective-permute-start(bf16[2,128,128]{2,1,0:T(8,128)(2,1)S(1)} %get-tuple-element.77), channel_id=1, source_target_pairs={{0,3},{1,2},{2,1},{3,0},{4,7},{5,6},{6,5},{7,4},{8,11},{9,10},{10,... | collective-permute-start | bytes 196616 | tf_op jit(solution)/shard_map/ppermute | solution.py:397
  31.1 4.4 %collective-permute-start.9 = (bf16[2,128,128]{2,1,0:T(8,128)(2,1)S(1)}, bf16[2,128,128]{2,1,0:T(8,128)(2,1)S(1)}, u32[]{:S(2)}, u32[]{:S(2)}) collective-permute-start(bf16[2,128,128]{2,1,0:T(8,128)(2,1)S(1)} %get-tuple-element.75), channel_id=1, source_target_pairs={{0,1},{1,0},{2,3},{3,2},{4,5},{5,4},{6,7},{7,6},{8,9},{9,8},{10,11... | collective-permute-start | bytes 196616 | tf_op jit(solution)/shard_map/ppermute | solution.py:397
